TPU v7x, 32 devices: a whole 2x2x4 slice. The times are simulated.
32 devices in a mesh: row: 8 (over z, x), col: 4 (over y, core).
Axes of the slice: x: 2, y: 2, z: 4, core: 2. Of those that a mesh axis runs over, the one named last changes fastest.
Arguments:
- features: bfloat16 [4096, 1024], P(('row', 'col')), may hold values from -6 to 6
- weight: bfloat16 [1024, 1024], replicated, may hold values from -0.1875 to 0.1875
- cotangent: bfloat16 [4096, 1024], P(('col', 'row')), may hold values from -6 to 6
- tile_values: bfloat16 [8, 4, 8, 128, 128], P('row', 'col'), may hold values from -0.5 to 0.5
- block_row: int32 [8, 4, 8], P('row', 'col'), may hold values from 0 to 7, as said below
- block_column: int32 [8, 4, 8], P('row', 'col'), may hold values from 0 to 3, as said below
- tile_count: int32 [8, 4], P('row', 'col'), may hold values from 2 to 8, as said below
Outputs:
- activated: bfloat16 [4096, 1024], P(('col', 'row'))
- feat_grad: bfloat16 [4096, 1024], P(('row', 'col'))
- weight_grad: float32 [1024, 1024], replicated
Inputs may be any that keep to these rules, and one draw needn't show every extreme that they name: `block_row`: within one grid position the slots name distinct region cells. `block_column`: within one grid position the slots name distinct region cells. `tile_count`: some grid position has exactly 8 live slots.
All inputs are finite; a program needn't handle non-finite values.
Results may differ from a plain program's by a relative error of at most 0.02.
Values may be sent and summed in bfloat16 or wider, within the bound.
No kernel may reach another device: no remote copies, remote signals or barrier semaphores. Data moves between devices by JAX's collectives and lax.ppermute only.
A program may use at most 128 MiB of HBM per device.

v0:
```python
import jax
import jax.numpy as jnp
from jax import lax
from jax.sharding import PartitionSpec as P


def silu_slope(hidden):
    sigmoid = jax.nn.sigmoid(hidden)
    return sigmoid * (1.0 + hidden * (1.0 - sigmoid))


def spread_tiles(source, tile_block, index_in, index_out, live_count, out_blocks, flipped):
    block_size = tile_block.shape[-1]
    width = source.shape[-1]
    blocks = source.reshape(-1, block_size, width)
    slots = tile_block.shape[0]
    per_turn = 16 if slots % 16 == 0 else 8
    form = "tba,tbf->taf" if flipped else "tab,tbf->taf"

    def add_turn(turn, summed):
        first = turn * per_turn
        matrix = lax.dynamic_slice_in_dim(tile_block, first, per_turn, 0)
        wanted = lax.dynamic_slice_in_dim(index_in, first, per_turn, 0)
        placed = lax.dynamic_slice_in_dim(index_out, first, per_turn, 0)
        is_live = first + jnp.arange(per_turn, dtype=jnp.int32) < live_count
        picked = blocks[wanted]
        products = jnp.einsum(form, matrix, picked, preferred_element_type=jnp.float32)
        products = products * is_live.astype(jnp.float32)[:, None, None]
        return summed.at[placed].add(products)

    turns = (live_count + per_turn - 1) // per_turn
    summed = lax.fori_loop(
        0, turns, add_turn, jnp.zeros((out_blocks, block_size, width), jnp.float32)
    )
    return summed.reshape(out_blocks * block_size, width)


def on_device(features, weight, cotangent, tile_values, block_row, block_column, tile_count):
    row_devices = lax.axis_size("row")
    col_devices = lax.axis_size("col")
    span = features.shape[0]
    block_size = tile_values.shape[-1]
    per_device = span // block_size
    tile_block = tile_values[0, 0]
    rows_index = block_row[0, 0]
    cols_index = block_column[0, 0]
    live_count = tile_count[0, 0]
    projected = jnp.dot(features, weight, preferred_element_type=jnp.float32).astype(jnp.bfloat16)
    gathered = lax.all_gather(projected, "col", axis=0, tiled=True)
    partial_value = spread_tiles(
        gathered, tile_block, cols_index, rows_index, live_count, row_devices * per_device, False
    )
    hidden = lax.psum_scatter(
        partial_value.astype(jnp.bfloat16), "row", scatter_dimension=0, tiled=True
    ).astype(jnp.float32)
    activated = jax.nn.silu(hidden).astype(jnp.bfloat16)
    hidden_grad = (cotangent.astype(jnp.float32) * silu_slope(hidden)).astype(jnp.bfloat16)
    grad_group = lax.all_gather(hidden_grad, "row", axis=0, tiled=True)
    back_partial = spread_tiles(
        grad_group, tile_block, rows_index, cols_index, live_count, col_devices * per_device, True
    )
    feat_delta = lax.psum_scatter(
        back_partial.astype(jnp.bfloat16), "col", scatter_dimension=0, tiled=True
    )
    feat_grad = jnp.dot(feat_delta, weight.T, preferred_element_type=jnp.float32).astype(
        jnp.bfloat16
    )
    weight_terms = lax.dot_general(
        features, feat_delta, (((0,), (0,)), ((), ())), preferred_element_type=jnp.float32
    )
    factor = (span * row_devices * col_devices) ** (-0.5)
    weight_grad = lax.psum(weight_terms, ("row", "col")) * factor
    return (activated, feat_grad, weight_grad)


def solution(mesh):
    return jax.shard_map(
        on_device,
        mesh=mesh,
        in_specs=(
            P(("row", "col"), None),
            P(),
            P(("col", "row"), None),
            P("row", "col", None, None, None),
            P("row", "col", None),
            P("row", "col", None),
            P("row", "col"),
        ),
        out_specs=(P(("col", "row"), None), P(("row", "col"), None), P()),
        check_vma=False,
    )
```

profile of v0, /device:TPU:0, one launch (start us, length us, event | category | flops | bytes accessed | tf_op | source)
XLA Modules:
  0.0 388.5 jit_solution(11174887389354764377)
XLA Ops:
  7.2 1.5 copy-done
  8.8 2.1 convolution_convert_fusion.1
  11.6 18.9 %all-gather.3.cloned.1.call-done = bf16[512,1024]{1,0:T(8,128)(2,1)} async-done(((bf16[128,1024]{1,0:T(8,128)(2,1)}), bf16[512,1024]{1,0:T(8,128)(2,1)}) %all-gather.3.cloned.1.call-update) | async-done | bytes 1048592 | tf_op jit(solution)/shard_map/all_gather | solution.py:49
  30.5 2.5 broadcast_in_dim.4
  33.0 21.8 %while.22 = (s32[]{:T(128)}, f32[8,128,1024]{2,1,0:T(8,128)}, s32[]{:T(128)}, s32[8]{0:T(128)S(1)}, s32[8]{0:T(128)S(1)}, /*index=5*/bf16[4,128,1024]{2,1,0:T(8,...) while((s32[]{:T(128)}, f32[8,128,1024]{2,1,0:T(8,128)}, s32[]{:T(128)}, ...), condition=%wide.region_2.3_spmd, body=%wide.region_0.2_spmd.sunk | while | flops 270533696 | bytes 31723936 | solution.py:32
  33.1 2.0 gather_fusion
  35.1 0.6 compare_convert_fusion.4
  35.7 4.5 %multiply_bitcast_fusion.2 = f32[8,128,1024]{1,2,0:T(8,128)} fusion(bf16[8,128,1024]{2,1,0:T(8,128)(2,1)} %gather_fusion, bf16[8,128,128]{2,1,0:T(8,128)(2,1)S(1)} %get-tuple-element.311, f32[8]{0:T(128)S(1)} %compare_convert_fusion.4), kind=kOutput, calls=%fused_computation.4.clone.1 | convolution fusion | flops 269484032 | bytes 6553632 | tf_op jit(solution)/shard_map/while/body/tab,tbf->taf/dot_general | solution.py:27
  40.3 5.4 %copy.18 = f32[8,128,1024]{2,1,0:T(8,128)} copy(f32[8,128,1024]{1,2,0:T(8,128)} %multiply_bitcast_fusion.2) | data formatting | bytes 8388608 | tf_op jit(solution)/shard_map/while/body/mul | solution.py:28
  45.6 9.2 %scatter_fusion = f32[8,128,1024]{2,1,0:T(8,128)} fusion(f32[8,128,1024]{2,1,0:T(8,128)} %get-tuple-element.296, s32[8]{0:T(128)S(1)} %get-tuple-element.276, f32[8,128,1024]{2,1,0:T(8,128)} %copy.18), kind=kCustom, calls=%fused_computation.2.clone.1 | custom fusion | flops 1048576 | bytes 12582944 | tf_op jit(solution)/shard_map/while/body/scatter-add | solution.py:29
  54.9 3.8 convert_element_type.47
  58.7 0.0 all-gather.5.cloned.1.call-start
  58.8 67.7 %reduce-scatter.3.cloned.1.call-done = bf16[128,1024]{1,0:T(8,128)(2,1)} async-done(((bf16[1024,1024]{1,0:T(8,128)(2,1)}), bf16[128,1024]{1,0:T(8,128)(2,1)}) %reduce-scatter.3.cloned.1.call-update) | async-done | bytes 262160 | tf_op jit(solution)/shard_map/reduce_scatter | solution.py:53
  126.5 2.0 fusion.10
  128.5 0.0 reduce-scatter.5.cloned.1.call-start
  128.5 0.2 copy.12
  128.7 48.8 %all-gather.5.cloned.1.call-done = bf16[1024,1024]{1,0:T(8,128)(2,1)} async-done(((bf16[128,1024]{1,0:T(8,128)(2,1)}), bf16[1024,1024]{1,0:T(8,128)(2,1)}) %all-gather.5.cloned.1.call-update) | async-done | bytes 2097168 | tf_op jit(solution)/shard_map/all_gather | solution.py:58
  177.5 3.6 gather_fusion.1
  181.1 1.6 broadcast_in_dim.8
  182.7 14.0 %while.23 = (s32[]{:T(128)}, f32[4,128,1024]{2,1,0:T(8,128)}, s32[]{:T(128)}, s32[8]{0:T(128)S(1)}, bf16[8,128,128]{1,2,0:T(8,128)(2,1)S(1)}, /*index=5*/bf16[8,...) while((s32[]{:T(128)}, f32[4,128,1024]{2,1,0:T(8,128)}, s32[]{:T(128)}, s32[8]{0:T(128)S(1)}, ...), condition=%wide.region_6.7_spmd, body=%wide.region_4.6_spmd.sunk | while | flops 270532672 | bytes 19136792 | solution.py:32
  182.7 0.6 compare_convert_fusion.5
  183.3 4.3 %convolution_multiply_fusion.2 = f32[8,128,1024]{2,1,0:T(8,128)} fusion(bf16[8,128,128]{1,2,0:T(8,128)(2,1)S(1)} %get-tuple-element.337, bf16[8,128,1024]{2,1,0:T(8,128)(2,1)} %get-tuple-element.338, f32[8]{0:T(128)S(1)} %compare_convert_fusion.5), kind=kOutput, calls=%fused_computation.11.clone.1 | convolution fusion | flops 269484032 | bytes 6553632 | tf_op jit(solution)/shard_map/while/body/tba,tbf->taf/dot_general | solution.py:27
  187.6 9.1 %scatter_fusion.1 = f32[4,128,1024]{2,1,0:T(8,128)} fusion(f32[4,128,1024]{2,1,0:T(8,128)} %get-tuple-element.325, s32[8]{0:T(128)S(1)} %fusion.33, f32[8,128,1024]{2,1,0:T(8,128)} %convolution_multiply_fusion.2), kind=kCustom, calls=%fused_computation.3.clone.1 | custom fusion | flops 1048576 | bytes 12582944 | tf_op jit(solution)/shard_map/while/body/scatter-add | solution.py:29
  196.7 2.8 convert_element_type.53
  199.5 0.0 all-reduce.2.cloned.1.call-start
  199.5 23.5 %reduce-scatter.5.cloned.1.call-done = bf16[128,1024]{1,0:T(8,128)(2,1)} async-done(((bf16[512,1024]{1,0:T(8,128)(2,1)}), bf16[128,1024]{1,0:T(8,128)(2,1)}) %reduce-scatter.5.cloned.1.call-update) | async-done | bytes 262160 | tf_op jit(solution)/shard_map/reduce_scatter | solution.py:62
  223.1 3.7 convolution_bitcast_fusion
  226.8 0.9 copy-done.4
  227.7 1.5 convolution_convert_fusion
  229.2 142.5 %all-reduce.2.cloned.1.call-done = f32[1024,1024]{0,1:T(8,128)} async-done(((f32[1024,1024]{0,1:T(8,128)}), f32[1024,1024]{0,1:T(8,128)}) %all-reduce.2.cloned.1.call-update) | async-done | bytes 4194320 | tf_op jit(solution)/shard_map/psum | solution.py:72
  371.7 5.0 %broadcast_multiply_fusion = f32[1024,1024]{0,1:T(8,128)} fusion(f32[1024,1024]{0,1:T(8,128)} %all-reduce.2.cloned.1.call-done), kind=kLoop, calls=%fused_computation.16 | loop fusion | flops 1048576 | bytes 8388608 | tf_op jit(solution)/shard_map/mul | solution.py:72
  376.7 5.3 %copy.14 = f32[1024,1024]{1,0:T(8,128)} copy(f32[1024,1024]{0,1:T(8,128)} %broadcast_multiply_fusion) | data formatting | bytes 8388608
  (26 shorter events, 0.2 us)
Async XLA Ops:
  7.2 1.6 copy-start
  7.2 23.3 %all-gather.3.cloned.1.call-start = ((), (), s32[]{:S(2)}) async-start(), calls=%async_computation.2 | async-start | bytes 1310720 | tf_op jit(solution)/shard_map/all_gather | solution.py:49
  10.9 115.6 %reduce-scatter.3.cloned.1.call-start = ((), (), s32[]{:S(2)}) async-start(), calls=%async_computation.3 | async-start | bytes 2359296 | tf_op jit(solution)/shard_map/reduce_scatter | solution.py:53
  30.5 2.6 copy-start.1
  30.5 2.6 copy-start.2
  30.5 2.6 copy-start.6
  30.5 2.6 copy-start.7
  58.7 67.8 %copy-start.5 = (bf16[128,1024]{1,0:T(8,128)(2,1)S(1)}, bf16[128,1024]{1,0:T(8,128)(2,1)}, u32[]{:S(2)}) copy-start(bf16[128,1024]{1,0:T(8,128)(2,1)} %param.13) | copy-start | bytes 786436
  58.7 118.8 %all-gather.5.cloned.1.call-start = ((), (), s32[]{:S(2)}) async-start(), calls=%async_computation.4 | async-start | bytes 2359296 | tf_op jit(solution)/shard_map/all_gather | solution.py:58
  128.5 94.6 %reduce-scatter.5.cloned.1.call-start = ((), (), s32[]{:S(2)}) async-start(), calls=%async_computation.5 | async-start | bytes 1310720 | tf_op jit(solution)/shard_map/reduce_scatter | solution.py:62
  196.7 26.4 %copy-start.3 = (bf16[128,1024]{1,0:T(8,128)(2,1)S(1)}, bf16[128,1024]{1,0:T(8,128)(2,1)}, u32[]{:S(2)}) copy-start(bf16[128,1024]{1,0:T(8,128)(2,1)} %param.11) | copy-start | bytes 786436
  199.5 172.2 %all-reduce.2.cloned.1.call-start = ((), (), s32[]{:S(2)}) async-start(), calls=%async_computation.6 | async-start | bytes 8388608 | tf_op jit(solution)/shard_map/psum | solution.py:72
  226.7 0.9 copy-start.4
Sparse Core Ops, SparseCore 0:
  11.0 19.4 all-gather.2
  58.9 67.5 reduce-scatter.2
  129.2 48.2 all-gather.4
  199.6 23.3 reduce-scatter.4
  229.9 141.7 all-reduce.1
where the time goes:
time: 389 us
  waiting for transfers between devices  301 us (77%)
  other arithmetic  33.2 us (9%)
  local copies, waits for them, and re-layouts  23.1 us (6%)
  matrix products  16.2 us (4%)
  between operations  14.5 us (4%)
    psum x1, waiting for transfers between devices, on_device(): weight_grad = lax.psum(weight_terms, ('row', 'col')) * factor  142 us
    reduce_scatter x1, waiting for transfers between devices, on_device(): lax.psum_scatter(partial_value.astype(jnp.bfloat16), 'row', scatter_dimen...  67.7 us
    all_gather x1, waiting for transfers between devices, on_device(): grad_group = lax.all_gather(hidden_grad, 'row', axis=0, tiled=True)  48.8 us
    reduce_scatter x1, waiting for transfers between devices, on_device(): lax.psum_scatter(back_partial.astype(jnp.bfloat16), 'col', scatter_dimens...  23.5 us
    all_gather x1, waiting for transfers between devices, on_device(): gathered = lax.all_gather(projected, 'col', axis=0, tiled=True)  18.9 us
    scatter-add x2, other arithmetic, add_turn(): return summed.at[placed].add(products)  18.3 us
    dot_general x2, matrix products, add_turn(): jnp.einsum(form, matrix, picked, preferred_element_type=jnp.float32)  8.84 us
    unnamed x18, local copies, waits for them, and re-layouts  8.01 us
  transfers between devices with their start and end apart: 5, of which 5 were waited for; matrix products, arithmetic and copies ran while one was open for 0% of the time, Pallas kernels for 0%

commit v1 on v0

v1 whole, which is shorter than its diff:
```python
import functools

import jax
import jax.numpy as jnp
from jax import lax
from jax.experimental import pallas as pl
from jax.experimental.pallas import tpu as pltpu
from jax.sharding import PartitionSpec as P

BF16 = jnp.bfloat16
F32 = jnp.float32
VMEM_LIMIT = 56 * 2**20
SMEM_SPEC = pl.BlockSpec(memory_space=pltpu.SMEM)
VMEM_SPEC = pl.BlockSpec(memory_space=pltpu.VMEM)


class Grid:
    def __init__(self, rows, cols):
        self.R, self.C = rows, cols
        self.X = 2 if rows % 2 == 0 else 1
        self.K = 2 if cols % 2 == 0 else 1
        self.Z, self.Y = rows // self.X, cols // self.K

    def move(self, value, dz=0, dx=0, dy=0, dcore=0):
        pairs = []
        for z in range(self.Z):
            for x in range(self.X):
                for y in range(self.Y):
                    for k in range(self.K):
                        source = (z * self.X + x) * self.C + y * self.K + k
                        row = ((z + dz) % self.Z) * self.X + (x ^ dx)
                        col = ((y + dy) % self.Y) * self.K + (k ^ dcore)
                        pairs.append((source, row * self.C + col))
        return lax.ppermute(value, ("row", "col"), pairs)


def params(**more):
    return pltpu.CompilerParams(vmem_limit_bytes=VMEM_LIMIT, **more)


def build_kernel(g, slots, block, n_sources, *refs):
    place = refs[0]
    lists = refs[1 : 1 + n_sources]
    tiles = refs[1 + n_sources : 1 + 2 * n_sources]
    forward, backward = refs[1 + 2 * n_sources :]
    z, x, y, core = place[0], place[1], place[2], place[3]
    forward[...] = jnp.zeros_like(forward)
    backward[...] = jnp.zeros_like(backward)
    for source in range(n_sources):
        s_core, s_x = source // g.X, source % g.X
        listed, held = lists[source], tiles[source]

        @pl.loop(0, slots)
        def _(s):
            block_row, block_col = listed[s], listed[slots + s]
            z_out, x_out = lax.div(block_row, g.X), lax.rem(block_row, g.X)
            y_in, core_in = lax.div(block_col, g.K), lax.rem(block_col, g.K)
            dz = lax.rem(z_out - z + g.Z, g.Z)
            dy = lax.rem(y - y_in + g.Y, g.Y)
            dcore = jnp.where(core_in == core, 0, 1)
            live = jnp.logical_and(s < listed[2 * slots], x_out == x)
            if s_core == 0:

                @pl.when(live)
                def _():
                    at = s_x * g.C + dy * g.K + dcore
                    forward[
                        pl.ds(pl.multiple_of(dz * block, block), block),
                        pl.ds(pl.multiple_of(at * block, block), block),
                    ] = held[s]

            @pl.when(jnp.logical_and(live, dcore == 0))
            def _():
                out = s_x * g.Y + dy
                at = s_core * g.Z + dz
                backward[
                    pl.ds(pl.multiple_of(out * block, block), block),
                    pl.ds(pl.multiple_of(at * block, block), block),
                ] = held[s].astype(F32).T.astype(BF16)


def build(g, place, lists, tiles):
    slots, block = tiles[0].shape[0], tiles[0].shape[1]
    forward = (g.Z * block, g.X * g.C * block)
    backward = (g.X * g.Y * block, g.K * g.Z * block)
    return pl.pallas_call(
        functools.partial(build_kernel, g, slots, block, len(tiles)),
        out_shape=[jax.ShapeDtypeStruct(forward, BF16), jax.ShapeDtypeStruct(backward, BF16)],
        in_specs=[SMEM_SPEC] * (1 + len(lists)) + [VMEM_SPEC] * len(tiles),
        out_specs=[VMEM_SPEC] * 2,
        compiler_params=params(),
        name="build",
    )(place, *lists, *tiles)


def spread_kernel(n_in, block, matrix, *refs):
    stacked = jnp.concatenate([r[...] for r in refs[:n_in]], axis=0)
    total = jnp.dot(matrix[...], stacked, preferred_element_type=F32)
    for i, out in enumerate(refs[n_in:]):
        out[...] = total[i * block : (i + 1) * block].astype(BF16)


def spread(matrix, blocks, name):
    block, width = blocks[0].shape
    n_out = matrix.shape[0] // block
    tile = 256 if width % 256 == 0 else width
    spec = pl.BlockSpec((block, tile), lambda j: (0, j))
    return pl.pallas_call(
        functools.partial(spread_kernel, len(blocks), block),
        grid=(width // tile,),
        out_shape=[jax.ShapeDtypeStruct((block, width), BF16)] * n_out,
        in_specs=[pl.BlockSpec(matrix.shape, lambda j: (0, 0))] + [spec] * len(blocks),
        out_specs=[spec] * n_out,
        compiler_params=params(),
        cost_estimate=pl.CostEstimate(
            flops=2 * matrix.size * width,
            bytes_accessed=2 * (matrix.size + (len(blocks) + n_out) * block * width),
            transcendentals=0,
        ),
        name=name,
    )(matrix, *blocks)


def layer_kernel(n_in, place, *refs):
    parts = refs[:n_in]
    weight, cotangent = refs[n_in : n_in + 2]
    activated, hidden_grad, back, keep, send = refs[n_in + 2 : n_in + 7]
    agg, total = refs[n_in + 7 :]
    j, last = pl.program_id(0), pl.num_programs(0) - 1
    half = keep.shape[1]

    @pl.when(j == 0)
    def _():
        summed = parts[0][...].astype(F32)
        for part in parts[1:]:
            summed += part[...].astype(F32)
        agg[...] = summed.astype(BF16)
        total[...] = jnp.zeros_like(total)
        core = place[3]
        keep[...] = agg[:, pl.ds(pl.multiple_of(core * half, half), half)]
        send[...] = agg[:, pl.ds(pl.multiple_of((1 - core) * half, half), half)]

    hidden = jnp.dot(agg[...], weight[...], preferred_element_type=F32)
    sigmoid = jax.nn.sigmoid(hidden)
    activated[...] = (hidden * sigmoid).astype(BF16)
    slope = sigmoid * (1.0 + hidden * (1.0 - sigmoid))
    grad = (cotangent[...].astype(F32) * slope).astype(BF16)
    hidden_grad[...] = grad
    total[...] += lax.dot_general(
        grad, weight[...], (((1,), (1,)), ((), ())), preferred_element_type=F32
    )

    @pl.when(j == last)
    def _():
        back[...] = total[...].astype(BF16)


def layer(place, parts, weight, cotangent):
    rows, depth = parts[0].shape
    width = weight.shape[1]
    tile = 256 if width % 256 == 0 else width
    whole = pl.BlockSpec((rows, depth), lambda j: (0, 0))
    half = pl.BlockSpec((rows, depth // 2), lambda j: (0, 0))
    cut = pl.BlockSpec((rows, tile), lambda j: (0, j))
    return pl.pallas_call(
        functools.partial(layer_kernel, len(parts)),
        grid=(width // tile,),
        out_shape=[
            jax.ShapeDtypeStruct((rows, width), BF16),
            jax.ShapeDtypeStruct((rows, width), BF16),
            jax.ShapeDtypeStruct((rows, depth), BF16),
            jax.ShapeDtypeStruct((rows, depth // 2), BF16),
            jax.ShapeDtypeStruct((rows, depth // 2), BF16),
        ],
        in_specs=[SMEM_SPEC]
        + [whole] * len(parts)
        + [pl.BlockSpec((depth, tile), lambda j: (0, j)), cut],
        out_specs=[cut, cut, whole, half, half],
        scratch_shapes=[pltpu.VMEM((rows, depth), BF16), pltpu.VMEM((rows, depth), F32)],
        compiler_params=params(),
        cost_estimate=pl.CostEstimate(
            flops=4 * rows * depth * width,
            bytes_accessed=2 * (depth * width + 9 * rows * width),
            transcendentals=rows * width,
        ),
        name="layer",
    )(place, *parts, weight, cotangent)


def terms_kernel(g, place, keep, got, grad, grad_got, *refs):
    outs, turned = refs[:-1], refs[-1]
    both = jnp.concatenate([keep[...].astype(F32), got[...].astype(F32)], axis=0)
    turned[...] = both.T.astype(BF16)
    grads = jnp.concatenate([grad[...], grad_got[...]], axis=0)
    x, y = place[1], place[2]
    rows = outs[0].shape[0]
    for dx in range(g.X):
        for dy in range(g.Y):
            at = (x if dx == 0 else 1 - x) * g.Y + lax.rem(y + dy, g.Y)
            mine = turned[pl.ds(pl.multiple_of(at * rows, rows), rows), :]
            outs[dx * g.Y + dy][...] = jnp.dot(
                mine, grads, preferred_element_type=F32
            ).astype(BF16)


def terms(g, place, keep, got, grad, grad_got):
    nodes, half = keep.shape
    width = grad.shape[1]
    n_out = g.X * g.Y
    return pl.pallas_call(
        functools.partial(terms_kernel, g),
        out_shape=[jax.ShapeDtypeStruct((half // n_out, width), BF16)] * n_out,
        in_specs=[SMEM_SPEC] + [VMEM_SPEC] * 4,
        out_specs=[VMEM_SPEC] * n_out,
        scratch_shapes=[pltpu.VMEM((half, 2 * nodes), BF16)],
        compiler_params=params(),
        cost_estimate=pl.CostEstimate(
            flops=4 * nodes * half * width,
            bytes_accessed=2 * half * width,
            transcendentals=0,
        ),
        name="terms",
    )(place, keep, got, grad, grad_got)


def split_kernel(g, n_in, place, *refs):
    outs, held = refs[n_in:-1], refs[-1]
    summed = refs[0][...].astype(F32)
    for part in refs[1:n_in]:
        summed += part[...].astype(F32)
    held[...] = summed.astype(BF16)
    width = outs[0].shape[1]
    for k, out in enumerate(outs):
        at = lax.rem(place[0] + k, g.Z)
        out[...] = held[:, pl.ds(pl.multiple_of(at * width, width), width)]


def split(g, place, parts):
    rows, width = parts[0].shape
    return pl.pallas_call(
        functools.partial(split_kernel, g, len(parts)),
        out_shape=[jax.ShapeDtypeStruct((rows, width // g.Z), BF16)] * g.Z,
        in_specs=[SMEM_SPEC] + [VMEM_SPEC] * len(parts),
        out_specs=[VMEM_SPEC] * g.Z,
        scratch_shapes=[pltpu.VMEM((rows, width), BF16)],
        compiler_params=params(),
        name="split",
    )(place, *parts)


def join_kernel(g, place, *refs):
    out = refs[-1]
    rows, width = refs[0].shape[1], refs[0].shape[2]
    z, x, y, core = place[0], place[1], place[2], place[3]
    for dcore in range(g.K):
        for dx in range(g.X):
            for dy in range(g.Y):
                held = refs[(dcore * g.X + dx) * g.Y + dy]
                at_core = core if dcore == 0 else 1 - core
                at_x = x if dx == 0 else 1 - x
                at = (at_core * g.X + at_x) * g.Y + lax.rem(y - dy + g.Y, g.Y)
                for dz in range(g.Z):
                    col = lax.rem(z - dz + g.Z, g.Z)
                    out[
                        pl.ds(pl.multiple_of(at * rows, rows), rows),
                        pl.ds(pl.multiple_of(col * width, width), width),
                    ] = held[dz].astype(F32)


def join(g, place, pieces, shape):
    return pl.pallas_call(
        functools.partial(join_kernel, g),
        out_shape=jax.ShapeDtypeStruct(shape, F32),
        in_specs=[SMEM_SPEC] + [VMEM_SPEC] * len(pieces),
        out_specs=VMEM_SPEC,
        compiler_params=params(),
        name="join",
    )(place, *pieces)


def on_device(g, features, weight, cotangent, tile_values, block_row, block_column, tile_count):
    r, c = lax.axis_index("row"), lax.axis_index("col")
    place = jnp.stack([r // g.X, r % g.X, c // g.K, c % g.K]).astype(jnp.int32)
    squares = [(dx, dy) for dx in range(g.X) for dy in range(g.Y)]
    moves = [(dx, dy) for dx, dy in squares if (dx, dy) != (0, 0)]

    near = {(0, 0): features}
    for dx, dy in moves:
        near[dx, dy] = g.move(features, dx=dx, dy=dy)
    listed = jnp.concatenate([block_row[0, 0], block_column[0, 0], tile_count[0]])
    lists, tiles = [listed], [tile_values[0, 0]]
    if g.X == 2:
        lists.append(g.move(listed, dx=1))
        tiles.append(g.move(tiles[0], dx=1))
    if g.K == 2:
        lists += [g.move(v, dcore=1) for v in lists]
        tiles += [g.move(v, dcore=1) for v in tiles]
    forward, backward = build(g, place, lists, tiles)
    blocks = []
    for at in squares:
        blocks.append(near[at])
        if g.K == 2:
            blocks.append(g.move(near[at], dcore=1))

    sums = spread(forward, blocks, "spread_forward")
    parts = [sums[0]] + [g.move(sums[k], dz=k) for k in range(1, g.Z)]
    activated, hidden_grad, back, keep, send = layer(place, parts, weight, cotangent)

    mine = [back] + [None] * (g.Z - 1)
    for k in range(1, g.Z):
        mine[(g.Z - k) % g.Z] = g.move(back, dz=k)
    backs = list(mine)
    if g.K == 2:
        backs += [g.move(v, dcore=1) for v in mine]
    deltas = spread(backward, backs, "spread_backward")
    feat = deltas[0].astype(F32)
    for i, (dx, dy) in enumerate(squares):
        if (dx, dy) != (0, 0):
            feat += g.move(deltas[i], dx=dx, dy=-dy).astype(F32)
    feat_grad = feat.astype(BF16)

    got, grad_got = g.move(send, dcore=1), g.move(hidden_grad, dcore=1)
    shares = terms(g, place, keep, got, hidden_grad, grad_got)
    shares = [
        v if at == (0, 0) else g.move(v, dx=at[0], dy=at[1]) for at, v in zip(squares, shares)
    ]
    pieces = split(g, place, shares)
    total = pieces[0].astype(F32)
    for k in range(1, g.Z):
        total += g.move(pieces[k], dz=k).astype(F32)
    factor = (features.shape[0] * g.R * g.C) ** (-0.5)
    own = (total * factor).astype(BF16)
    column = jnp.stack([own] + [g.move(own, dz=k) for k in range(1, g.Z)])
    held = [column if at == (0, 0) else g.move(column, dx=at[0], dy=at[1]) for at in squares]
    if g.K == 2:
        held += [g.move(v, dcore=1) for v in held]
    weight_grad = join(g, place, held, weight.shape)
    return (activated, feat_grad, weight_grad)


def solution(mesh):
    g = Grid(mesh.shape["row"], mesh.shape["col"])
    return jax.shard_map(
        functools.partial(on_device, g),
        mesh=mesh,
        in_specs=(
            P(("row", "col"), None),
            P(),
            P(("col", "row"), None),
            P("row", "col", None, None, None),
            P("row", "col", None),
            P("row", "col", None),
            P("row", "col"),
        ),
        out_specs=(P(("col", "row"), None), P(("row", "col"), None), P()),
        check_vma=False,
    )
```

time: 389 us -> 148 us (0.38)
  waiting for transfers between devices: 301 us -> 63.8 us
  starting transfers between devices: 0.21 us -> 43.4 us
  other arithmetic: 33.2 us -> 4.17 us
  Pallas kernels: 0 us -> 27.6 us
  local copies, waits for them, and re-layouts: 23.1 us -> 6.14 us
  matrix products: 16.2 us -> 0 us
  between operations: 14.5 us -> 1.68 us
    psum x1 -> x0, waiting for transfers between devices: 142 us -> none  [on_device(): weight_grad = lax.psum(weight_terms, ('row', 'col')) * factor]
    reduce_scatter x2 -> x0, waiting for transfers between devices: 91.2 us -> none  [the longest x1 67.7 us: on_device(): lax.psum_scatter(partial_value.astype(jnp.bfloat16), 'row', scatter_dimen...]
    all_gather x2 -> x0, waiting for transfers between devices: 67.6 us -> none  [the longest x1 48.8 us: on_device(): grad_group = lax.all_gather(hidden_grad, 'row', axis=0, tiled=True)]
    ppermute x0 -> x44, waiting for transfers between devices: none -> 63.8 us  [move(): return lax.ppermute(value, ('row', 'col'), pairs)]
    ppermute x0 -> x44, starting transfers between devices: none -> 43.4 us  [move(): return lax.ppermute(value, ('row', 'col'), pairs)]
    pallas_call x0 -> x7, Pallas kernels: none -> 27.6 us  [the longest x2 9.64 us: spread(): pl.pallas_call(functools.partial(spread_kernel, len(blocks), block), grid...]
    scatter-add x2 -> x0, other arithmetic: 18.3 us -> none  [add_turn(): return summed.at[placed].add(products)]
    dot_general x5 -> x0, matrix products: 16.2 us -> none  [the longest x2 8.84 us: add_turn(): jnp.einsum(form, matrix, picked, preferred_element_type=jnp.float32)]
  transfers between devices with their start and end apart: 5 -> 44, of which waited for: 5 -> 13; matrix products, arithmetic and copies ran while one was open for 0% -> 2% of each run, Pallas kernels for 0% -> 9%
where the time goes in v1:
time: 148 us; the launch traced here: 147 us
  waiting for transfers between devices  63.8 us (43%)
  starting transfers between devices  43.4 us (29%)
  Pallas kernels  27.6 us (19%)
  local copies, waits for them, and re-layouts  6.14 us (4%)
  other arithmetic  4.17 us (3%)
  between operations  1.68 us (1%)
    ppermute x44, waiting for transfers between devices, move(): return lax.ppermute(value, ('row', 'col'), pairs)  63.8 us
    ppermute x44, starting transfers between devices, move(): return lax.ppermute(value, ('row', 'col'), pairs)  43.4 us
    pallas_call x2, Pallas kernels, spread(): pl.pallas_call(functools.partial(spread_kernel, len(blocks), block), grid...  9.64 us
    unnamed x74, local copies, waits for them, and re-layouts  6.14 us
    pallas_call x1, Pallas kernels, layer(): pl.pallas_call(functools.partial(layer_kernel, len(parts)), grid=(width /...  5.44 us
    pallas_call x1, Pallas kernels, build(): pl.pallas_call(functools.partial(build_kernel, g, slots, block, len(tiles...  4.11 us
    pallas_call x1, Pallas kernels, join(): pl.pallas_call(functools.partial(join_kernel, g), out_shape=jax.ShapeDtyp...  3.81 us
  transfers between devices with their start and end apart: 44, of which 13 were waited for; matrix products, arithmetic and copies ran while one was open for 2% of the time, Pallas kernels for 9%

profile of v1, /device:TPU:0, one launch (start us, length us, event | category | flops | bytes accessed | tf_op | source)
XLA Modules:
  0.0 146.9 jit_solution(6040501718912705886)
XLA Ops:
  2.5 2.6 %collective-permute-start = (s32[17]{0:T(128)S(1)}, s32[17]{0:T(128)S(1)}, u32[]{:S(2)}, u32[]{:S(2)}) collective-permute-start(s32[17]{0:T(128)S(1)} %pad_add_fusion.1.refs_1_), channel_id=1, source_target_pairs={{0,4},{1,5},{2,6},{3,7},{4,0},{5,1},{6,2},{7,3},{8,12},{9,13},{10,... | collective-permute-start | bytes 212 | tf_op jit(solution)/shard_map/ppermute | solution.py:34
  5.5 1.8 %collective-permute-start.9 = (bf16[128,1024]{1,0:T(8,128)(2,1)}, bf16[128,1024]{1,0:T(8,128)(2,1)S(1)}, u32[]{:S(2)}, u32[]{:S(2)}) collective-permute-start(bf16[128,1024]{1,0:T(8,128)(2,1)} %refs_0_.1), channel_id=1, source_target_pairs={{0,4},{1,5},{2,6},{3,7},{4,0},{5,1},{6,2},{7,3},{8,12},{9,13},{10,... | collective-permute-start | bytes 786440 | tf_op jit(solution)/shard_map/ppermute | solution.py:34
  7.3 1.6 %collective-permute-start.7 = (bf16[128,1024]{1,0:T(8,128)(2,1)}, bf16[128,1024]{1,0:T(8,128)(2,1)S(1)}, u32[]{:S(2)}, u32[]{:S(2)}) collective-permute-start(bf16[128,1024]{1,0:T(8,128)(2,1)} %refs_0_.1), channel_id=1, source_target_pairs={{0,2},{1,3},{2,0},{3,1},{4,6},{5,7},{6,4},{7,5},{8,10},{9,11},{10,... | collective-permute-start | bytes 786440 | tf_op jit(solution)/shard_map/ppermute | solution.py:34
  8.9 1.8 %collective-permute-start.11 = (bf16[128,1024]{1,0:T(8,128)(2,1)}, bf16[128,1024]{1,0:T(8,128)(2,1)S(1)}, u32[]{:S(2)}, u32[]{:S(2)}) collective-permute-start(bf16[128,1024]{1,0:T(8,128)(2,1)} %refs_0_.1), channel_id=1, source_target_pairs={{0,6},{1,7},{2,4},{3,5},{4,2},{5,3},{6,0},{7,1},{8,14},{9,15},{10,... | collective-permute-start | bytes 786440 | tf_op jit(solution)/shard_map/ppermute | solution.py:34
  10.7 3.9 %collective-permute-done.3.refs_6_ = bf16[8,128,128]{2,1,0:T(8,128)(2,1)S(1)} collective-permute-done((bf16[8,128,128]{2,1,0:T(8,128)(2,1)}, bf16[8,128,128]{2,1,0:T(8,128)(2,1)S(1)}, u32[]{:S(2)}, u32[]{:S(2)}) %collective-permute-start.3) | collective-permute-done | bytes 262176 | tf_op jit(solution)/shard_map/ppermute | solution.py:34
  14.6 5.6 %collective-permute-done.9.refs_4_ = bf16[128,1024]{1,0:T(8,128)(2,1)S(1)} collective-permute-done((bf16[128,1024]{1,0:T(8,128)(2,1)}, bf16[128,1024]{1,0:T(8,128)(2,1)S(1)}, u32[]{:S(2)}, u32[]{:S(2)}) %collective-permute-start.9) | collective-permute-done | bytes 262176 | tf_op jit(solution)/shard_map/ppermute | solution.py:34
  20.7 5.5 %collective-permute-done.11.refs_6_ = bf16[128,1024]{1,0:T(8,128)(2,1)S(1)} collective-permute-done((bf16[128,1024]{1,0:T(8,128)(2,1)}, bf16[128,1024]{1,0:T(8,128)(2,1)S(1)}, u32[]{:S(2)}, u32[]{:S(2)}) %collective-permute-start.11) | collective-permute-done | bytes 262176 | tf_op jit(solution)/shard_map/ppermute | solution.py:34
  27.6 4.1 %build.1 = (bf16[512,1024]{1,0:T(8,128)(2,1)}, bf16[512,1024]{1,0:T(8,128)(2,1)}) custom-call(s32[4]{0:T(128)} %pad_add_fusion.refs_0_.place, s32[17]{0:T(128)} %copy-done.17, s32[17]{0:T(128)} %copy-done.19, s32[17]{0:T(128)} %copy-done.18, s32[17]{0:T(128)} %copy-done.20, bf16[8,128,128]{2,1,0:T(8,128)(2,1)} %bitcast.15, bf16[8,128,128]{2,1,0:T(8,128)(2,1)} %copy-done.12, ...), custom_call_target="tpu_custom_call" | custom-call | tf_op jit(solution)/shard_map/build/pallas_call | solution.py:86
  32.7 4.8 %spread_forward.1 = (bf16[128,1024]{1,0:T(8,128)(2,1)}, bf16[128,1024]{1,0:T(8,128)(2,1)}, bf16[128,1024]{1,0:T(8,128)(2,1)}, bf16[128,1024]{1,0:T(8,128)(2,1)}) custom-call(bf16[512,1024]{1,0:T(8,128)(2,1)} %get-tuple-element.26.matrix, bf16[128,1024]{1,0:T(8,128)(2,1)} %refs_0_.1, bf16[128,1024]{1,0:T(8,128)(2,1)} %copy-done.24, ...), custom_call_target="tpu_custom_call" | custom-call | flops 1073741824 | bytes 4194304 | tf_op jit(solution)/shard_map/spread_forward/pallas_call | solution.py:108
  37.5 1.8 %collective-permute-start.13 = (bf16[128,1024]{1,0:T(8,128)(2,1)}, bf16[128,1024]{1,0:T(8,128)(2,1)S(1)}, u32[]{:S(2)}, u32[]{:S(2)}) collective-permute-start(bf16[128,1024]{1,0:T(8,128)(2,1)} %get-tuple-element.28), channel_id=1, source_target_pairs={{0,8},{1,9},{2,10},{3,11},{4,12},{5,13},{6,14},{7,15},{8,16},{9,17... | collective-permute-start | bytes 786440 | tf_op jit(solution)/shard_map/ppermute | solution.py:34
  39.3 1.8 %collective-permute-start.14 = (bf16[128,1024]{1,0:T(8,128)(2,1)}, bf16[128,1024]{1,0:T(8,128)(2,1)S(1)}, u32[]{:S(2)}, u32[]{:S(2)}) collective-permute-start(bf16[128,1024]{1,0:T(8,128)(2,1)} %get-tuple-element.29), channel_id=1, source_target_pairs={{0,16},{1,17},{2,18},{3,19},{4,20},{5,21},{6,22},{7,23},{8,24},{9,... | collective-permute-start | bytes 786440 | tf_op jit(solution)/shard_map/ppermute | solution.py:34
  41.2 1.8 %collective-permute-start.15 = (bf16[128,1024]{1,0:T(8,128)(2,1)}, bf16[128,1024]{1,0:T(8,128)(2,1)S(1)}, u32[]{:S(2)}, u32[]{:S(2)}) collective-permute-start(bf16[128,1024]{1,0:T(8,128)(2,1)} %get-tuple-element.30), channel_id=1, source_target_pairs={{0,24},{1,25},{2,26},{3,27},{4,28},{5,29},{6,30},{7,31},{8,0},{9,1... | collective-permute-start | bytes 786440 | tf_op jit(solution)/shard_map/ppermute | solution.py:34
  43.0 5.8 %collective-permute-done.13.refs_1_ = bf16[128,1024]{1,0:T(8,128)(2,1)S(1)} collective-permute-done((bf16[128,1024]{1,0:T(8,128)(2,1)}, bf16[128,1024]{1,0:T(8,128)(2,1)S(1)}, u32[]{:S(2)}, u32[]{:S(2)}) %collective-permute-start.13) | collective-permute-done | bytes 262176 | tf_op jit(solution)/shard_map/ppermute | solution.py:34
  48.8 10.9 %collective-permute-done.14.refs_2_ = bf16[128,1024]{1,0:T(8,128)(2,1)S(1)} collective-permute-done((bf16[128,1024]{1,0:T(8,128)(2,1)}, bf16[128,1024]{1,0:T(8,128)(2,1)S(1)}, u32[]{:S(2)}, u32[]{:S(2)}) %collective-permute-start.14) | collective-permute-done | bytes 262176 | tf_op jit(solution)/shard_map/ppermute | solution.py:34
  60.5 5.4 %layer.1 = (bf16[128,1024]{1,0:T(8,128)(2,1)}, bf16[128,1024]{1,0:T(8,128)(2,1)}, bf16[128,1024]{1,0:T(8,128)(2,1)}, bf16[128,512]{1,0:T(8,128)(2,1)}, bf16[128,512]{1,0:T(8,128)(2,1)}) custom-call(s32[4]{0:T(128)} %pad_add_fusion.refs_0_.place, bf16[128,1024]{1,0:T(8,128)(2,1)} %get-tuple-element.27.refs_0_, bf16[128,1024]{1,0:T(8,128)(2,1)} %copy-done.8, ...), custom_call_target="tpu_custom_call" | custom-call | flops 536870912 | bytes 4456448 | tf_op jit(solution)/shard_map/layer/pallas_call | solution.py:165
  66.5 6.0 %collective-permute-start.18 = (bf16[128,1024]{1,0:T(8,128)(2,1)}, bf16[128,1024]{1,0:T(8,128)(2,1)S(1)}, u32[]{:S(2)}, u32[]{:S(2)}) collective-permute-start(bf16[128,1024]{1,0:T(8,128)(2,1)} %get-tuple-element.33.refs_0_), channel_id=1, source_target_pairs={{0,8},{1,9},{2,10},{3,11},{4,12},{5,13},{6,14},{7,15},{8,16},{9,17... | collective-permute-start | bytes 786440 | tf_op jit(solution)/shard_map/ppermute | solution.py:34
  72.5 1.6 %collective-permute-start.17 = (bf16[128,1024]{1,0:T(8,128)(2,1)}, bf16[128,1024]{1,0:T(8,128)(2,1)S(1)}, u32[]{:S(2)}, u32[]{:S(2)}) collective-permute-start(bf16[128,1024]{1,0:T(8,128)(2,1)} %get-tuple-element.33.refs_0_), channel_id=1, source_target_pairs={{0,16},{1,17},{2,18},{3,19},{4,20},{5,21},{6,22},{7,23},{8,24},{9,... | collective-permute-start | bytes 786440 | tf_op jit(solution)/shard_map/ppermute | solution.py:34
  75.6 2.5 %terms.1 = (bf16[128,1024]{1,0:T(8,128)(2,1)}, bf16[128,1024]{1,0:T(8,128)(2,1)}, bf16[128,1024]{1,0:T(8,128)(2,1)}, bf16[128,1024]{1,0:T(8,128)(2,1)}) custom-call(s32[4]{0:T(128)} %pad_add_fusion.refs_0_.place, bf16[128,512]{1,0:T(8,128)(2,1)} %get-tuple-element.38.keep, bf16[128,512]{1,0:T(8,128)(2,1)} %copy-done.36, ...), custom_call_target="tpu_custom_call" | custom-call | flops 268435456 | bytes 1048576 | tf_op jit(solution)/shard_map/terms/pallas_call | solution.py:210
  79.1 1.9 %collective-permute-done.18.refs_3_ = bf16[128,1024]{1,0:T(8,128)(2,1)S(1)} collective-permute-done((bf16[128,1024]{1,0:T(8,128)(2,1)}, bf16[128,1024]{1,0:T(8,128)(2,1)S(1)}, u32[]{:S(2)}, u32[]{:S(2)}) %collective-permute-start.18) | collective-permute-done | bytes 262176 | tf_op jit(solution)/shard_map/ppermute | solution.py:34
  81.6 10.1 %collective-permute-done.17.refs_2_ = bf16[128,1024]{1,0:T(8,128)(2,1)S(1)} collective-permute-done((bf16[128,1024]{1,0:T(8,128)(2,1)}, bf16[128,1024]{1,0:T(8,128)(2,1)S(1)}, u32[]{:S(2)}, u32[]{:S(2)}) %collective-permute-start.17) | collective-permute-done | bytes 262176 | tf_op jit(solution)/shard_map/ppermute | solution.py:34
  93.6 2.2 %split.1 = (bf16[128,256]{1,0:T(8,128)(2,1)}, bf16[128,256]{1,0:T(8,128)(2,1)}, bf16[128,256]{1,0:T(8,128)(2,1)}, bf16[128,256]{1,0:T(8,128)(2,1)}) custom-call(s32[4]{0:T(128)} %pad_add_fusion.refs_0_.place, bf16[128,1024]{1,0:T(8,128)(2,1)} %get-tuple-element.41.refs_0_, bf16[128,1024]{1,0:T(8,128)(2,1)} %copy-done.14, bf16[128,1024]{1,0:T(8,128)(2,1)} %copy-done.15, ...), custom_call_target="tpu_custom_call" | custom-call | tf_op jit(solution)/shard_map/split/pallas_call | solution.py:240
  95.7 5.5 %collective-permute-start.31 = (bf16[128,256]{1,0:T(8,128)(2,1)}, bf16[128,256]{1,0:T(8,128)(2,1)S(1)}, u32[]{:S(2)}, u32[]{:S(2)}) collective-permute-start(bf16[128,256]{1,0:T(8,128)(2,1)} %get-tuple-element.46), channel_id=1, source_target_pairs={{0,8},{1,9},{2,10},{3,11},{4,12},{5,13},{6,14},{7,15},{8,16},{9,17... | collective-permute-start | bytes 196616 | tf_op jit(solution)/shard_map/ppermute | solution.py:34
  101.3 1.7 %collective-permute-start.32 = (bf16[128,256]{1,0:T(8,128)(2,1)}, bf16[128,256]{1,0:T(8,128)(2,1)S(1)}, u32[]{:S(2)}, u32[]{:S(2)}) collective-permute-start(bf16[128,256]{1,0:T(8,128)(2,1)} %get-tuple-element.47), channel_id=1, source_target_pairs={{0,16},{1,17},{2,18},{3,19},{4,20},{5,21},{6,22},{7,23},{8,24},{9,... | collective-permute-start | bytes 196616 | tf_op jit(solution)/shard_map/ppermute | solution.py:34
  104.5 4.8 %spread_backward.1 = (bf16[128,1024]{1,0:T(8,128)(2,1)}, bf16[128,1024]{1,0:T(8,128)(2,1)}, bf16[128,1024]{1,0:T(8,128)(2,1)}, bf16[128,1024]{1,0:T(8,128)(2,1)}) custom-call(bf16[512,1024]{1,0:T(8,128)(2,1)} %get-tuple-element.32.matrix, bf16[128,1024]{1,0:T(8,128)(2,1)} %get-tuple-element.33.refs_0_, bf16[128,1024]{1,0:T(8,128)(2,1)} %copy-done.30, ...), custom_call_target="tpu_custom_call" | custom-call | flops 1073741824 | bytes 4194304 | tf_op jit(solution)/shard_map/spread_backward/pallas_call | solution.py:108
  111.1 2.0 %collective-permute-start.36 = (bf16[128,256]{1,0:T(8,128)(2,1)S(1)}, bf16[128,256]{1,0:T(8,128)(2,1)S(1)}, u32[]{:S(2)}, u32[]{:S(2)}) collective-permute-start(bf16[128,256]{1,0:T(8,128)(2,1)S(1)} %multiply_convert_fusion), channel_id=1, source_target_pairs={{0,24},{1,25},{2,26},{3,27},{4,28},{5,29},{6,30},{7,31},{8,0},{9,1... | collective-permute-start | bytes 196616 | tf_op jit(solution)/shard_map/ppermute | solution.py:34
  115.5 4.8 %collective-permute-done.35 = bf16[128,256]{1,0:T(8,128)(2,1)S(1)} collective-permute-done((bf16[128,256]{1,0:T(8,128)(2,1)S(1)}, bf16[128,256]{1,0:T(8,128)(2,1)S(1)}, u32[]{:S(2)}, u32[]{:S(2)}) %collective-permute-start.35) | collective-permute-done | bytes 65568 | tf_op jit(solution)/shard_map/ppermute | solution.py:34
  120.3 1.4 collective-permute-start.39
  125.2 5.3 %collective-permute-done.39.refs_3_ = bf16[4,128,256]{2,1,0:T(8,128)(2,1)S(1)} collective-permute-done((bf16[4,128,256]{2,1,0:T(8,128)(2,1)S(1)}, bf16[4,128,256]{2,1,0:T(8,128)(2,1)S(1)}, u32[]{:S(2)}, u32[]{:S(2)}) %collective-permute-start.39) | collective-permute-done | bytes 262176 | tf_op jit(solution)/shard_map/ppermute | solution.py:34
  130.5 5.5 %collective-permute-done.38.refs_2_ = bf16[4,128,256]{2,1,0:T(8,128)(2,1)S(1)} collective-permute-done((bf16[4,128,256]{2,1,0:T(8,128)(2,1)S(1)}, bf16[4,128,256]{2,1,0:T(8,128)(2,1)S(1)}, u32[]{:S(2)}, u32[]{:S(2)}) %collective-permute-start.38) | collective-permute-done | bytes 262176 | tf_op jit(solution)/shard_map/ppermute | solution.py:34
  136.6 3.1 %collective-permute-done.25 = bf16[128,1024]{1,0:T(8,128)(2,1)S(1)} collective-permute-done((bf16[128,1024]{1,0:T(8,128)(2,1)}, bf16[128,1024]{1,0:T(8,128)(2,1)S(1)}, u32[]{:S(2)}, u32[]{:S(2)}) %collective-permute-start.25) | collective-permute-done | bytes 262176 | tf_op jit(solution)/shard_map/ppermute | solution.py:34
  139.7 1.8 %add_convert_fusion = bf16[128,1024]{1,0:T(8,128)(2,1)} fusion(bf16[128,1024]{1,0:T(8,128)(2,1)S(1)} %collective-permute-done.25, bf16[128,1024]{1,0:T(8,128)(2,1)S(1)} %collective-permute-done.24, bf16[128,1024]{1,0:T(8,128)(2,1)S(1)} %collective-permute-done.23, bf16[128,1024]{1,0:T(8,128)(2,1)} %get-tuple-element.34), kind=kLoop, calls=%fused_computation | loop fusion | flops 1048576 | bytes 1310720 | tf_op jit(solution)/shard_map/convert_element_type | solution.py:320
  143.1 3.8 %join.1 = f32[1024,1024]{1,0:T(8,128)} custom-call(s32[4]{0:T(128)} %pad_add_fusion.refs_0_.place, bf16[4,128,256]{2,1,0:T(8,128)(2,1)} %copy-done, bf16[4,128,256]{2,1,0:T(8,128)(2,1)} %copy-done.3, bf16[4,128,256]{2,1,0:T(8,128)(2,1)} %copy-done.2, bf16[4,128,256]{2,1,0:T(8,128)(2,1)} %copy-done.1, bf16[4,128,256]{2,1,0:T(8,128)(2,1)} %copy-done.4, ...), custom_call_target="tpu_custom_call" | custom-call | tf_op jit(solution)/shard_map/join/pallas_call | solution.py:271
  (142 shorter events, 21.9 us)
Async XLA Ops:
  5.2 9.3 %collective-permute-start.3 = (bf16[8,128,128]{2,1,0:T(8,128)(2,1)}, bf16[8,128,128]{2,1,0:T(8,128)(2,1)S(1)}, u32[]{:S(2)}, u32[]{:S(2)}) collective-permute-start(bf16[8,128,128]{2,1,0:T(8,128)(2,1)} %bitcast.14), channel_id=1, source_target_pairs={{0,4},{1,5},{2,6},{3,7},{4,0},{5,1},{6,2},{7,3},{8,12},{9,13},{10,... | collective-permute-start | bytes 786440 | tf_op jit(solution)/shard_map/ppermute | solution.py:34
  5.5 14.7 %collective-permute-start.9 = (bf16[128,1024]{1,0:T(8,128)(2,1)}, bf16[128,1024]{1,0:T(8,128)(2,1)S(1)}, u32[]{:S(2)}, u32[]{:S(2)}) collective-permute-start(bf16[128,1024]{1,0:T(8,128)(2,1)} %refs_0_.1), channel_id=1, source_target_pairs={{0,4},{1,5},{2,6},{3,7},{4,0},{5,1},{6,2},{7,3},{8,12},{9,13},{10,... | collective-permute-start | bytes 786440 | tf_op jit(solution)/shard_map/ppermute | solution.py:34
  7.3 12.9 %collective-permute-start.7 = (bf16[128,1024]{1,0:T(8,128)(2,1)}, bf16[128,1024]{1,0:T(8,128)(2,1)S(1)}, u32[]{:S(2)}, u32[]{:S(2)}) collective-permute-start(bf16[128,1024]{1,0:T(8,128)(2,1)} %refs_0_.1), channel_id=1, source_target_pairs={{0,2},{1,3},{2,0},{3,1},{4,6},{5,7},{6,4},{7,5},{8,10},{9,11},{10,... | collective-permute-start | bytes 786440 | tf_op jit(solution)/shard_map/ppermute | solution.py:34
  8.9 17.3 %collective-permute-start.11 = (bf16[128,1024]{1,0:T(8,128)(2,1)}, bf16[128,1024]{1,0:T(8,128)(2,1)S(1)}, u32[]{:S(2)}, u32[]{:S(2)}) collective-permute-start(bf16[128,1024]{1,0:T(8,128)(2,1)} %refs_0_.1), channel_id=1, source_target_pairs={{0,6},{1,7},{2,4},{3,5},{4,2},{5,3},{6,0},{7,1},{8,14},{9,15},{10,... | collective-permute-start | bytes 786440 | tf_op jit(solution)/shard_map/ppermute | solution.py:34
  10.7 21.0 %collective-permute-start.6 = (bf16[128,1024]{1,0:T(8,128)(2,1)}, bf16[128,1024]{1,0:T(8,128)(2,1)S(1)}, u32[]{:S(2)}, u32[]{:S(2)}) collective-permute-start(bf16[128,1024]{1,0:T(8,128)(2,1)} %refs_0_.1), channel_id=1, source_target_pairs={{0,1},{1,0},{2,3},{3,2},{4,5},{5,4},{6,7},{7,6},{8,9},{9,8},{10,11... | collective-permute-start | bytes 786440 | tf_op jit(solution)/shard_map/ppermute | solution.py:34
  14.6 12.3 %collective-permute-start.5 = (bf16[8,128,128]{2,1,0:T(8,128)(2,1)S(1)}, bf16[8,128,128]{2,1,0:T(8,128)(2,1)S(1)}, u32[]{:S(2)}, u32[]{:S(2)}) collective-permute-start(bf16[8,128,128]{2,1,0:T(8,128)(2,1)S(1)} %collective-permute-done.3.refs_6_), channel_id=1, source_target_pairs={{0,1},{1,0},{2,3},{3,2},{4,5},{5,4},{6,7},{7,6},{8,9},{9,8},{10,11... | collective-permute-start | bytes 786440 | tf_op jit(solution)/shard_map/ppermute | solution.py:34
  20.2 11.6 %collective-permute-start.10 = (bf16[128,1024]{1,0:T(8,128)(2,1)S(1)}, bf16[128,1024]{1,0:T(8,128)(2,1)S(1)}, u32[]{:S(2)}, u32[]{:S(2)}) collective-permute-start(bf16[128,1024]{1,0:T(8,128)(2,1)S(1)} %collective-permute-done.9.refs_4_), channel_id=1, source_target_pairs={{0,1},{1,0},{2,3},{3,2},{4,5},{5,4},{6,7},{7,6},{8,9},{9,8},{10,11... | collective-permute-start | bytes 786440 | tf_op jit(solution)/shard_map/ppermute | solution.py:34
  20.2 11.6 %collective-permute-start.8 = (bf16[128,1024]{1,0:T(8,128)(2,1)S(1)}, bf16[128,1024]{1,0:T(8,128)(2,1)S(1)}, u32[]{:S(2)}, u32[]{:S(2)}) collective-permute-start(bf16[128,1024]{1,0:T(8,128)(2,1)S(1)} %collective-permute-done.7.refs_2_), channel_id=1, source_target_pairs={{0,1},{1,0},{2,3},{3,2},{4,5},{5,4},{6,7},{7,6},{8,9},{9,8},{10,11... | collective-permute-start | bytes 786440 | tf_op jit(solution)/shard_map/ppermute | solution.py:34
  37.5 11.3 %collective-permute-start.13 = (bf16[128,1024]{1,0:T(8,128)(2,1)}, bf16[128,1024]{1,0:T(8,128)(2,1)S(1)}, u32[]{:S(2)}, u32[]{:S(2)}) collective-permute-start(bf16[128,1024]{1,0:T(8,128)(2,1)} %get-tuple-element.28), channel_id=1, source_target_pairs={{0,8},{1,9},{2,10},{3,11},{4,12},{5,13},{6,14},{7,15},{8,16},{9,17... | collective-permute-start | bytes 786440 | tf_op jit(solution)/shard_map/ppermute | solution.py:34
  39.3 20.4 %collective-permute-start.14 = (bf16[128,1024]{1,0:T(8,128)(2,1)}, bf16[128,1024]{1,0:T(8,128)(2,1)S(1)}, u32[]{:S(2)}, u32[]{:S(2)}) collective-permute-start(bf16[128,1024]{1,0:T(8,128)(2,1)} %get-tuple-element.29), channel_id=1, source_target_pairs={{0,16},{1,17},{2,18},{3,19},{4,20},{5,21},{6,22},{7,23},{8,24},{9,... | collective-permute-start | bytes 786440 | tf_op jit(solution)/shard_map/ppermute | solution.py:34
  41.2 18.5 %collective-permute-start.15 = (bf16[128,1024]{1,0:T(8,128)(2,1)}, bf16[128,1024]{1,0:T(8,128)(2,1)S(1)}, u32[]{:S(2)}, u32[]{:S(2)}) collective-permute-start(bf16[128,1024]{1,0:T(8,128)(2,1)} %get-tuple-element.30), channel_id=1, source_target_pairs={{0,24},{1,25},{2,26},{3,27},{4,28},{5,29},{6,30},{7,31},{8,0},{9,1... | collective-permute-start | bytes 786440 | tf_op jit(solution)/shard_map/ppermute | solution.py:34
  65.9 9.0 %collective-permute-start.27 = (bf16[128,1024]{1,0:T(8,128)(2,1)}, bf16[128,1024]{1,0:T(8,128)(2,1)S(1)}, u32[]{:S(2)}, u32[]{:S(2)}) collective-permute-start(bf16[128,1024]{1,0:T(8,128)(2,1)} %get-tuple-element.40.grad), channel_id=1, source_target_pairs={{0,1},{1,0},{2,3},{3,2},{4,5},{5,4},{6,7},{7,6},{8,9},{9,8},{10,11... | collective-permute-start | bytes 786440 | tf_op jit(solution)/shard_map/ppermute | solution.py:34
  66.5 14.5 %collective-permute-start.18 = (bf16[128,1024]{1,0:T(8,128)(2,1)}, bf16[128,1024]{1,0:T(8,128)(2,1)S(1)}, u32[]{:S(2)}, u32[]{:S(2)}) collective-permute-start(bf16[128,1024]{1,0:T(8,128)(2,1)} %get-tuple-element.33.refs_0_), channel_id=1, source_target_pairs={{0,8},{1,9},{2,10},{3,11},{4,12},{5,13},{6,14},{7,15},{8,16},{9,17... | collective-permute-start | bytes 786440 | tf_op jit(solution)/shard_map/ppermute | solution.py:34
  72.5 19.2 %collective-permute-start.17 = (bf16[128,1024]{1,0:T(8,128)(2,1)}, bf16[128,1024]{1,0:T(8,128)(2,1)S(1)}, u32[]{:S(2)}, u32[]{:S(2)}) collective-permute-start(bf16[128,1024]{1,0:T(8,128)(2,1)} %get-tuple-element.33.refs_0_), channel_id=1, source_target_pairs={{0,16},{1,17},{2,18},{3,19},{4,20},{5,21},{6,22},{7,23},{8,24},{9,... | collective-permute-start | bytes 786440 | tf_op jit(solution)/shard_map/ppermute | solution.py:34
  74.1 17.6 %collective-permute-start.16 = (bf16[128,1024]{1,0:T(8,128)(2,1)}, bf16[128,1024]{1,0:T(8,128)(2,1)S(1)}, u32[]{:S(2)}, u32[]{:S(2)}) collective-permute-start(bf16[128,1024]{1,0:T(8,128)(2,1)} %get-tuple-element.33.refs_0_), channel_id=1, source_target_pairs={{0,24},{1,25},{2,26},{3,27},{4,28},{5,29},{6,30},{7,31},{8,0},{9,1... | collective-permute-start | bytes 786440 | tf_op jit(solution)/shard_map/ppermute | solution.py:34
  78.1 14.1 %collective-permute-start.28 = (bf16[128,1024]{1,0:T(8,128)(2,1)}, bf16[128,1024]{1,0:T(8,128)(2,1)S(1)}, u32[]{:S(2)}, u32[]{:S(2)}) collective-permute-start(bf16[128,1024]{1,0:T(8,128)(2,1)} %get-tuple-element.42), channel_id=1, source_target_pairs={{0,2},{1,3},{2,0},{3,1},{4,6},{5,7},{6,4},{7,5},{8,10},{9,11},{10,... | collective-permute-start | bytes 786440 | tf_op jit(solution)/shard_map/ppermute | solution.py:34
  78.8 13.5 %collective-permute-start.29 = (bf16[128,1024]{1,0:T(8,128)(2,1)}, bf16[128,1024]{1,0:T(8,128)(2,1)S(1)}, u32[]{:S(2)}, u32[]{:S(2)}) collective-permute-start(bf16[128,1024]{1,0:T(8,128)(2,1)} %get-tuple-element.43), channel_id=1, source_target_pairs={{0,4},{1,5},{2,6},{3,7},{4,0},{5,1},{6,2},{7,3},{8,12},{9,13},{10,... | collective-permute-start | bytes 786440 | tf_op jit(solution)/shard_map/ppermute | solution.py:34
  81.0 11.9 %collective-permute-start.30 = (bf16[128,1024]{1,0:T(8,128)(2,1)}, bf16[128,1024]{1,0:T(8,128)(2,1)S(1)}, u32[]{:S(2)}, u32[]{:S(2)}) collective-permute-start(bf16[128,1024]{1,0:T(8,128)(2,1)} %get-tuple-element.44), channel_id=1, source_target_pairs={{0,6},{1,7},{2,4},{3,5},{4,2},{5,3},{6,0},{7,1},{8,14},{9,15},{10,... | collective-permute-start | bytes 786440 | tf_op jit(solution)/shard_map/ppermute | solution.py:34
  91.7 9.6 %collective-permute-start.19 = (bf16[128,1024]{1,0:T(8,128)(2,1)}, bf16[128,1024]{1,0:T(8,128)(2,1)S(1)}, u32[]{:S(2)}, u32[]{:S(2)}) collective-permute-start(bf16[128,1024]{1,0:T(8,128)(2,1)} %get-tuple-element.33.refs_0_), channel_id=1, source_target_pairs={{0,1},{1,0},{2,3},{3,2},{4,5},{5,4},{6,7},{7,6},{8,9},{9,8},{10,11... | collective-permute-start | bytes 786440 | tf_op jit(solution)/shard_map/ppermute | solution.py:34
  91.7 11.3 %collective-permute-start.22 = (bf16[128,1024]{1,0:T(8,128)(2,1)S(1)}, bf16[128,1024]{1,0:T(8,128)(2,1)S(1)}, u32[]{:S(2)}, u32[]{:S(2)}) collective-permute-start(bf16[128,1024]{1,0:T(8,128)(2,1)S(1)} %collective-permute-done.18.refs_3_), channel_id=1, source_target_pairs={{0,1},{1,0},{2,3},{3,2},{4,5},{5,4},{6,7},{7,6},{8,9},{9,8},{10,11... | collective-permute-start | bytes 786440 | tf_op jit(solution)/shard_map/ppermute | solution.py:34
  92.2 11.5 %collective-permute-start.21 = (bf16[128,1024]{1,0:T(8,128)(2,1)S(1)}, bf16[128,1024]{1,0:T(8,128)(2,1)S(1)}, u32[]{:S(2)}, u32[]{:S(2)}) collective-permute-start(bf16[128,1024]{1,0:T(8,128)(2,1)S(1)} %collective-permute-done.17.refs_2_), channel_id=1, source_target_pairs={{0,1},{1,0},{2,3},{3,2},{4,5},{5,4},{6,7},{7,6},{8,9},{9,8},{10,11... | collective-permute-start | bytes 786440 | tf_op jit(solution)/shard_map/ppermute | solution.py:34
  92.3 11.4 %collective-permute-start.20 = (bf16[128,1024]{1,0:T(8,128)(2,1)S(1)}, bf16[128,1024]{1,0:T(8,128)(2,1)S(1)}, u32[]{:S(2)}, u32[]{:S(2)}) collective-permute-start(bf16[128,1024]{1,0:T(8,128)(2,1)S(1)} %collective-permute-done.16.refs_1_), channel_id=1, source_target_pairs={{0,1},{1,0},{2,3},{3,2},{4,5},{5,4},{6,7},{7,6},{8,9},{9,8},{10,11... | collective-permute-start | bytes 786440 | tf_op jit(solution)/shard_map/ppermute | solution.py:34
  95.7 14.5 %collective-permute-start.31 = (bf16[128,256]{1,0:T(8,128)(2,1)}, bf16[128,256]{1,0:T(8,128)(2,1)S(1)}, u32[]{:S(2)}, u32[]{:S(2)}) collective-permute-start(bf16[128,256]{1,0:T(8,128)(2,1)} %get-tuple-element.46), channel_id=1, source_target_pairs={{0,8},{1,9},{2,10},{3,11},{4,12},{5,13},{6,14},{7,15},{8,16},{9,17... | collective-permute-start | bytes 196616 | tf_op jit(solution)/shard_map/ppermute | solution.py:34
  101.3 9.0 %collective-permute-start.32 = (bf16[128,256]{1,0:T(8,128)(2,1)}, bf16[128,256]{1,0:T(8,128)(2,1)S(1)}, u32[]{:S(2)}, u32[]{:S(2)}) collective-permute-start(bf16[128,256]{1,0:T(8,128)(2,1)} %get-tuple-element.47), channel_id=1, source_target_pairs={{0,16},{1,17},{2,18},{3,19},{4,20},{5,21},{6,22},{7,23},{8,24},{9,... | collective-permute-start | bytes 196616 | tf_op jit(solution)/shard_map/ppermute | solution.py:34
  109.4 14.5 %collective-permute-start.23 = (bf16[128,1024]{1,0:T(8,128)(2,1)}, bf16[128,1024]{1,0:T(8,128)(2,1)S(1)}, u32[]{:S(2)}, u32[]{:S(2)}) collective-permute-start(bf16[128,1024]{1,0:T(8,128)(2,1)} %get-tuple-element.35), channel_id=1, source_target_pairs={{0,2},{1,3},{2,0},{3,1},{4,6},{5,7},{6,4},{7,5},{8,10},{9,11},{10,... | collective-permute-start | bytes 786440 | tf_op jit(solution)/shard_map/ppermute | solution.py:34
  113.9 11.4 %collective-permute-start.24 = (bf16[128,1024]{1,0:T(8,128)(2,1)}, bf16[128,1024]{1,0:T(8,128)(2,1)S(1)}, u32[]{:S(2)}, u32[]{:S(2)}) collective-permute-start(bf16[128,1024]{1,0:T(8,128)(2,1)} %get-tuple-element.36), channel_id=1, source_target_pairs={{0,4},{1,5},{2,6},{3,7},{4,0},{5,1},{6,2},{7,3},{8,12},{9,13},{10,... | collective-permute-start | bytes 786440 | tf_op jit(solution)/shard_map/ppermute | solution.py:34
  120.3 10.3 %collective-permute-start.39 = (bf16[4,128,256]{2,1,0:T(8,128)(2,1)S(1)}, bf16[4,128,256]{2,1,0:T(8,128)(2,1)S(1)}, u32[]{:S(2)}, u32[]{:S(2)}) collective-permute-start(bf16[4,128,256]{2,1,0:T(8,128)(2,1)S(1)} %pad_maximum_fusion.refs_0_), channel_id=1, source_target_pairs={{0,6},{1,7},{2,4},{3,5},{4,2},{5,3},{6,0},{7,1},{8,14},{9,15},{10,... | collective-permute-start | bytes 786440 | tf_op jit(solution)/shard_map/ppermute | solution.py:34
  121.7 14.3 %collective-permute-start.38 = (bf16[4,128,256]{2,1,0:T(8,128)(2,1)S(1)}, bf16[4,128,256]{2,1,0:T(8,128)(2,1)S(1)}, u32[]{:S(2)}, u32[]{:S(2)}) collective-permute-start(bf16[4,128,256]{2,1,0:T(8,128)(2,1)S(1)} %pad_maximum_fusion.refs_0_), channel_id=1, source_target_pairs={{0,4},{1,5},{2,6},{3,7},{4,0},{5,1},{6,2},{7,3},{8,12},{9,13},{10,... | collective-permute-start | bytes 786440 | tf_op jit(solution)/shard_map/ppermute | solution.py:34
  123.2 12.9 %collective-permute-start.37 = (bf16[4,128,256]{2,1,0:T(8,128)(2,1)S(1)}, bf16[4,128,256]{2,1,0:T(8,128)(2,1)S(1)}, u32[]{:S(2)}, u32[]{:S(2)}) collective-permute-start(bf16[4,128,256]{2,1,0:T(8,128)(2,1)S(1)} %pad_maximum_fusion.refs_0_), channel_id=1, source_target_pairs={{0,2},{1,3},{2,0},{3,1},{4,6},{5,7},{6,4},{7,5},{8,10},{9,11},{10,... | collective-permute-start | bytes 786440 | tf_op jit(solution)/shard_map/ppermute | solution.py:34
  123.8 15.8 %collective-permute-start.25 = (bf16[128,1024]{1,0:T(8,128)(2,1)}, bf16[128,1024]{1,0:T(8,128)(2,1)S(1)}, u32[]{:S(2)}, u32[]{:S(2)}) collective-permute-start(bf16[128,1024]{1,0:T(8,128)(2,1)} %get-tuple-element.37), channel_id=1, source_target_pairs={{0,6},{1,7},{2,4},{3,5},{4,2},{5,3},{6,0},{7,1},{8,14},{9,15},{10,... | collective-permute-start | bytes 786440 | tf_op jit(solution)/shard_map/ppermute | solution.py:34
  125.2 16.3 %collective-permute-start.40 = (bf16[4,128,256]{2,1,0:T(8,128)(2,1)S(1)}, bf16[4,128,256]{2,1,0:T(8,128)(2,1)S(1)}, u32[]{:S(2)}, u32[]{:S(2)}) collective-permute-start(bf16[4,128,256]{2,1,0:T(8,128)(2,1)S(1)} %pad_maximum_fusion.refs_0_), channel_id=1, source_target_pairs={{0,1},{1,0},{2,3},{3,2},{4,5},{5,4},{6,7},{7,6},{8,9},{9,8},{10,11... | collective-permute-start | bytes 786440 | tf_op jit(solution)/shard_map/ppermute | solution.py:34
  130.5 11.0 %collective-permute-start.43 = (bf16[4,128,256]{2,1,0:T(8,128)(2,1)S(1)}, bf16[4,128,256]{2,1,0:T(8,128)(2,1)S(1)}, u32[]{:S(2)}, u32[]{:S(2)}) collective-permute-start(bf16[4,128,256]{2,1,0:T(8,128)(2,1)S(1)} %collective-permute-done.39.refs_3_), channel_id=1, source_target_pairs={{0,1},{1,0},{2,3},{3,2},{4,5},{5,4},{6,7},{7,6},{8,9},{9,8},{10,11... | collective-permute-start | bytes 786440 | tf_op jit(solution)/shard_map/ppermute | solution.py:34
  (49 other events, 325.2 us)

commit v2 on v0

v2 whole, which is shorter than its diff:
```python
import functools

import jax
import jax.numpy as jnp
from jax import lax
from jax.experimental import pallas as pl
from jax.experimental.pallas import tpu as pltpu
from jax.sharding import PartitionSpec as P

BF16 = jnp.bfloat16
F32 = jnp.float32
VMEM_LIMIT = 56 * 2**20
SMEM_SPEC = pl.BlockSpec(memory_space=pltpu.SMEM)
VMEM_SPEC = pl.BlockSpec(memory_space=pltpu.VMEM)


COST = {}


def cost(name):
    return pl.CostEstimate(flops=0, bytes_accessed=COST.get(name, 0), transcendentals=0)


class Grid:
    def __init__(self, rows, cols):
        if rows & (rows - 1) or cols & (cols - 1) or min(rows, cols) < 2:
            raise ValueError("mesh axes")
        self.R, self.C = rows, cols
        self.X, self.K = 2, 2
        self.Z, self.Y = rows // 2, cols // 2

    def devices(self):
        for z in range(self.Z):
            for x in range(self.X):
                for y in range(self.Y):
                    for k in range(self.K):
                        yield z, x, y, k

    def index(self, z, x, y, k):
        return (z * self.X + x) * self.C + y * self.K + k

    def move(self, value, dz=0, dx=0, dy=0, dk=0):
        pairs = [
            (self.index(z, x, y, k), self.index(z ^ dz, x ^ dx, y ^ dy, k ^ dk))
            for z, x, y, k in self.devices()
        ]
        return lax.ppermute(value, ("row", "col"), pairs)

    def along(self, value, hops):
        pairs = [
            (self.index(z, x, y, k), self.index(hops[z], x, y, k))
            for z, x, y, k in self.devices()
            if z in hops
        ]
        return lax.ppermute(value, ("row", "col"), pairs)

    def here(self):
        r, c = lax.axis_index("row"), lax.axis_index("col")
        return r // 2, r % 2, c // 2, c % 2


def params(**more):
    return pltpu.CompilerParams(vmem_limit_bytes=VMEM_LIMIT, **more)


def add_tiles(g, out, held, listed, slots, block, place):
    block_rows, block_cols, count = listed

    def one(s):
        wanted, row, col, turned = place(block_rows(s), block_cols(s))

        @pl.when(jnp.logical_and(s < count(), wanted))
        def _():
            tile = held[s]
            if turned:
                tile = tile.astype(F32).T.astype(BF16)
            out[
                pl.ds(pl.multiple_of(row * block, block), block),
                pl.ds(pl.multiple_of(col * block, block), block),
            ] = tile

    if slots <= 16:
        for s in range(slots):
            one(s)
    else:
        pl.loop(0, slots)(one)


def reader(listed, slots):
    return (lambda s: listed[s]), (lambda s: listed[slots + s]), (lambda: listed[2 * slots])


def multiply(matrix, stacked, outs, block):
    width = stacked.shape[1]
    tile = 256 if width % 256 == 0 else width

    def one(j):
        cols = pl.ds(j * tile if isinstance(j, int) else pl.multiple_of(j * tile, tile), tile)
        total = jnp.dot(matrix[...], stacked[:, cols], preferred_element_type=F32)
        for i, out in enumerate(outs):
            out[:, cols] = total[i * block : (i + 1) * block].astype(BF16)

    if matrix.shape[0] * matrix.shape[1] <= 2**20:
        for j in range(width // tile):
            one(j)
    else:
        pl.loop(0, width // tile)(one)


def forward_kernel(g, slots, block, n_in, *refs):
    lists, tiles = refs[:2], refs[2:4]
    blocks, outs = refs[4 : 4 + n_in], refs[4 + n_in : 4 + n_in + g.Z]
    matrix, stacked = refs[4 + n_in + g.Z :]
    z, x, y, k = g.here()
    matrix[...] = jnp.zeros_like(matrix)
    for dx in range(g.X):

        def place(row, col, dx=dx):
            at_z, at_x = row // g.X, row % g.X
            at_y, at_k = col // g.K, col % g.K
            at = dx * g.C + (at_y ^ y) * g.K + (at_k ^ k)
            return at_x == x, at_z ^ z, at, False

        add_tiles(g, matrix, tiles[dx], reader(lists[dx], slots), slots, block, place)
    for i, held in enumerate(blocks):
        stacked[pl.ds(i * block, block), :] = held[...]
    multiply(matrix, stacked, outs, block)


def forward(g, lists, tiles, blocks):
    slots = tiles[0].shape[0]
    block, width = blocks[0].shape
    n = len(blocks)
    return pl.pallas_call(
        functools.partial(forward_kernel, g, slots, block, n),
        out_shape=[jax.ShapeDtypeStruct((block, width), BF16)] * g.Z,
        in_specs=[SMEM_SPEC] * 2 + [VMEM_SPEC] * (2 + n),
        out_specs=[VMEM_SPEC] * g.Z,
        scratch_shapes=[
            pltpu.VMEM((g.Z * block, n * block), BF16),
            pltpu.VMEM((n * block, width), BF16),
        ],
        compiler_params=params(),
        cost_estimate=cost("forward"),
        name="forward",
    )(*lists, *tiles, *blocks)


def build_kernel(g, slots, block, *refs):
    lists, tiles, bundle, matrix = refs[:4], refs[4:6], refs[6], refs[7]
    z, x, y, k = g.here()
    matrix[...] = jnp.zeros_like(matrix)
    for dk in range(g.K):
        for dx in range(g.X):

            def place(row, col, dk=dk, dx=dx):
                at_z, at_x = row // g.X, row % g.X
                at_y, at_k = col // g.K, col % g.K
                wanted = jnp.logical_and(at_x == x, at_k == k)
                return wanted, dx * g.Y + (at_y ^ y), dk * g.Z + (at_z ^ z), True

            held = tiles[dx] if dk == 0 else bundle.at[pl.ds(dx * slots, slots)]
            listed = reader(lists[dk * g.X + dx], slots)
            add_tiles(g, matrix, held, listed, slots, block, place)


def build(g, lists, tiles, bundle):
    slots, block = tiles[0].shape[0], tiles[0].shape[1]
    return pl.pallas_call(
        functools.partial(build_kernel, g, slots, block),
        out_shape=jax.ShapeDtypeStruct((g.X * g.Y * block, g.K * g.Z * block), BF16),
        in_specs=[SMEM_SPEC] * 4 + [VMEM_SPEC] * 3,
        out_specs=VMEM_SPEC,
        compiler_params=params(),
        cost_estimate=cost("build"),
        name="build",
    )(*lists, *tiles, bundle)


def backward_kernel(g, block, groups, matrix, *refs):
    n_in = sum(groups)
    outs, stacked = refs[n_in:-1], refs[-1]
    at = 0
    for i, n in enumerate(groups):
        held = refs[at][...]
        for more in refs[at + 1 : at + n]:
            held = held + more[...]
        stacked[pl.ds(i * block, block), :] = held
        at += n
    multiply(matrix, stacked, outs, block)


def backward(g, matrix, groups):
    block, width = groups[0][0].shape
    n_out = matrix.shape[0] // block
    flat = [v for group in groups for v in group]
    return pl.pallas_call(
        functools.partial(backward_kernel, g, block, [len(group) for group in groups]),
        out_shape=[jax.ShapeDtypeStruct((block, width), BF16)] * n_out,
        in_specs=[VMEM_SPEC] * (1 + len(flat)),
        out_specs=[VMEM_SPEC] * n_out,
        scratch_shapes=[pltpu.VMEM((len(groups) * block, width), BF16)],
        compiler_params=params(),
        cost_estimate=cost("backward"),
        name="backward",
    )(matrix, *flat)


def fold(g, split):
    total = split[0].astype(F32)
    for i in range(1, g.X * g.Y):
        total += g.move(split[i], dx=i // g.Y, dy=i % g.Y).astype(F32)
    return total


def layer_kernel(g, n_in, *refs):
    parts = refs[:n_in]
    weight, cotangent = refs[n_in : n_in + 2]
    activated, share, back, keep = refs[n_in + 2 : n_in + 6]
    agg, total = refs[n_in + 6 :]
    j, last = pl.program_id(0), pl.num_programs(0) - 1
    half = keep.shape[1]

    @pl.when(j == 0)
    def _():
        summed = parts[0][...].astype(F32)
        for part in parts[1:]:
            summed += part[...].astype(F32)
        agg[...] = summed.astype(BF16)
        total[...] = jnp.zeros_like(total)
        core = g.here()[3]
        keep[...] = agg[:, pl.ds(pl.multiple_of(core * half, half), half)]
        share[:, :half] = agg[:, pl.ds(pl.multiple_of((1 - core) * half, half), half)]

    hidden = jnp.dot(agg[...], weight[...], preferred_element_type=F32)
    sigmoid = jax.nn.sigmoid(hidden)
    activated[...] = (hidden * sigmoid).astype(BF16)
    slope = sigmoid * (1.0 + hidden * (1.0 - sigmoid))
    grad = (cotangent[...].astype(F32) * slope).astype(BF16)
    share[:, pl.ds(pl.multiple_of(half + j * grad.shape[1], grad.shape[1]), grad.shape[1])] = grad
    total[...] += lax.dot_general(
        grad, weight[...], (((1,), (1,)), ((), ())), preferred_element_type=F32
    )

    @pl.when(j == last)
    def _():
        back[...] = total[...].astype(BF16)


def layer(g, parts, weight, cotangent):
    rows, depth = parts[0].shape
    width = weight.shape[1]
    tile = 256 if width % 256 == 0 else width
    whole = pl.BlockSpec((rows, depth), lambda j: (0, 0))
    half = pl.BlockSpec((rows, depth // 2), lambda j: (0, 0))
    shared = pl.BlockSpec((rows, depth // 2 + width), lambda j: (0, 0))
    cut = pl.BlockSpec((rows, tile), lambda j: (0, j))
    return pl.pallas_call(
        functools.partial(layer_kernel, g, len(parts)),
        grid=(width // tile,),
        out_shape=[
            jax.ShapeDtypeStruct((rows, width), BF16),
            jax.ShapeDtypeStruct((rows, depth // 2 + width), BF16),
            jax.ShapeDtypeStruct((rows, depth), BF16),
            jax.ShapeDtypeStruct((rows, depth // 2), BF16),
        ],
        in_specs=[whole] * len(parts)
        + [pl.BlockSpec((depth, tile), lambda j: (0, j)), cut],
        out_specs=[cut, shared, whole, half],
        scratch_shapes=[pltpu.VMEM((rows, depth), BF16), pltpu.VMEM((rows, depth), F32)],
        compiler_params=params(),
        cost_estimate=cost("layer"),
        name="layer",
    )(*parts, weight, cotangent)


def terms_kernel(g, keep, share, share_got, *refs):
    outs, turned, grads = refs[:-2], refs[-2], refs[-1]
    nodes, half = keep.shape
    both = jnp.concatenate([keep[...].astype(F32), share_got[:, :half].astype(F32)], axis=0)
    turned[...] = both.T.astype(BF16)
    z, x, y, _ = g.here()
    rows, width = outs[0].shape[1:]
    for dz in range(g.Z):
        cols = pl.ds(pl.multiple_of(half + (z ^ dz) * width, width), width)
        grads[0:nodes, dz * width : (dz + 1) * width] = share[:, cols]
        grads[nodes:, dz * width : (dz + 1) * width] = share_got[:, cols]
    for dx in range(g.X):
        for dy in range(g.Y):
            at = (x ^ dx) * g.Y + (y ^ dy)
            mine = turned[pl.ds(pl.multiple_of(at * rows, rows), rows), :]
            total = jnp.dot(mine, grads[...], preferred_element_type=F32).astype(BF16)
            for dz in range(g.Z):
                outs[dx * g.Y + dy][dz] = total[:, dz * width : (dz + 1) * width]


def terms(g, keep, share, share_got):
    nodes, half = keep.shape
    width = share.shape[1] - half
    n_out = g.X * g.Y
    shapes = [jax.ShapeDtypeStruct((g.Z, half // n_out, width // g.Z), BF16)] * n_out
    return pl.pallas_call(
        functools.partial(terms_kernel, g),
        out_shape=shapes,
        in_specs=[VMEM_SPEC] * 3,
        out_specs=[VMEM_SPEC] * len(shapes),
        scratch_shapes=[
            pltpu.VMEM((half, 2 * nodes), BF16),
            pltpu.VMEM((2 * nodes, width), BF16),
        ],
        compiler_params=params(),
        cost_estimate=cost("terms"),
        name="terms",
    )(keep, share, share_got)


def join_kernel(g, places, *refs):
    out = refs[-1]
    rows, width = refs[0].shape[1:]
    z, x, y, k = g.here()
    for (dk, dx, dy, first), held in zip(places, refs):
        at = ((k ^ dk) * g.X + (x ^ dx)) * g.Y + (y ^ dy)
        for i in range(held.shape[0]):
            col = z ^ (first + i)
            out[
                pl.ds(pl.multiple_of(at * rows, rows), rows),
                pl.ds(pl.multiple_of(col * width, width), width),
            ] = held[i].astype(F32)


def join(g, places, pieces, shape):
    return pl.pallas_call(
        functools.partial(join_kernel, g, places),
        out_shape=jax.ShapeDtypeStruct(shape, F32),
        in_specs=[VMEM_SPEC] * len(pieces),
        out_specs=VMEM_SPEC,
        compiler_params=params(),
        cost_estimate=cost("join"),
        name="join",
    )(*pieces)


def on_device(g, features, weight, cotangent, tile_values, block_row, block_column, tile_count):
    pin = lax.optimization_barrier

    def after(value, *others):
        return pin((value, others))[0]

    squares = [(dx, dy) for dx in range(g.X) for dy in range(g.Y)]

    listed = jnp.concatenate([block_row[0, 0], block_column[0, 0], tile_count[0]])
    lists = [listed, g.move(listed, dx=1)]
    tiles = [tile_values[0, 0], g.move(after(tile_values[0, 0], listed), dx=1)]
    near = {(0, 0): features}
    for dx, dy in squares[1:]:
        near[dx, dy] = g.move(after(features, listed), dx=dx, dy=dy)
    blocks = []
    for at in squares:
        value = near[at] if at != (0, 0) else after(features, near[1, 0])
        blocks += [near[at], g.move(value, dk=1)]
    sums = forward(g, lists, tiles, blocks)
    parts = [sums[0]] + [g.move(sums[dz], dz=dz) for dz in range(1, g.Z)]

    slots, block = tiles[0].shape[:2]
    rows = [jnp.broadcast_to(v, slots) for at in lists for v in (at[:slots], at[slots:-1], at[-1])]
    codes = jnp.pad(jnp.stack(rows).astype(BF16), ((0, block - len(rows)), (0, block - slots)))[None]
    bundle = g.move(jnp.concatenate(after(tiles, sums) + [codes], axis=0), dk=1)
    got = bundle[2 * slots, : len(rows), :slots].astype(jnp.int32)
    others = [jnp.concatenate([got[i], got[i + 1], got[i + 2, :1]]) for i in (0, 3)]
    matrix = build(g, lists + others, tiles, bundle)
    parts, matrix = pin((parts, matrix))
    activated, share, back, keep = layer(g, parts, weight, cotangent)

    shares = terms(g, keep, share, g.move(share, dk=1))

    if g.Z == 0:
        far = g.move(back, dz=2)
        far = after(far, shares)
        groups = [[back], [g.move(back, dz=1)], [far]]
        groups.append([g.along(back, {1: 2, 2: 1}), g.along(far, {1: 0, 2: 3})])
    else:
        groups = [[back]] + [[g.move(back, dz=dz)] for dz in range(1, g.Z)]
    arrived = groups[1:]
    groups += [[g.move(v, dk=1) for v in group] for group in groups]
    deltas = backward(g, matrix, groups)
    feat_grad = fold(g, deltas).astype(BF16)

    pieces = after(fold(g, shares).astype(BF16), arrived)
    total = pieces[0].astype(F32)
    for dz in range(1, g.Z):
        total += g.move(pieces[dz], dz=dz).astype(F32)
    factor = (features.shape[0] * g.R * g.C) ** (-0.5)
    own = (total * factor).astype(BF16)
    column = jnp.stack([own] + [g.move(own, dz=dz) for dz in range(1, g.Z)])
    column = after(column, deltas)
    held = [column if at == (0, 0) else g.move(column, dx=at[0], dy=at[1]) for at in squares]
    held += [g.move(v, dk=1) for v in held]
    places = [(dk, *at, 0) for dk in range(g.K) for at in squares]
    weight_grad = join(g, places, held, weight.shape)
    return (activated, feat_grad, weight_grad)


def solution(mesh):
    g = Grid(mesh.shape["row"], mesh.shape["col"])
    return jax.shard_map(
        functools.partial(on_device, g),
        mesh=mesh,
        in_specs=(
            P(("row", "col"), None),
            P(),
            P(("col", "row"), None),
            P("row", "col", None, None, None),
            P("row", "col", None),
            P("row", "col", None),
            P("row", "col"),
        ),
        out_specs=(P(("col", "row"), None), P(("row", "col"), None), P()),
        check_vma=False,
    )
```

time: 389 us -> 139 us (0.36)
  waiting for transfers between devices: 301 us -> 53.6 us
  starting transfers between devices: 0.21 us -> 42.8 us
  other arithmetic: 33.2 us -> 8.04 us
  Pallas kernels: 0 us -> 23.4 us
  matrix products: 16.2 us -> 0 us
  local copies, waits for them, and re-layouts: 23.1 us -> 8.03 us
  between operations: 14.5 us -> 2.31 us
    psum x1 -> x0, waiting for transfers between devices: 142 us -> none  [on_device(): weight_grad = lax.psum(weight_terms, ('row', 'col')) * factor]
    reduce_scatter x2 -> x0, waiting for transfers between devices: 91.2 us -> none  [the longest x1 67.7 us: on_device(): lax.psum_scatter(partial_value.astype(jnp.bfloat16), 'row', scatter_dimen...]
    all_gather x2 -> x0, waiting for transfers between devices: 67.6 us -> none  [the longest x1 48.8 us: on_device(): grad_group = lax.all_gather(hidden_grad, 'row', axis=0, tiled=True)]
    ppermute x0 -> x40, waiting for transfers between devices: none -> 53.6 us  [move(): return lax.ppermute(value, ('row', 'col'), pairs)]
    ppermute x0 -> x40, starting transfers between devices: none -> 42.8 us  [move(): return lax.ppermute(value, ('row', 'col'), pairs)]
    pallas_call x0 -> x6, Pallas kernels: none -> 23.4 us  [the longest x1 5.46 us: layer(): pl.pallas_call(functools.partial(layer_kernel, g, len(parts)), grid=(widt...]
    scatter-add x2 -> x0, other arithmetic: 18.3 us -> none  [add_turn(): return summed.at[placed].add(products)]
    dot_general x5 -> x0, matrix products: 16.2 us -> none  [the longest x2 8.84 us: add_turn(): jnp.einsum(form, matrix, picked, preferred_element_type=jnp.float32)]
  transfers between devices with their start and end apart: 5 -> 40, of which waited for: 5 -> 10; matrix products, arithmetic and copies ran while one was open for 0% -> 5% of each run, Pallas kernels for 0% -> 7%
where the time goes in v2:
time: 139 us; the launch traced here: 138 us
  waiting for transfers between devices  53.6 us (39%)
  starting transfers between devices  42.8 us (31%)
  Pallas kernels  23.4 us (17%)
  other arithmetic  8.04 us (6%)
  local copies, waits for them, and re-layouts  8.03 us (6%)
  between operations  2.31 us (2%)
    ppermute x40, waiting for transfers between devices, move(): return lax.ppermute(value, ('row', 'col'), pairs)  53.6 us
    ppermute x40, starting transfers between devices, move(): return lax.ppermute(value, ('row', 'col'), pairs)  42.8 us
    unnamed x60, local copies, waits for them, and re-layouts  6.72 us
    pallas_call x1, Pallas kernels, layer(): pl.pallas_call(functools.partial(layer_kernel, g, len(parts)), grid=(widt...  5.46 us
    pallas_call x1, Pallas kernels, forward(): pl.pallas_call(functools.partial(forward_kernel, g, slots, block, n), out...  4.21 us
    pallas_call x1, Pallas kernels, backward(): pl.pallas_call(functools.partial(backward_kernel, g, block, [len(group) f...  3.94 us
    pallas_call x1, Pallas kernels, join(): pl.pallas_call(functools.partial(join_kernel, g, places), out_shape=jax.S...  3.8 us
    pallas_call x1, Pallas kernels, build(): pl.pallas_call(functools.partial(build_kernel, g, slots, block), out_shap...  3.43 us
  transfers between devices with their start and end apart: 40, of which 10 were waited for; matrix products, arithmetic and copies ran while one was open for 5% of the time, Pallas kernels for 7%

profile of v2, /device:TPU:0, one launch (start us, length us, event | category | flops | bytes accessed | tf_op | source)
XLA Modules:
  0.0 138.2 jit_solution(2982008459819707088)
XLA Ops:
  2.0 2.9 %collective-permute-start.2 = (bf16[128,1024]{1,0:T(8,128)(2,1)}, bf16[128,1024]{1,0:T(8,128)(2,1)S(1)}, u32[]{:S(2)}, u32[]{:S(2)}) collective-permute-start(bf16[128,1024]{1,0:T(8,128)(2,1)} %refs_4_.2), channel_id=1, source_target_pairs={{0,4},{1,5},{2,6},{3,7},{4,0},{5,1},{6,2},{7,3},{8,12},{9,13},{10,... | collective-permute-start | bytes 786440 | tf_op jit(solution)/shard_map/ppermute | solution.py:47
  6.5 1.9 %collective-permute-start = (s32[17]{0:T(128)S(1)}, s32[17]{0:T(128)S(1)}, u32[]{:S(2)}, u32[]{:S(2)}) collective-permute-start(s32[17]{0:T(128)S(1)} %pad_add_fusion.refs_0_), channel_id=1, source_target_pairs={{0,4},{1,5},{2,6},{3,7},{4,0},{5,1},{6,2},{7,3},{8,12},{9,13},{10,... | collective-permute-start | bytes 212 | tf_op jit(solution)/shard_map/ppermute | solution.py:47
  9.2 8.7 %collective-permute-done.refs_1_ = s32[17]{0:T(128)S(1)} collective-permute-done((s32[17]{0:T(128)S(1)}, s32[17]{0:T(128)S(1)}, u32[]{:S(2)}, u32[]{:S(2)}) %collective-permute-start) | collective-permute-done | bytes 100 | tf_op jit(solution)/shard_map/ppermute | solution.py:47
  20.5 2.3 %collective-permute-done.1.refs_3_.refs_5_ = bf16[8,128,128]{2,1,0:T(8,128)(2,1)S(1)} collective-permute-done((bf16[8,128,128]{2,1,0:T(8,128)(2,1)}, bf16[8,128,128]{2,1,0:T(8,128)(2,1)S(1)}, u32[]{:S(2)}, u32[]{:S(2)}) %collective-permute-start.1) | collective-permute-done | bytes 262176 | tf_op jit(solution)/shard_map/ppermute | solution.py:47
  24.5 4.2 %forward.1 = (bf16[128,1024]{1,0:T(8,128)(2,1)}, bf16[128,1024]{1,0:T(8,128)(2,1)}, bf16[128,1024]{1,0:T(8,128)(2,1)}, bf16[128,1024]{1,0:T(8,128)(2,1)}) custom-call(s32[17]{0:T(128)} %copy-done.28, s32[17]{0:T(128)} %copy-done.29, bf16[8,128,128]{2,1,0:T(8,128)(2,1)} %bitcast.43, bf16[8,128,128]{2,1,0:T(8,128)(2,1)} %copy-done, bf16[128,1024]{1,0:T(8,128)(2,1)} %refs_4_.2, ...), custom_call_target="tpu_custom_call" | custom-call | tf_op jit(solution)/shard_map/forward/pallas_call | solution.py:134
  29.9 1.9 %collective-permute-start.9 = (bf16[128,1024]{1,0:T(8,128)(2,1)}, bf16[128,1024]{1,0:T(8,128)(2,1)S(1)}, u32[]{:S(2)}, u32[]{:S(2)}) collective-permute-start(bf16[128,1024]{1,0:T(8,128)(2,1)} %get-tuple-element.35), channel_id=1, source_target_pairs={{0,8},{1,9},{2,10},{3,11},{4,12},{5,13},{6,14},{7,15},{8,0},{9,1},... | collective-permute-start | bytes 786440 | tf_op jit(solution)/shard_map/ppermute | solution.py:47
  31.7 2.6 %collective-permute-start.10 = (bf16[128,1024]{1,0:T(8,128)(2,1)}, bf16[128,1024]{1,0:T(8,128)(2,1)S(1)}, u32[]{:S(2)}, u32[]{:S(2)}) collective-permute-start(bf16[128,1024]{1,0:T(8,128)(2,1)} %get-tuple-element.36), channel_id=1, source_target_pairs={{0,16},{1,17},{2,18},{3,19},{4,20},{5,21},{6,22},{7,23},{8,24},{9,... | collective-permute-start | bytes 786440 | tf_op jit(solution)/shard_map/ppermute | solution.py:47
  37.4 3.4 %build.1.matrix = bf16[512,1024]{1,0:T(8,128)(2,1)} custom-call(s32[17]{0:T(128)} %copy-done.28, s32[17]{0:T(128)} %copy-done.29, s32[17]{0:T(128)} %pad_add_fusion.1.refs_2_, s32[17]{0:T(128)} %pad_add_fusion.2.refs_3_, bf16[8,128,128]{2,1,0:T(8,128)(2,1)} %bitcast.45, bf16[8,128,128]{2,1,0:T(8,128)(2,1)} %copy-done, bf16[17,128,128]{2,1,0:T(8,128)(2,1)} %copy-done.2), custom_call_target="tpu_custom_call" | custom-call | tf_op jit(solution)/shard_map/build/pallas_call | solution.py:169
  40.9 3.1 %collective-permute-done.9.refs_1_ = bf16[128,1024]{1,0:T(8,128)(2,1)S(1)} collective-permute-done((bf16[128,1024]{1,0:T(8,128)(2,1)}, bf16[128,1024]{1,0:T(8,128)(2,1)S(1)}, u32[]{:S(2)}, u32[]{:S(2)}) %collective-permute-start.9) | collective-permute-done | bytes 262176 | tf_op jit(solution)/shard_map/ppermute | solution.py:47
  44.0 9.3 %collective-permute-done.10.refs_2_ = bf16[128,1024]{1,0:T(8,128)(2,1)S(1)} collective-permute-done((bf16[128,1024]{1,0:T(8,128)(2,1)}, bf16[128,1024]{1,0:T(8,128)(2,1)S(1)}, u32[]{:S(2)}, u32[]{:S(2)}) %collective-permute-start.10) | collective-permute-done | bytes 262176 | tf_op jit(solution)/shard_map/ppermute | solution.py:47
  54.7 5.5 %layer.1 = (bf16[128,1024]{1,0:T(8,128)(2,1)}, bf16[128,1536]{1,0:T(8,128)(2,1)}, bf16[128,1024]{1,0:T(8,128)(2,1)}, bf16[128,512]{1,0:T(8,128)(2,1)}) custom-call(bf16[128,1024]{1,0:T(8,128)(2,1)} %get-tuple-element.40.refs_0_, bf16[128,1024]{1,0:T(8,128)(2,1)} %copy-done.25, bf16[128,1024]{1,0:T(8,128)(2,1)} %copy-done.26, bf16[128,1024]{1,0:T(8,128)(2,1)} %copy-done.27, ...), custom_call_target="tpu_custom_call" | custom-call | tf_op jit(solution)/shard_map/layer/pallas_call | solution.py:258
  60.2 2.5 %collective-permute-start.15 = (bf16[128,1024]{1,0:T(8,128)(2,1)}, bf16[128,1024]{1,0:T(8,128)(2,1)S(1)}, u32[]{:S(2)}, u32[]{:S(2)}) collective-permute-start(bf16[128,1024]{1,0:T(8,128)(2,1)} %get-tuple-element.46.refs_0_), channel_id=1, source_target_pairs={{0,24},{1,25},{2,26},{3,27},{4,28},{5,29},{6,30},{7,31},{8,16},{9,... | collective-permute-start | bytes 786440 | tf_op jit(solution)/shard_map/ppermute | solution.py:47
  62.7 3.7 %collective-permute-start.14 = (bf16[128,1024]{1,0:T(8,128)(2,1)}, bf16[128,1024]{1,0:T(8,128)(2,1)S(1)}, u32[]{:S(2)}, u32[]{:S(2)}) collective-permute-start(bf16[128,1024]{1,0:T(8,128)(2,1)} %get-tuple-element.46.refs_0_), channel_id=1, source_target_pairs={{0,16},{1,17},{2,18},{3,19},{4,20},{5,21},{6,22},{7,23},{8,24},{9,... | collective-permute-start | bytes 786440 | tf_op jit(solution)/shard_map/ppermute | solution.py:47
  67.3 2.5 %terms.1 = (bf16[4,128,256]{2,1,0:T(8,128)(2,1)}, bf16[4,128,256]{2,1,0:T(8,128)(2,1)}, bf16[4,128,256]{2,1,0:T(8,128)(2,1)}, bf16[4,128,256]{2,1,0:T(8,128)(2,1)}) custom-call(bf16[128,512]{1,0:T(8,128)(2,1)} %get-tuple-element.51.keep, bf16[128,1536]{1,0:T(8,128)(2,1)} %get-tuple-element.52.share, bf16[128,1536]{1,0:T(8,128)(2,1)} %copy-done.3), custom_call_target="tpu_custom_call" | custom-call | tf_op jit(solution)/shard_map/terms/pallas_call | solution.py:302
  69.8 1.5 %collective-permute-start.24 = (bf16[4,128,256]{2,1,0:T(8,128)(2,1)}, bf16[4,128,256]{2,1,0:T(8,128)(2,1)S(1)}, u32[]{:S(2)}, u32[]{:S(2)}) collective-permute-start(bf16[4,128,256]{2,1,0:T(8,128)(2,1)} %get-tuple-element.54), channel_id=1, source_target_pairs={{0,2},{1,3},{2,0},{3,1},{4,6},{5,7},{6,4},{7,5},{8,10},{9,11},{10,... | collective-permute-start | bytes 786440 | tf_op jit(solution)/shard_map/ppermute | solution.py:47
  71.3 1.5 %collective-permute-start.25 = (bf16[4,128,256]{2,1,0:T(8,128)(2,1)}, bf16[4,128,256]{2,1,0:T(8,128)(2,1)S(1)}, u32[]{:S(2)}, u32[]{:S(2)}) collective-permute-start(bf16[4,128,256]{2,1,0:T(8,128)(2,1)} %get-tuple-element.55), channel_id=1, source_target_pairs={{0,4},{1,5},{2,6},{3,7},{4,0},{5,1},{6,2},{7,3},{8,12},{9,13},{10,... | collective-permute-start | bytes 786440 | tf_op jit(solution)/shard_map/ppermute | solution.py:47
  73.9 13.9 %collective-permute-done.14.refs_2_ = bf16[128,1024]{1,0:T(8,128)(2,1)S(1)} collective-permute-done((bf16[128,1024]{1,0:T(8,128)(2,1)}, bf16[128,1024]{1,0:T(8,128)(2,1)S(1)}, u32[]{:S(2)}, u32[]{:S(2)}) %collective-permute-start.14) | collective-permute-done | bytes 262176 | tf_op jit(solution)/shard_map/ppermute | solution.py:47
  89.9 3.4 %collective-permute-start.27 = (bf16[128,256]{1,0:T(8,128)(2,1)S(1)}, bf16[128,256]{1,0:T(8,128)(2,1)S(1)}, u32[]{:S(2)}, u32[]{:S(2)}) collective-permute-start(bf16[128,256]{1,0:T(8,128)(2,1)S(1)} %get-tuple-element.61), channel_id=1, source_target_pairs={{0,8},{1,9},{2,10},{3,11},{4,12},{5,13},{6,14},{7,15},{8,0},{9,1},... | collective-permute-start | bytes 196616 | tf_op jit(solution)/shard_map/ppermute | solution.py:47
  93.3 2.5 %collective-permute-start.29 = (bf16[128,256]{1,0:T(8,128)(2,1)S(1)}, bf16[128,256]{1,0:T(8,128)(2,1)S(1)}, u32[]{:S(2)}, u32[]{:S(2)}) collective-permute-start(bf16[128,256]{1,0:T(8,128)(2,1)S(1)} %get-tuple-element.62), channel_id=1, source_target_pairs={{0,24},{1,25},{2,26},{3,27},{4,28},{5,29},{6,30},{7,31},{8,16},{9,... | collective-permute-start | bytes 196616 | tf_op jit(solution)/shard_map/ppermute | solution.py:47
  97.3 3.9 %backward.1 = (bf16[128,1024]{1,0:T(8,128)(2,1)}, bf16[128,1024]{1,0:T(8,128)(2,1)}, bf16[128,1024]{1,0:T(8,128)(2,1)}, bf16[128,1024]{1,0:T(8,128)(2,1)}) custom-call(bf16[512,1024]{1,0:T(8,128)(2,1)} %build.1.matrix, bf16[128,1024]{1,0:T(8,128)(2,1)} %get-tuple-element.46.refs_0_, bf16[128,1024]{1,0:T(8,128)(2,1)} %copy-done.6, ...), custom_call_target="tpu_custom_call" | custom-call | tf_op jit(solution)/shard_map/backward/pallas_call | solution.py:197
  101.2 1.5 %collective-permute-start.20 = (bf16[128,1024]{1,0:T(8,128)(2,1)}, bf16[128,1024]{1,0:T(8,128)(2,1)S(1)}, u32[]{:S(2)}, u32[]{:S(2)}) collective-permute-start(bf16[128,1024]{1,0:T(8,128)(2,1)} %get-tuple-element.48), channel_id=1, source_target_pairs={{0,2},{1,3},{2,0},{3,1},{4,6},{5,7},{6,4},{7,5},{8,10},{9,11},{10,... | collective-permute-start | bytes 786440 | tf_op jit(solution)/shard_map/ppermute | solution.py:47
  102.8 1.5 %collective-permute-start.32 = (bf16[128,256]{1,0:T(8,128)(2,1)S(1)}, bf16[128,256]{1,0:T(8,128)(2,1)S(1)}, u32[]{:S(2)}, u32[]{:S(2)}) collective-permute-start(bf16[128,256]{1,0:T(8,128)(2,1)S(1)} %fusion.3), channel_id=1, source_target_pairs={{0,24},{1,25},{2,26},{3,27},{4,28},{5,29},{6,30},{7,31},{8,16},{9,... | collective-permute-start | bytes 196616 | tf_op jit(solution)/shard_map/ppermute | solution.py:47
  104.3 1.8 %collective-permute-start.31 = (bf16[128,256]{1,0:T(8,128)(2,1)S(1)}, bf16[128,256]{1,0:T(8,128)(2,1)S(1)}, u32[]{:S(2)}, u32[]{:S(2)}) collective-permute-start(bf16[128,256]{1,0:T(8,128)(2,1)S(1)} %fusion.3), channel_id=1, source_target_pairs={{0,16},{1,17},{2,18},{3,19},{4,20},{5,21},{6,22},{7,23},{8,24},{9,... | collective-permute-start | bytes 196616 | tf_op jit(solution)/shard_map/ppermute | solution.py:47
  107.3 1.5 %collective-permute-start.21 = (bf16[128,1024]{1,0:T(8,128)(2,1)}, bf16[128,1024]{1,0:T(8,128)(2,1)S(1)}, u32[]{:S(2)}, u32[]{:S(2)}) collective-permute-start(bf16[128,1024]{1,0:T(8,128)(2,1)} %get-tuple-element.49), channel_id=1, source_target_pairs={{0,4},{1,5},{2,6},{3,7},{4,0},{5,1},{6,2},{7,3},{8,12},{9,13},{10,... | collective-permute-start | bytes 786440 | tf_op jit(solution)/shard_map/ppermute | solution.py:47
  109.5 1.5 %collective-permute-done.31 = bf16[128,256]{1,0:T(8,128)(2,1)S(1)} collective-permute-done((bf16[128,256]{1,0:T(8,128)(2,1)S(1)}, bf16[128,256]{1,0:T(8,128)(2,1)S(1)}, u32[]{:S(2)}, u32[]{:S(2)}) %collective-permute-start.31) | collective-permute-done | bytes 65568 | tf_op jit(solution)/shard_map/ppermute | solution.py:47
  111.1 1.9 %collective-permute-start.35 = (bf16[4,128,256]{2,1,0:T(8,128)(2,1)S(1)}, bf16[4,128,256]{2,1,0:T(8,128)(2,1)S(1)}, u32[]{:S(2)}, u32[]{:S(2)}) collective-permute-start(bf16[4,128,256]{2,1,0:T(8,128)(2,1)S(1)} %pad_maximum_fusion.1.refs_0_), channel_id=1, source_target_pairs={{0,6},{1,7},{2,4},{3,5},{4,2},{5,3},{6,0},{7,1},{8,14},{9,15},{10,... | collective-permute-start | bytes 786440 | tf_op jit(solution)/shard_map/ppermute | solution.py:47
  114.6 1.8 %collective-permute-start.22 = (bf16[128,1024]{1,0:T(8,128)(2,1)}, bf16[128,1024]{1,0:T(8,128)(2,1)S(1)}, u32[]{:S(2)}, u32[]{:S(2)}) collective-permute-start(bf16[128,1024]{1,0:T(8,128)(2,1)} %get-tuple-element.50), channel_id=1, source_target_pairs={{0,6},{1,7},{2,4},{3,5},{4,2},{5,3},{6,0},{7,1},{8,14},{9,15},{10,... | collective-permute-start | bytes 786440 | tf_op jit(solution)/shard_map/ppermute | solution.py:47
  116.5 4.8 %collective-permute-done.35.refs_3_ = bf16[4,128,256]{2,1,0:T(8,128)(2,1)S(1)} collective-permute-done((bf16[4,128,256]{2,1,0:T(8,128)(2,1)S(1)}, bf16[4,128,256]{2,1,0:T(8,128)(2,1)S(1)}, u32[]{:S(2)}, u32[]{:S(2)}) %collective-permute-start.35) | collective-permute-done | bytes 262176 | tf_op jit(solution)/shard_map/ppermute | solution.py:47
  121.3 5.1 %collective-permute-done.34.refs_2_ = bf16[4,128,256]{2,1,0:T(8,128)(2,1)S(1)} collective-permute-done((bf16[4,128,256]{2,1,0:T(8,128)(2,1)S(1)}, bf16[4,128,256]{2,1,0:T(8,128)(2,1)S(1)}, u32[]{:S(2)}, u32[]{:S(2)}) %collective-permute-start.34) | collective-permute-done | bytes 262176 | tf_op jit(solution)/shard_map/ppermute | solution.py:47
  127.0 4.0 %collective-permute-done.22 = bf16[128,1024]{1,0:T(8,128)(2,1)S(1)} collective-permute-done((bf16[128,1024]{1,0:T(8,128)(2,1)}, bf16[128,1024]{1,0:T(8,128)(2,1)S(1)}, u32[]{:S(2)}, u32[]{:S(2)}) %collective-permute-start.22) | collective-permute-done | bytes 262176 | tf_op jit(solution)/shard_map/ppermute | solution.py:47
  131.0 1.8 %add_convert_fusion.1 = bf16[128,1024]{1,0:T(8,128)(2,1)} fusion(bf16[128,1024]{1,0:T(8,128)(2,1)S(1)} %collective-permute-done.22, bf16[128,1024]{1,0:T(8,128)(2,1)S(1)} %collective-permute-done.21, bf16[128,1024]{1,0:T(8,128)(2,1)S(1)} %collective-permute-done.20, bf16[128,1024]{1,0:T(8,128)(2,1)} %get-tuple-element.47), kind=kLoop, calls=%fused_computation.2 | loop fusion | flops 1048576 | bytes 1310720 | tf_op jit(solution)/shard_map/convert_element_type | solution.py:386
  134.4 3.8 %join.1 = f32[1024,1024]{1,0:T(8,128)} custom-call(bf16[4,128,256]{2,1,0:T(8,128)(2,1)} %copy-done.1, bf16[4,128,256]{2,1,0:T(8,128)(2,1)} %copy-done.14, bf16[4,128,256]{2,1,0:T(8,128)(2,1)} %copy-done.13, bf16[4,128,256]{2,1,0:T(8,128)(2,1)} %copy-done.11, bf16[4,128,256]{2,1,0:T(8,128)(2,1)} %copy-done.20, bf16[4,128,256]{2,1,0:T(8,128)(2,1)} %copy-done.24, ...), custom_call_target="tpu_custom_call" | custom-call | tf_op jit(solution)/shard_map/join/pallas_call | solution.py:332
  (134 shorter events, 23.3 us)
Async XLA Ops:
  2.0 17.2 %collective-permute-start.2 = (bf16[128,1024]{1,0:T(8,128)(2,1)}, bf16[128,1024]{1,0:T(8,128)(2,1)S(1)}, u32[]{:S(2)}, u32[]{:S(2)}) collective-permute-start(bf16[128,1024]{1,0:T(8,128)(2,1)} %refs_4_.2), channel_id=1, source_target_pairs={{0,4},{1,5},{2,6},{3,7},{4,0},{5,1},{6,2},{7,3},{8,12},{9,13},{10,... | collective-permute-start | bytes 786440 | tf_op jit(solution)/shard_map/ppermute | solution.py:47
  5.0 14.8 %collective-permute-start.7 = (bf16[128,1024]{1,0:T(8,128)(2,1)}, bf16[128,1024]{1,0:T(8,128)(2,1)S(1)}, u32[]{:S(2)}, u32[]{:S(2)}) collective-permute-start(bf16[128,1024]{1,0:T(8,128)(2,1)} %refs_4_.2), channel_id=1, source_target_pairs={{0,6},{1,7},{2,4},{3,5},{4,2},{5,3},{6,0},{7,1},{8,14},{9,15},{10,... | collective-permute-start | bytes 786440 | tf_op jit(solution)/shard_map/ppermute | solution.py:47
  6.5 13.4 %collective-permute-start.4 = (bf16[128,1024]{1,0:T(8,128)(2,1)}, bf16[128,1024]{1,0:T(8,128)(2,1)S(1)}, u32[]{:S(2)}, u32[]{:S(2)}) collective-permute-start(bf16[128,1024]{1,0:T(8,128)(2,1)} %refs_4_.2), channel_id=1, source_target_pairs={{0,2},{1,3},{2,0},{3,1},{4,6},{5,7},{6,4},{7,5},{8,10},{9,11},{10,... | collective-permute-start | bytes 786440 | tf_op jit(solution)/shard_map/ppermute | solution.py:47
  6.5 11.4 %collective-permute-start = (s32[17]{0:T(128)S(1)}, s32[17]{0:T(128)S(1)}, u32[]{:S(2)}, u32[]{:S(2)}) collective-permute-start(s32[17]{0:T(128)S(1)} %pad_add_fusion.refs_0_), channel_id=1, source_target_pairs={{0,4},{1,5},{2,6},{3,7},{4,0},{5,1},{6,2},{7,3},{8,12},{9,13},{10,... | collective-permute-start | bytes 212 | tf_op jit(solution)/shard_map/ppermute | solution.py:47
  8.5 14.3 %collective-permute-start.1 = (bf16[8,128,128]{2,1,0:T(8,128)(2,1)}, bf16[8,128,128]{2,1,0:T(8,128)(2,1)S(1)}, u32[]{:S(2)}, u32[]{:S(2)}) collective-permute-start(bf16[8,128,128]{2,1,0:T(8,128)(2,1)} %bitcast.42), channel_id=1, source_target_pairs={{0,4},{1,5},{2,6},{3,7},{4,0},{5,1},{6,2},{7,3},{8,12},{9,13},{10,... | collective-permute-start | bytes 786440 | tf_op jit(solution)/shard_map/ppermute | solution.py:47
  29.9 14.2 %collective-permute-start.9 = (bf16[128,1024]{1,0:T(8,128)(2,1)}, bf16[128,1024]{1,0:T(8,128)(2,1)S(1)}, u32[]{:S(2)}, u32[]{:S(2)}) collective-permute-start(bf16[128,1024]{1,0:T(8,128)(2,1)} %get-tuple-element.35), channel_id=1, source_target_pairs={{0,8},{1,9},{2,10},{3,11},{4,12},{5,13},{6,14},{7,15},{8,0},{9,1},... | collective-permute-start | bytes 786440 | tf_op jit(solution)/shard_map/ppermute | solution.py:47
  31.7 21.5 %collective-permute-start.10 = (bf16[128,1024]{1,0:T(8,128)(2,1)}, bf16[128,1024]{1,0:T(8,128)(2,1)S(1)}, u32[]{:S(2)}, u32[]{:S(2)}) collective-permute-start(bf16[128,1024]{1,0:T(8,128)(2,1)} %get-tuple-element.36), channel_id=1, source_target_pairs={{0,16},{1,17},{2,18},{3,19},{4,20},{5,21},{6,22},{7,23},{8,24},{9,... | collective-permute-start | bytes 786440 | tf_op jit(solution)/shard_map/ppermute | solution.py:47
  34.3 19.0 %collective-permute-start.11 = (bf16[128,1024]{1,0:T(8,128)(2,1)}, bf16[128,1024]{1,0:T(8,128)(2,1)S(1)}, u32[]{:S(2)}, u32[]{:S(2)}) collective-permute-start(bf16[128,1024]{1,0:T(8,128)(2,1)} %get-tuple-element.37), channel_id=1, source_target_pairs={{0,24},{1,25},{2,26},{3,27},{4,28},{5,29},{6,30},{7,31},{8,16},{9,... | collective-permute-start | bytes 786440 | tf_op jit(solution)/shard_map/ppermute | solution.py:47
  60.1 6.4 %collective-permute-start.23 = (bf16[128,1536]{1,0:T(8,128)(2,1)}, bf16[128,1536]{1,0:T(8,128)(2,1)S(1)}, u32[]{:S(2)}, u32[]{:S(2)}) collective-permute-start(bf16[128,1536]{1,0:T(8,128)(2,1)} %get-tuple-element.52.share), channel_id=1, source_target_pairs={{0,1},{1,0},{2,3},{3,2},{4,5},{5,4},{6,7},{7,6},{8,9},{9,8},{10,11... | collective-permute-start | bytes 1179656 | tf_op jit(solution)/shard_map/ppermute | solution.py:47
  60.2 12.7 %collective-permute-start.15 = (bf16[128,1024]{1,0:T(8,128)(2,1)}, bf16[128,1024]{1,0:T(8,128)(2,1)S(1)}, u32[]{:S(2)}, u32[]{:S(2)}) collective-permute-start(bf16[128,1024]{1,0:T(8,128)(2,1)} %get-tuple-element.46.refs_0_), channel_id=1, source_target_pairs={{0,24},{1,25},{2,26},{3,27},{4,28},{5,29},{6,30},{7,31},{8,16},{9,... | collective-permute-start | bytes 786440 | tf_op jit(solution)/shard_map/ppermute | solution.py:47
  62.7 25.1 %collective-permute-start.14 = (bf16[128,1024]{1,0:T(8,128)(2,1)}, bf16[128,1024]{1,0:T(8,128)(2,1)S(1)}, u32[]{:S(2)}, u32[]{:S(2)}) collective-permute-start(bf16[128,1024]{1,0:T(8,128)(2,1)} %get-tuple-element.46.refs_0_), channel_id=1, source_target_pairs={{0,16},{1,17},{2,18},{3,19},{4,20},{5,21},{6,22},{7,23},{8,24},{9,... | collective-permute-start | bytes 786440 | tf_op jit(solution)/shard_map/ppermute | solution.py:47
  66.4 21.4 %collective-permute-start.13 = (bf16[128,1024]{1,0:T(8,128)(2,1)}, bf16[128,1024]{1,0:T(8,128)(2,1)S(1)}, u32[]{:S(2)}, u32[]{:S(2)}) collective-permute-start(bf16[128,1024]{1,0:T(8,128)(2,1)} %get-tuple-element.46.refs_0_), channel_id=1, source_target_pairs={{0,8},{1,9},{2,10},{3,11},{4,12},{5,13},{6,14},{7,15},{8,0},{9,1},... | collective-permute-start | bytes 786440 | tf_op jit(solution)/shard_map/ppermute | solution.py:47
  69.8 18.5 %collective-permute-start.24 = (bf16[4,128,256]{2,1,0:T(8,128)(2,1)}, bf16[4,128,256]{2,1,0:T(8,128)(2,1)S(1)}, u32[]{:S(2)}, u32[]{:S(2)}) collective-permute-start(bf16[4,128,256]{2,1,0:T(8,128)(2,1)} %get-tuple-element.54), channel_id=1, source_target_pairs={{0,2},{1,3},{2,0},{3,1},{4,6},{5,7},{6,4},{7,5},{8,10},{9,11},{10,... | collective-permute-start | bytes 786440 | tf_op jit(solution)/shard_map/ppermute | solution.py:47
  71.3 17.0 %collective-permute-start.25 = (bf16[4,128,256]{2,1,0:T(8,128)(2,1)}, bf16[4,128,256]{2,1,0:T(8,128)(2,1)S(1)}, u32[]{:S(2)}, u32[]{:S(2)}) collective-permute-start(bf16[4,128,256]{2,1,0:T(8,128)(2,1)} %get-tuple-element.55), channel_id=1, source_target_pairs={{0,4},{1,5},{2,6},{3,7},{4,0},{5,1},{6,2},{7,3},{8,12},{9,13},{10,... | collective-permute-start | bytes 786440 | tf_op jit(solution)/shard_map/ppermute | solution.py:47
  72.9 16.0 %collective-permute-start.26 = (bf16[4,128,256]{2,1,0:T(8,128)(2,1)}, bf16[4,128,256]{2,1,0:T(8,128)(2,1)S(1)}, u32[]{:S(2)}, u32[]{:S(2)}) collective-permute-start(bf16[4,128,256]{2,1,0:T(8,128)(2,1)} %get-tuple-element.56), channel_id=1, source_target_pairs={{0,6},{1,7},{2,4},{3,5},{4,2},{5,3},{6,0},{7,1},{8,14},{9,15},{10,... | collective-permute-start | bytes 786440 | tf_op jit(solution)/shard_map/ppermute | solution.py:47
  87.9 7.9 %collective-permute-start.19 = (bf16[128,1024]{1,0:T(8,128)(2,1)S(1)}, bf16[128,1024]{1,0:T(8,128)(2,1)S(1)}, u32[]{:S(2)}, u32[]{:S(2)}) collective-permute-start(bf16[128,1024]{1,0:T(8,128)(2,1)S(1)} %collective-permute-done.15.refs_3_), channel_id=1, source_target_pairs={{0,1},{1,0},{2,3},{3,2},{4,5},{5,4},{6,7},{7,6},{8,9},{9,8},{10,11... | collective-permute-start | bytes 786440 | tf_op jit(solution)/shard_map/ppermute | solution.py:47
  88.3 7.5 %collective-permute-start.18 = (bf16[128,1024]{1,0:T(8,128)(2,1)S(1)}, bf16[128,1024]{1,0:T(8,128)(2,1)S(1)}, u32[]{:S(2)}, u32[]{:S(2)}) collective-permute-start(bf16[128,1024]{1,0:T(8,128)(2,1)S(1)} %collective-permute-done.14.refs_2_), channel_id=1, source_target_pairs={{0,1},{1,0},{2,3},{3,2},{4,5},{5,4},{6,7},{7,6},{8,9},{9,8},{10,11... | collective-permute-start | bytes 786440 | tf_op jit(solution)/shard_map/ppermute | solution.py:47
  88.4 7.4 %collective-permute-start.17 = (bf16[128,1024]{1,0:T(8,128)(2,1)S(1)}, bf16[128,1024]{1,0:T(8,128)(2,1)S(1)}, u32[]{:S(2)}, u32[]{:S(2)}) collective-permute-start(bf16[128,1024]{1,0:T(8,128)(2,1)S(1)} %collective-permute-done.13.refs_1_), channel_id=1, source_target_pairs={{0,1},{1,0},{2,3},{3,2},{4,5},{5,4},{6,7},{7,6},{8,9},{9,8},{10,11... | collective-permute-start | bytes 786440 | tf_op jit(solution)/shard_map/ppermute | solution.py:47
  89.9 12.8 %collective-permute-start.27 = (bf16[128,256]{1,0:T(8,128)(2,1)S(1)}, bf16[128,256]{1,0:T(8,128)(2,1)S(1)}, u32[]{:S(2)}, u32[]{:S(2)}) collective-permute-start(bf16[128,256]{1,0:T(8,128)(2,1)S(1)} %get-tuple-element.61), channel_id=1, source_target_pairs={{0,8},{1,9},{2,10},{3,11},{4,12},{5,13},{6,14},{7,15},{8,0},{9,1},... | collective-permute-start | bytes 196616 | tf_op jit(solution)/shard_map/ppermute | solution.py:47
  93.3 9.5 %collective-permute-start.29 = (bf16[128,256]{1,0:T(8,128)(2,1)S(1)}, bf16[128,256]{1,0:T(8,128)(2,1)S(1)}, u32[]{:S(2)}, u32[]{:S(2)}) collective-permute-start(bf16[128,256]{1,0:T(8,128)(2,1)S(1)} %get-tuple-element.62), channel_id=1, source_target_pairs={{0,24},{1,25},{2,26},{3,27},{4,28},{5,29},{6,30},{7,31},{8,16},{9,... | collective-permute-start | bytes 196616 | tf_op jit(solution)/shard_map/ppermute | solution.py:47
  95.8 7.0 %collective-permute-start.28 = (bf16[128,256]{1,0:T(8,128)(2,1)S(1)}, bf16[128,256]{1,0:T(8,128)(2,1)S(1)}, u32[]{:S(2)}, u32[]{:S(2)}) collective-permute-start(bf16[128,256]{1,0:T(8,128)(2,1)S(1)} %get-tuple-element.63), channel_id=1, source_target_pairs={{0,16},{1,17},{2,18},{3,19},{4,20},{5,21},{6,22},{7,23},{8,24},{9,... | collective-permute-start | bytes 196616 | tf_op jit(solution)/shard_map/ppermute | solution.py:47
  101.2 13.4 %collective-permute-start.20 = (bf16[128,1024]{1,0:T(8,128)(2,1)}, bf16[128,1024]{1,0:T(8,128)(2,1)S(1)}, u32[]{:S(2)}, u32[]{:S(2)}) collective-permute-start(bf16[128,1024]{1,0:T(8,128)(2,1)} %get-tuple-element.48), channel_id=1, source_target_pairs={{0,2},{1,3},{2,0},{3,1},{4,6},{5,7},{6,4},{7,5},{8,10},{9,11},{10,... | collective-permute-start | bytes 786440 | tf_op jit(solution)/shard_map/ppermute | solution.py:47
  102.8 6.7 %collective-permute-start.32 = (bf16[128,256]{1,0:T(8,128)(2,1)S(1)}, bf16[128,256]{1,0:T(8,128)(2,1)S(1)}, u32[]{:S(2)}, u32[]{:S(2)}) collective-permute-start(bf16[128,256]{1,0:T(8,128)(2,1)S(1)} %fusion.3), channel_id=1, source_target_pairs={{0,24},{1,25},{2,26},{3,27},{4,28},{5,29},{6,30},{7,31},{8,16},{9,... | collective-permute-start | bytes 196616 | tf_op jit(solution)/shard_map/ppermute | solution.py:47
  104.3 6.7 %collective-permute-start.31 = (bf16[128,256]{1,0:T(8,128)(2,1)S(1)}, bf16[128,256]{1,0:T(8,128)(2,1)S(1)}, u32[]{:S(2)}, u32[]{:S(2)}) collective-permute-start(bf16[128,256]{1,0:T(8,128)(2,1)S(1)} %fusion.3), channel_id=1, source_target_pairs={{0,16},{1,17},{2,18},{3,19},{4,20},{5,21},{6,22},{7,23},{8,24},{9,... | collective-permute-start | bytes 196616 | tf_op jit(solution)/shard_map/ppermute | solution.py:47
  107.3 9.2 %collective-permute-start.21 = (bf16[128,1024]{1,0:T(8,128)(2,1)}, bf16[128,1024]{1,0:T(8,128)(2,1)S(1)}, u32[]{:S(2)}, u32[]{:S(2)}) collective-permute-start(bf16[128,1024]{1,0:T(8,128)(2,1)} %get-tuple-element.49), channel_id=1, source_target_pairs={{0,4},{1,5},{2,6},{3,7},{4,0},{5,1},{6,2},{7,3},{8,12},{9,13},{10,... | collective-permute-start | bytes 786440 | tf_op jit(solution)/shard_map/ppermute | solution.py:47
  111.1 10.3 %collective-permute-start.35 = (bf16[4,128,256]{2,1,0:T(8,128)(2,1)S(1)}, bf16[4,128,256]{2,1,0:T(8,128)(2,1)S(1)}, u32[]{:S(2)}, u32[]{:S(2)}) collective-permute-start(bf16[4,128,256]{2,1,0:T(8,128)(2,1)S(1)} %pad_maximum_fusion.1.refs_0_), channel_id=1, source_target_pairs={{0,6},{1,7},{2,4},{3,5},{4,2},{5,3},{6,0},{7,1},{8,14},{9,15},{10,... | collective-permute-start | bytes 786440 | tf_op jit(solution)/shard_map/ppermute | solution.py:47
  113.0 13.5 %collective-permute-start.34 = (bf16[4,128,256]{2,1,0:T(8,128)(2,1)S(1)}, bf16[4,128,256]{2,1,0:T(8,128)(2,1)S(1)}, u32[]{:S(2)}, u32[]{:S(2)}) collective-permute-start(bf16[4,128,256]{2,1,0:T(8,128)(2,1)S(1)} %pad_maximum_fusion.1.refs_0_), channel_id=1, source_target_pairs={{0,4},{1,5},{2,6},{3,7},{4,0},{5,1},{6,2},{7,3},{8,12},{9,13},{10,... | collective-permute-start | bytes 786440 | tf_op jit(solution)/shard_map/ppermute | solution.py:47
  113.6 12.9 %collective-permute-start.33 = (bf16[4,128,256]{2,1,0:T(8,128)(2,1)S(1)}, bf16[4,128,256]{2,1,0:T(8,128)(2,1)S(1)}, u32[]{:S(2)}, u32[]{:S(2)}) collective-permute-start(bf16[4,128,256]{2,1,0:T(8,128)(2,1)S(1)} %pad_maximum_fusion.1.refs_0_), channel_id=1, source_target_pairs={{0,2},{1,3},{2,0},{3,1},{4,6},{5,7},{6,4},{7,5},{8,10},{9,11},{10,... | collective-permute-start | bytes 786440 | tf_op jit(solution)/shard_map/ppermute | solution.py:47
  114.6 16.4 %collective-permute-start.22 = (bf16[128,1024]{1,0:T(8,128)(2,1)}, bf16[128,1024]{1,0:T(8,128)(2,1)S(1)}, u32[]{:S(2)}, u32[]{:S(2)}) collective-permute-start(bf16[128,1024]{1,0:T(8,128)(2,1)} %get-tuple-element.50), channel_id=1, source_target_pairs={{0,6},{1,7},{2,4},{3,5},{4,2},{5,3},{6,0},{7,1},{8,14},{9,15},{10,... | collective-permute-start | bytes 786440 | tf_op jit(solution)/shard_map/ppermute | solution.py:47
  116.5 16.4 %collective-permute-start.36 = (bf16[4,128,256]{2,1,0:T(8,128)(2,1)S(1)}, bf16[4,128,256]{2,1,0:T(8,128)(2,1)S(1)}, u32[]{:S(2)}, u32[]{:S(2)}) collective-permute-start(bf16[4,128,256]{2,1,0:T(8,128)(2,1)S(1)} %pad_maximum_fusion.1.refs_0_), channel_id=1, source_target_pairs={{0,1},{1,0},{2,3},{3,2},{4,5},{5,4},{6,7},{7,6},{8,9},{9,8},{10,11... | collective-permute-start | bytes 786440 | tf_op jit(solution)/shard_map/ppermute | solution.py:47
  121.3 11.5 %collective-permute-start.39 = (bf16[4,128,256]{2,1,0:T(8,128)(2,1)S(1)}, bf16[4,128,256]{2,1,0:T(8,128)(2,1)S(1)}, u32[]{:S(2)}, u32[]{:S(2)}) collective-permute-start(bf16[4,128,256]{2,1,0:T(8,128)(2,1)S(1)} %collective-permute-done.35.refs_3_), channel_id=1, source_target_pairs={{0,1},{1,0},{2,3},{3,2},{4,5},{5,4},{6,7},{7,6},{8,9},{9,8},{10,11... | collective-permute-start | bytes 786440 | tf_op jit(solution)/shard_map/ppermute | solution.py:47
  126.5 6.4 %collective-permute-start.37 = (bf16[4,128,256]{2,1,0:T(8,128)(2,1)S(1)}, bf16[4,128,256]{2,1,0:T(8,128)(2,1)S(1)}, u32[]{:S(2)}, u32[]{:S(2)}) collective-permute-start(bf16[4,128,256]{2,1,0:T(8,128)(2,1)S(1)} %collective-permute-done.33.refs_1_), channel_id=1, source_target_pairs={{0,1},{1,0},{2,3},{3,2},{4,5},{5,4},{6,7},{7,6},{8,9},{9,8},{10,11... | collective-permute-start | bytes 786440 | tf_op jit(solution)/shard_map/ppermute | solution.py:47
  (38 other events, 181.2 us)

commit v3 on v2

--- a/solution.py
+++ b/solution.py
@@ -12,6 +12,7 @@
 VMEM_LIMIT = 56 * 2**20
 SMEM_SPEC = pl.BlockSpec(memory_space=pltpu.SMEM)
 VMEM_SPEC = pl.BlockSpec(memory_space=pltpu.VMEM)
+HBM_SPEC = pl.BlockSpec(memory_space=pl.ANY)
 
 
 COST = {}
@@ -46,13 +47,13 @@
         ]
         return lax.ppermute(value, ("row", "col"), pairs)
 
-    def along(self, value, hops):
-        pairs = [
-            (self.index(z, x, y, k), self.index(hops[z], x, y, k))
-            for z, x, y, k in self.devices()
-            if z in hops
+    def swap_xy(self, value):
+        groups = [
+            [self.index(z, x, y, k) for x in range(self.X) for y in range(self.Y)]
+            for z in range(self.Z)
+            for k in range(self.K)
         ]
-        return lax.ppermute(value, ("row", "col"), pairs)
+        return lax.all_to_all(value, ("row", "col"), 0, 0, axis_index_groups=groups, tiled=True)
 
     def here(self):
         r, c = lax.axis_index("row"), lax.axis_index("col")
@@ -86,8 +87,13 @@
         pl.loop(0, slots)(one)
 
 
-def reader(listed, slots):
-    return (lambda s: listed[s]), (lambda s: listed[slots + s]), (lambda: listed[2 * slots])
+def reader(listed, slots, at=0):
+    first = at * (2 * slots + 1)
+    return (
+        lambda s: listed[first + s],
+        lambda s: listed[first + slots + s],
+        lambda: listed[first + 2 * slots],
+    )
 
 
 def multiply(matrix, stacked, outs, block):
@@ -147,7 +153,7 @@
 
 
 def build_kernel(g, slots, block, *refs):
-    lists, tiles, bundle, matrix = refs[:4], refs[4:6], refs[6], refs[7]
+    lists, tiles, matrix = refs[:3], refs[3:7], refs[7]
     z, x, y, k = g.here()
     matrix[...] = jnp.zeros_like(matrix)
     for dk in range(g.K):
@@ -157,29 +163,29 @@
                 at_z, at_x = row // g.X, row % g.X
                 at_y, at_k = col // g.K, col % g.K
                 wanted = jnp.logical_and(at_x == x, at_k == k)
-                return wanted, dx * g.Y + (at_y ^ y), dk * g.Z + (at_z ^ z), True
-
-            held = tiles[dx] if dk == 0 else bundle.at[pl.ds(dx * slots, slots)]
-            listed = reader(lists[dk * g.X + dx], slots)
-            add_tiles(g, matrix, held, listed, slots, block, place)
-
-
-def build(g, lists, tiles, bundle):
+                return wanted, (x ^ dx) * g.Y + at_y, dk * g.Z + (at_z ^ z), True
+
+            listed = reader(lists[2], slots, dx) if dk else reader(lists[dx], slots)
+            add_tiles(g, matrix, tiles[dk * g.X + dx], listed, slots, block, place)
+
+
+def build(g, lists, tiles):
     slots, block = tiles[0].shape[0], tiles[0].shape[1]
     return pl.pallas_call(
         functools.partial(build_kernel, g, slots, block),
         out_shape=jax.ShapeDtypeStruct((g.X * g.Y * block, g.K * g.Z * block), BF16),
-        in_specs=[SMEM_SPEC] * 4 + [VMEM_SPEC] * 3,
+        in_specs=[SMEM_SPEC] * 3 + [VMEM_SPEC] * 4,
         out_specs=VMEM_SPEC,
         compiler_params=params(),
         cost_estimate=cost("build"),
         name="build",
-    )(*lists, *tiles, bundle)
+    )(*lists, *tiles)
 
 
 def backward_kernel(g, block, groups, matrix, *refs):
     n_in = sum(groups)
-    outs, stacked = refs[n_in:-1], refs[-1]
+    out, stacked = refs[n_in:]
+    outs = [out.at[pl.ds(i * block, block)] for i in range(matrix.shape[0] // block)]
     at = 0
     for i, n in enumerate(groups):
         held = refs[at][...]
@@ -192,13 +198,12 @@
 
 def backward(g, matrix, groups):
     block, width = groups[0][0].shape
-    n_out = matrix.shape[0] // block
     flat = [v for group in groups for v in group]
     return pl.pallas_call(
         functools.partial(backward_kernel, g, block, [len(group) for group in groups]),
-        out_shape=[jax.ShapeDtypeStruct((block, width), BF16)] * n_out,
+        out_shape=jax.ShapeDtypeStruct((matrix.shape[0], width), BF16),
         in_specs=[VMEM_SPEC] * (1 + len(flat)),
-        out_specs=[VMEM_SPEC] * n_out,
+        out_specs=VMEM_SPEC,
         scratch_shapes=[pltpu.VMEM((len(groups) * block, width), BF16)],
         compiler_params=params(),
         cost_estimate=cost("backward"),
@@ -217,57 +222,44 @@
     parts = refs[:n_in]
     weight, cotangent = refs[n_in : n_in + 2]
     activated, share, back, keep = refs[n_in + 2 : n_in + 6]
-    agg, total = refs[n_in + 6 :]
-    j, last = pl.program_id(0), pl.num_programs(0) - 1
+    agg = refs[n_in + 6]
     half = keep.shape[1]
-
-    @pl.when(j == 0)
-    def _():
-        summed = parts[0][...].astype(F32)
-        for part in parts[1:]:
-            summed += part[...].astype(F32)
-        agg[...] = summed.astype(BF16)
-        total[...] = jnp.zeros_like(total)
-        core = g.here()[3]
-        keep[...] = agg[:, pl.ds(pl.multiple_of(core * half, half), half)]
-        share[:, :half] = agg[:, pl.ds(pl.multiple_of((1 - core) * half, half), half)]
-
-    hidden = jnp.dot(agg[...], weight[...], preferred_element_type=F32)
-    sigmoid = jax.nn.sigmoid(hidden)
-    activated[...] = (hidden * sigmoid).astype(BF16)
-    slope = sigmoid * (1.0 + hidden * (1.0 - sigmoid))
-    grad = (cotangent[...].astype(F32) * slope).astype(BF16)
-    share[:, pl.ds(pl.multiple_of(half + j * grad.shape[1], grad.shape[1]), grad.shape[1])] = grad
-    total[...] += lax.dot_general(
-        grad, weight[...], (((1,), (1,)), ((), ())), preferred_element_type=F32
-    )
-
-    @pl.when(j == last)
-    def _():
-        back[...] = total[...].astype(BF16)
+    summed = parts[0][...].astype(F32)
+    for part in parts[1:]:
+        summed += part[...].astype(F32)
+    agg[...] = summed.astype(BF16)
+    core = g.here()[3]
+    keep[...] = agg[:, pl.ds(pl.multiple_of(core * half, half), half)]
+    share[:, :half] = agg[:, pl.ds(pl.multiple_of((1 - core) * half, half), half)]
+    width = weight.shape[1]
+    tile = 256 if width % 256 == 0 else width
+    for j in range(width // tile):
+        cols = slice(j * tile, (j + 1) * tile)
+        hidden = jnp.dot(agg[...], weight[:, cols], preferred_element_type=F32)
+        sigmoid = jax.nn.sigmoid(hidden)
+        activated[:, cols] = (hidden * sigmoid).astype(BF16)
+        slope = sigmoid * (1.0 + hidden * (1.0 - sigmoid))
+        grad = (cotangent[:, cols].astype(F32) * slope).astype(BF16)
+        share[:, half + j * tile : half + (j + 1) * tile] = grad
+    back[...] = lax.dot_general(
+        share[:, half:], weight[...], (((1,), (1,)), ((), ())), preferred_element_type=F32
+    ).astype(BF16)
 
 
 def layer(g, parts, weight, cotangent):
     rows, depth = parts[0].shape
     width = weight.shape[1]
-    tile = 256 if width % 256 == 0 else width
-    whole = pl.BlockSpec((rows, depth), lambda j: (0, 0))
-    half = pl.BlockSpec((rows, depth // 2), lambda j: (0, 0))
-    shared = pl.BlockSpec((rows, depth // 2 + width), lambda j: (0, 0))
-    cut = pl.BlockSpec((rows, tile), lambda j: (0, j))
     return pl.pallas_call(
         functools.partial(layer_kernel, g, len(parts)),
-        grid=(width // tile,),
         out_shape=[
             jax.ShapeDtypeStruct((rows, width), BF16),
             jax.ShapeDtypeStruct((rows, depth // 2 + width), BF16),
             jax.ShapeDtypeStruct((rows, depth), BF16),
             jax.ShapeDtypeStruct((rows, depth // 2), BF16),
         ],
-        in_specs=[whole] * len(parts)
-        + [pl.BlockSpec((depth, tile), lambda j: (0, j)), cut],
-        out_specs=[cut, shared, whole, half],
-        scratch_shapes=[pltpu.VMEM((rows, depth), BF16), pltpu.VMEM((rows, depth), F32)],
+        in_specs=[VMEM_SPEC] * (len(parts) + 2),
+        out_specs=[VMEM_SPEC] * 4,
+        scratch_shapes=[pltpu.VMEM((rows, depth), BF16)],
         compiler_params=params(),
         cost_estimate=cost("layer"),
         name="layer",
@@ -315,25 +307,43 @@
 
 
 def join_kernel(g, places, *refs):
-    out = refs[-1]
-    rows, width = refs[0].shape[1:]
+    n = len(places)
+    pieces, out = refs[:n], refs[n]
+    held, whole, in_sems, out_sems = refs[n + 1 :]
+    some, rows, width = pieces[0].shape
     z, x, y, k = g.here()
-    for (dk, dx, dy, first), held in zip(places, refs):
+    copies = [pltpu.make_async_copy(v, held.at[i], in_sems.at[i]) for i, v in enumerate(pieces)]
+    for copy in copies:
+        copy.start()
+    sent = []
+    for i, (dk, dx, dy) in enumerate(places):
+        copies[i].wait()
         at = ((k ^ dk) * g.X + (x ^ dx)) * g.Y + (y ^ dy)
-        for i in range(held.shape[0]):
-            col = z ^ (first + i)
-            out[
-                pl.ds(pl.multiple_of(at * rows, rows), rows),
-                pl.ds(pl.multiple_of(col * width, width), width),
-            ] = held[i].astype(F32)
+        at = pl.ds(pl.multiple_of(at * rows, rows), rows)
+        for dz in range(some):
+            cols = pl.ds(pl.multiple_of((z ^ dz) * width, width), width)
+            whole[i, :, cols] = held[i, dz].astype(F32)
+        copy = pltpu.make_async_copy(whole.at[i], out.at[at], out_sems.at[i])
+        copy.start()
+        sent.append(copy)
+    for copy in sent:
+        copy.wait()
 
 
 def join(g, places, pieces, shape):
+    n = len(pieces)
+    some, rows, width = pieces[0].shape
     return pl.pallas_call(
         functools.partial(join_kernel, g, places),
         out_shape=jax.ShapeDtypeStruct(shape, F32),
-        in_specs=[VMEM_SPEC] * len(pieces),
-        out_specs=VMEM_SPEC,
+        in_specs=[HBM_SPEC] * n,
+        out_specs=HBM_SPEC,
+        scratch_shapes=[
+            pltpu.VMEM((n, some, rows, width), BF16),
+            pltpu.VMEM((n, rows, some * width), F32),
+            pltpu.SemaphoreType.DMA((n,)),
+            pltpu.SemaphoreType.DMA((n,)),
+        ],
         compiler_params=params(),
         cost_estimate=cost("join"),
         name="join",
@@ -352,38 +362,33 @@
     lists = [listed, g.move(listed, dx=1)]
     tiles = [tile_values[0, 0], g.move(after(tile_values[0, 0], listed), dx=1)]
     near = {(0, 0): features}
-    for dx, dy in squares[1:]:
-        near[dx, dy] = g.move(after(features, listed), dx=dx, dy=dy)
+    for dx, dy in [(1, 0)] + [at for at in squares[1:] if at != (1, 0)]:
+        if dx and dy:
+            near[dx, dy] = g.move(after(near[1, 0], lists[1]), dy=dy)
+        else:
+            near[dx, dy] = g.move(after(features, listed), dx=dx, dy=dy)
     blocks = []
     for at in squares:
         value = near[at] if at != (0, 0) else after(features, near[1, 0])
         blocks += [near[at], g.move(value, dk=1)]
-    sums = forward(g, lists, tiles, blocks)
+    others = [g.move(after(tiles[0], near[1, 0]), dk=1)]
+    lists.append(g.move(jnp.concatenate(lists), dk=1))
+    blocks[0] = after(blocks[0], (others, lists[2]))
+    sums = forward(g, lists[:2], tiles, blocks)
     parts = [sums[0]] + [g.move(sums[dz], dz=dz) for dz in range(1, g.Z)]
-
-    slots, block = tiles[0].shape[:2]
-    rows = [jnp.broadcast_to(v, slots) for at in lists for v in (at[:slots], at[slots:-1], at[-1])]
-    codes = jnp.pad(jnp.stack(rows).astype(BF16), ((0, block - len(rows)), (0, block - slots)))[None]
-    bundle = g.move(jnp.concatenate(after(tiles, sums) + [codes], axis=0), dk=1)
-    got = bundle[2 * slots, : len(rows), :slots].astype(jnp.int32)
-    others = [jnp.concatenate([got[i], got[i + 1], got[i + 2, :1]]) for i in (0, 3)]
-    matrix = build(g, lists + others, tiles, bundle)
+    others.append(g.move(after(tiles[1], sums), dk=1))
+    matrix = build(g, lists, tiles + others)
     parts, matrix = pin((parts, matrix))
     activated, share, back, keep = layer(g, parts, weight, cotangent)
 
     shares = terms(g, keep, share, g.move(share, dk=1))
 
-    if g.Z == 0:
-        far = g.move(back, dz=2)
-        far = after(far, shares)
-        groups = [[back], [g.move(back, dz=1)], [far]]
-        groups.append([g.along(back, {1: 2, 2: 1}), g.along(far, {1: 0, 2: 3})])
-    else:
-        groups = [[back]] + [[g.move(back, dz=dz)] for dz in range(1, g.Z)]
+    groups = [[back]] + [[g.move(back, dz=dz)] for dz in range(1, g.Z)]
     arrived = groups[1:]
     groups += [[g.move(v, dk=1) for v in group] for group in groups]
     deltas = backward(g, matrix, groups)
-    feat_grad = fold(g, deltas).astype(BF16)
+    feat = g.swap_xy(deltas).astype(F32).reshape(g.X * g.Y, -1, deltas.shape[1])
+    feat_grad = jnp.sum(feat, axis=0).astype(BF16)
 
     pieces = after(fold(g, shares).astype(BF16), arrived)
     total = pieces[0].astype(F32)
@@ -395,7 +400,8 @@
     column = after(column, deltas)
     held = [column if at == (0, 0) else g.move(column, dx=at[0], dy=at[1]) for at in squares]
     held += [g.move(v, dk=1) for v in held]
-    places = [(dk, *at, 0) for dk in range(g.K) for at in squares]
+    places = [(dk, *at) for dk in range(g.K) for at in squares]
+    held[-1] = after(held[-1], feat_grad)
     weight_grad = join(g, places, held, weight.shape)
     return (activated, feat_grad, weight_grad)
 

time: 139 us -> 132 us (0.950)
  other arithmetic: 8.04 us -> 3.59 us
  Pallas kernels: 23.4 us -> 21.3 us
    ppermute x40 -> x39, starting transfers between devices: 42.8 us -> 39.2 us  [move(): return lax.ppermute(value, ('row', 'col'), pairs)]
    all_to_all x0 -> x1, starting transfers between devices: none -> 3.51 us  [swap_xy(): lax.all_to_all(value, ('row', 'col'), 0, 0, axis_index_groups=groups, til...]
    concatenate x3 -> x1, other arithmetic: 3.62 us -> 0.75 us  [on_device(): lists.append(g.move(jnp.concatenate(lists), dk=1))]
    convert_element_type x2 -> x0, other arithmetic: 1.83 us -> none  [the longest x1 1.82 us: on_device(): feat_grad = fold(g, deltas).astype(BF16)]
    pallas_call x1, Pallas kernels: 5.46 us -> 3.89 us  [layer(): pl.pallas_call(functools.partial(layer_kernel, g, len(parts)), out_shape=...]
    ppermute x40 -> x39, waiting for transfers between devices: 53.6 us -> 54.9 us  [move(): return lax.ppermute(value, ('row', 'col'), pairs)]
    unnamed x60 -> x64, local copies, waits for them, and re-layouts: 6.72 us -> 7.02 us
  transfers between devices with their start and end apart: 40 -> 40, of which waited for: 10 -> 14; matrix products, arithmetic and copies ran while one was open for 5% -> 2% of each run, Pallas kernels for 7% -> 8%
where the time goes in v3:
time: 132 us; the launch traced here: 131 us
  waiting for transfers between devices  54.9 us (42%)
  starting transfers between devices  42.8 us (32%)
  Pallas kernels  21.3 us (16%)
  local copies, waits for them, and re-layouts  7.03 us (5%)
  other arithmetic  3.59 us (3%)
  between operations  1.59 us (1%)
    ppermute x39, waiting for transfers between devices, move(): return lax.ppermute(value, ('row', 'col'), pairs)  54.9 us
    ppermute x39, starting transfers between devices, move(): return lax.ppermute(value, ('row', 'col'), pairs)  39.2 us
    unnamed x64, local copies, waits for them, and re-layouts  7.02 us
    pallas_call x1, Pallas kernels, forward(): pl.pallas_call(functools.partial(forward_kernel, g, slots, block, n), out...  4.19 us
    pallas_call x1, Pallas kernels, backward(): pl.pallas_call(functools.partial(backward_kernel, g, block, [len(group) f...  4.09 us
    pallas_call x1, Pallas kernels, layer(): pl.pallas_call(functools.partial(layer_kernel, g, len(parts)), out_shape=...  3.89 us
    all_to_all x1, starting transfers between devices, swap_xy(): lax.all_to_all(value, ('row', 'col'), 0, 0, axis_index_groups=groups, til...  3.51 us
    pallas_call x1, Pallas kernels, build(): pl.pallas_call(functools.partial(build_kernel, g, slots, block), out_shap...  3.42 us
  transfers between devices with their start and end apart: 40, of which 14 were waited for; matrix products, arithmetic and copies ran while one was open for 2% of the time, Pallas kernels for 8%

profile of v3, /device:TPU:0, one launch (start us, length us, event | category | flops | bytes accessed | tf_op | source)
XLA Modules:
  0.0 131.2 jit_solution(14306562584646969488)
XLA Ops:
  2.0 2.9 %collective-permute-start.2 = (bf16[128,1024]{1,0:T(8,128)(2,1)}, bf16[128,1024]{1,0:T(8,128)(2,1)S(1)}, u32[]{:S(2)}, u32[]{:S(2)}) collective-permute-start(bf16[128,1024]{1,0:T(8,128)(2,1)} %refs_4_.1), channel_id=1, source_target_pairs={{0,4},{1,5},{2,6},{3,7},{4,0},{5,1},{6,2},{7,3},{8,12},{9,13},{10,... | collective-permute-start | bytes 786440 | tf_op jit(solution)/shard_map/ppermute | solution.py:48
  5.1 2.0 %collective-permute-start.6 = (bf16[128,1024]{1,0:T(8,128)(2,1)}, bf16[128,1024]{1,0:T(8,128)(2,1)S(1)}, u32[]{:S(2)}, u32[]{:S(2)}) collective-permute-start(bf16[128,1024]{1,0:T(8,128)(2,1)} %refs_4_.1), channel_id=1, source_target_pairs={{0,2},{1,3},{2,0},{3,1},{4,6},{5,7},{6,4},{7,5},{8,10},{9,11},{10,... | collective-permute-start | bytes 786440 | tf_op jit(solution)/shard_map/ppermute | solution.py:48
  7.0 4.5 %collective-permute-done.refs_1_ = s32[17]{0:T(128)S(1)} collective-permute-done((s32[17]{0:T(128)S(1)}, s32[17]{0:T(128)S(1)}, u32[]{:S(2)}, u32[]{:S(2)}) %collective-permute-start) | collective-permute-done | bytes 100 | tf_op jit(solution)/shard_map/ppermute | solution.py:48
  11.6 1.8 %collective-permute-start.9 = (bf16[128,1024]{1,0:T(8,128)(2,1)S(1)}, bf16[128,1024]{1,0:T(8,128)(2,1)S(1)}, u32[]{:S(2)}, u32[]{:S(2)}) collective-permute-start(bf16[128,1024]{1,0:T(8,128)(2,1)S(1)} %collective-permute-done.2.refs_8_), channel_id=1, source_target_pairs={{0,2},{1,3},{2,0},{3,1},{4,6},{5,7},{6,4},{7,5},{8,10},{9,11},{10,... | collective-permute-start | bytes 786440 | tf_op jit(solution)/shard_map/ppermute | solution.py:48
  13.5 1.5 %collective-permute-start.1 = (bf16[8,128,128]{2,1,0:T(8,128)(2,1)}, bf16[8,128,128]{2,1,0:T(8,128)(2,1)S(1)}, u32[]{:S(2)}, u32[]{:S(2)}) collective-permute-start(bf16[8,128,128]{2,1,0:T(8,128)(2,1)} %bitcast.22), channel_id=1, source_target_pairs={{0,4},{1,5},{2,6},{3,7},{4,0},{5,1},{6,2},{7,3},{8,12},{9,13},{10,... | collective-permute-start | bytes 786440 | tf_op jit(solution)/shard_map/ppermute | solution.py:48
  17.6 2.8 %collective-permute-done.9.refs_10_ = bf16[128,1024]{1,0:T(8,128)(2,1)S(1)} collective-permute-done((bf16[128,1024]{1,0:T(8,128)(2,1)S(1)}, bf16[128,1024]{1,0:T(8,128)(2,1)S(1)}, u32[]{:S(2)}, u32[]{:S(2)}) %collective-permute-start.9) | collective-permute-done | bytes 262176 | tf_op jit(solution)/shard_map/ppermute | solution.py:48
  20.4 1.7 %collective-permute-done.1.refs_3_.refs_4_ = bf16[8,128,128]{2,1,0:T(8,128)(2,1)S(1)} collective-permute-done((bf16[8,128,128]{2,1,0:T(8,128)(2,1)}, bf16[8,128,128]{2,1,0:T(8,128)(2,1)S(1)}, u32[]{:S(2)}, u32[]{:S(2)}) %collective-permute-start.1) | collective-permute-done | bytes 262176 | tf_op jit(solution)/shard_map/ppermute | solution.py:48
  23.7 4.2 %forward.1 = (bf16[128,1024]{1,0:T(8,128)(2,1)}, bf16[128,1024]{1,0:T(8,128)(2,1)}, bf16[128,1024]{1,0:T(8,128)(2,1)}, bf16[128,1024]{1,0:T(8,128)(2,1)}) custom-call(s32[17]{0:T(128)} %copy-done.30, s32[17]{0:T(128)} %copy-done.29, bf16[8,128,128]{2,1,0:T(8,128)(2,1)} %bitcast.23, bf16[8,128,128]{2,1,0:T(8,128)(2,1)} %copy-done, bf16[128,1024]{1,0:T(8,128)(2,1)} %refs_4_.1, ...), custom_call_target="tpu_custom_call" | custom-call | tf_op jit(solution)/shard_map/forward/pallas_call | solution.py:140
  27.9 1.6 %collective-permute-start.11 = (bf16[128,1024]{1,0:T(8,128)(2,1)}, bf16[128,1024]{1,0:T(8,128)(2,1)S(1)}, u32[]{:S(2)}, u32[]{:S(2)}) collective-permute-start(bf16[128,1024]{1,0:T(8,128)(2,1)} %get-tuple-element.37), channel_id=1, source_target_pairs={{0,8},{1,9},{2,10},{3,11},{4,12},{5,13},{6,14},{7,15},{8,0},{9,1},... | collective-permute-start | bytes 786440 | tf_op jit(solution)/shard_map/ppermute | solution.py:48
  29.5 2.6 %collective-permute-start.12 = (bf16[128,1024]{1,0:T(8,128)(2,1)}, bf16[128,1024]{1,0:T(8,128)(2,1)S(1)}, u32[]{:S(2)}, u32[]{:S(2)}) collective-permute-start(bf16[128,1024]{1,0:T(8,128)(2,1)} %get-tuple-element.38), channel_id=1, source_target_pairs={{0,16},{1,17},{2,18},{3,19},{4,20},{5,21},{6,22},{7,23},{8,24},{9,... | collective-permute-start | bytes 786440 | tf_op jit(solution)/shard_map/ppermute | solution.py:48
  33.1 3.4 %build.1.matrix = bf16[512,1024]{1,0:T(8,128)(2,1)} custom-call(s32[17]{0:T(128)} %copy-done.30, s32[17]{0:T(128)} %copy-done.29, s32[34]{0:T(128)} %copy-done.31, bf16[8,128,128]{2,1,0:T(8,128)(2,1)} %bitcast.24, bf16[8,128,128]{2,1,0:T(8,128)(2,1)} %copy-done, bf16[8,128,128]{2,1,0:T(8,128)(2,1)} %copy-done.6, bf16[8,128,128]{2,1,0:T(8,128)(2,1)} %copy-done.25), custom_call_target="tpu_custom_call" | custom-call | tf_op jit(solution)/shard_map/build/pallas_call | solution.py:174
  36.5 5.5 %collective-permute-done.11.refs_1_ = bf16[128,1024]{1,0:T(8,128)(2,1)S(1)} collective-permute-done((bf16[128,1024]{1,0:T(8,128)(2,1)}, bf16[128,1024]{1,0:T(8,128)(2,1)S(1)}, u32[]{:S(2)}, u32[]{:S(2)}) %collective-permute-start.11) | collective-permute-done | bytes 262176 | tf_op jit(solution)/shard_map/ppermute | solution.py:48
  42.0 9.1 %collective-permute-done.12.refs_2_ = bf16[128,1024]{1,0:T(8,128)(2,1)S(1)} collective-permute-done((bf16[128,1024]{1,0:T(8,128)(2,1)}, bf16[128,1024]{1,0:T(8,128)(2,1)S(1)}, u32[]{:S(2)}, u32[]{:S(2)}) %collective-permute-start.12) | collective-permute-done | bytes 262176 | tf_op jit(solution)/shard_map/ppermute | solution.py:48
  52.5 3.9 %layer.1 = (bf16[128,1024]{1,0:T(8,128)(2,1)}, bf16[128,1536]{1,0:T(8,128)(2,1)}, bf16[128,1024]{1,0:T(8,128)(2,1)}, bf16[128,512]{1,0:T(8,128)(2,1)}) custom-call(bf16[128,1024]{1,0:T(8,128)(2,1)} %get-tuple-element.41.refs_0_, bf16[128,1024]{1,0:T(8,128)(2,1)} %copy-done.26, bf16[128,1024]{1,0:T(8,128)(2,1)} %copy-done.27, bf16[128,1024]{1,0:T(8,128)(2,1)} %copy-done.28, ...), custom_call_target="tpu_custom_call" | custom-call | tf_op jit(solution)/shard_map/layer/pallas_call | solution.py:252
  56.4 2.5 %collective-permute-start.17 = (bf16[128,1024]{1,0:T(8,128)(2,1)}, bf16[128,1024]{1,0:T(8,128)(2,1)S(1)}, u32[]{:S(2)}, u32[]{:S(2)}) collective-permute-start(bf16[128,1024]{1,0:T(8,128)(2,1)} %get-tuple-element.47.refs_0_), channel_id=1, source_target_pairs={{0,24},{1,25},{2,26},{3,27},{4,28},{5,29},{6,30},{7,31},{8,16},{9,... | collective-permute-start | bytes 786440 | tf_op jit(solution)/shard_map/ppermute | solution.py:48
  58.9 3.7 %collective-permute-start.16 = (bf16[128,1024]{1,0:T(8,128)(2,1)}, bf16[128,1024]{1,0:T(8,128)(2,1)S(1)}, u32[]{:S(2)}, u32[]{:S(2)}) collective-permute-start(bf16[128,1024]{1,0:T(8,128)(2,1)} %get-tuple-element.47.refs_0_), channel_id=1, source_target_pairs={{0,16},{1,17},{2,18},{3,19},{4,20},{5,21},{6,22},{7,23},{8,24},{9,... | collective-permute-start | bytes 786440 | tf_op jit(solution)/shard_map/ppermute | solution.py:48
  63.4 2.5 %terms.1 = (bf16[4,128,256]{2,1,0:T(8,128)(2,1)}, bf16[4,128,256]{2,1,0:T(8,128)(2,1)}, bf16[4,128,256]{2,1,0:T(8,128)(2,1)}, bf16[4,128,256]{2,1,0:T(8,128)(2,1)}) custom-call(bf16[128,512]{1,0:T(8,128)(2,1)} %get-tuple-element.48.keep, bf16[128,1536]{1,0:T(8,128)(2,1)} %get-tuple-element.49.share, bf16[128,1536]{1,0:T(8,128)(2,1)} %copy-done.2), custom_call_target="tpu_custom_call" | custom-call | tf_op jit(solution)/shard_map/terms/pallas_call | solution.py:294
  66.7 1.5 %collective-permute-start.24 = (bf16[4,128,256]{2,1,0:T(8,128)(2,1)}, bf16[4,128,256]{2,1,0:T(8,128)(2,1)S(1)}, u32[]{:S(2)}, u32[]{:S(2)}) collective-permute-start(bf16[4,128,256]{2,1,0:T(8,128)(2,1)} %get-tuple-element.52), channel_id=1, source_target_pairs={{0,4},{1,5},{2,6},{3,7},{4,0},{5,1},{6,2},{7,3},{8,12},{9,13},{10,... | collective-permute-start | bytes 786440 | tf_op jit(solution)/shard_map/ppermute | solution.py:48
  68.2 1.3 collective-permute-start.25
  69.5 14.5 %collective-permute-done.16.refs_2_ = bf16[128,1024]{1,0:T(8,128)(2,1)S(1)} collective-permute-done((bf16[128,1024]{1,0:T(8,128)(2,1)}, bf16[128,1024]{1,0:T(8,128)(2,1)S(1)}, u32[]{:S(2)}, u32[]{:S(2)}) %collective-permute-start.16) | collective-permute-done | bytes 262176 | tf_op jit(solution)/shard_map/ppermute | solution.py:48
  86.1 3.4 %collective-permute-start.26 = (bf16[128,256]{1,0:T(8,128)(2,1)S(1)}, bf16[128,256]{1,0:T(8,128)(2,1)S(1)}, u32[]{:S(2)}, u32[]{:S(2)}) collective-permute-start(bf16[128,256]{1,0:T(8,128)(2,1)S(1)} %get-tuple-element.57), channel_id=1, source_target_pairs={{0,8},{1,9},{2,10},{3,11},{4,12},{5,13},{6,14},{7,15},{8,0},{9,1},... | collective-permute-start | bytes 196616 | tf_op jit(solution)/shard_map/ppermute | solution.py:48
  89.5 2.5 %collective-permute-start.28 = (bf16[128,256]{1,0:T(8,128)(2,1)S(1)}, bf16[128,256]{1,0:T(8,128)(2,1)S(1)}, u32[]{:S(2)}, u32[]{:S(2)}) collective-permute-start(bf16[128,256]{1,0:T(8,128)(2,1)S(1)} %get-tuple-element.58), channel_id=1, source_target_pairs={{0,24},{1,25},{2,26},{3,27},{4,28},{5,29},{6,30},{7,31},{8,16},{9,... | collective-permute-start | bytes 196616 | tf_op jit(solution)/shard_map/ppermute | solution.py:48
  93.5 4.1 %backward.1 = bf16[512,1024]{1,0:T(8,128)(2,1)} custom-call(bf16[512,1024]{1,0:T(8,128)(2,1)} %build.1.matrix, bf16[128,1024]{1,0:T(8,128)(2,1)} %get-tuple-element.47.refs_0_, bf16[128,1024]{1,0:T(8,128)(2,1)} %copy-done.5, bf16[128,1024]{1,0:T(8,128)(2,1)} %copy-done.4, bf16[128,1024]{1,0:T(8,128)(2,1)} %copy-done.3, bf16[128,1024]{1,0:T(8,128)(2,1)} %copy-done.9, ...), custom_call_target="tpu_custom_call" | custom-call | tf_op jit(solution)/shard_map/backward/pallas_call | solution.py:202
  97.6 3.5 %all-to-all-start = ((bf16[4,128,1024]{2,1,0:T(8,128)(2,1)}), bf16[4,128,1024]{2,1,0:T(8,128)(2,1)S(1)}, u32[]{:S(2)}, u32[]{:S(2)}) async-start(bf16[4,128,1024]{2,1,0:T(8,128)(2,1)} %bitcast.20), calls=%async_computation | async-start | bytes 2097152 | tf_op jit(solution)/shard_map/all_to_all | solution.py:56
  101.2 1.5 %collective-permute-start.31 = (bf16[128,256]{1,0:T(8,128)(2,1)S(1)}, bf16[128,256]{1,0:T(8,128)(2,1)S(1)}, u32[]{:S(2)}, u32[]{:S(2)}) collective-permute-start(bf16[128,256]{1,0:T(8,128)(2,1)S(1)} %fusion.3), channel_id=1, source_target_pairs={{0,24},{1,25},{2,26},{3,27},{4,28},{5,29},{6,30},{7,31},{8,16},{9,... | collective-permute-start | bytes 196616 | tf_op jit(solution)/shard_map/ppermute | solution.py:48
  102.7 1.8 %collective-permute-start.30 = (bf16[128,256]{1,0:T(8,128)(2,1)S(1)}, bf16[128,256]{1,0:T(8,128)(2,1)S(1)}, u32[]{:S(2)}, u32[]{:S(2)}) collective-permute-start(bf16[128,256]{1,0:T(8,128)(2,1)S(1)} %fusion.3), channel_id=1, source_target_pairs={{0,16},{1,17},{2,18},{3,19},{4,20},{5,21},{6,22},{7,23},{8,24},{9,... | collective-permute-start | bytes 196616 | tf_op jit(solution)/shard_map/ppermute | solution.py:48
  104.5 1.1 collective-permute-start.29
  105.6 2.1 %collective-permute-done.31 = bf16[128,256]{1,0:T(8,128)(2,1)S(1)} collective-permute-done((bf16[128,256]{1,0:T(8,128)(2,1)S(1)}, bf16[128,256]{1,0:T(8,128)(2,1)S(1)}, u32[]{:S(2)}, u32[]{:S(2)}) %collective-permute-start.31) | collective-permute-done | bytes 65568 | tf_op jit(solution)/shard_map/ppermute | solution.py:48
  109.2 2.7 %collective-permute-start.34 = (bf16[4,128,256]{2,1,0:T(8,128)(2,1)S(1)}, bf16[4,128,256]{2,1,0:T(8,128)(2,1)S(1)}, u32[]{:S(2)}, u32[]{:S(2)}) collective-permute-start(bf16[4,128,256]{2,1,0:T(8,128)(2,1)S(1)} %pad_maximum_fusion.refs_0_), channel_id=1, source_target_pairs={{0,6},{1,7},{2,4},{3,5},{4,2},{5,3},{6,0},{7,1},{8,14},{9,15},{10,... | collective-permute-start | bytes 786440 | tf_op jit(solution)/shard_map/ppermute | solution.py:48
  112.8 9.9 %collective-permute-done.34.refs_3_ = bf16[4,128,256]{2,1,0:T(8,128)(2,1)S(1)} collective-permute-done((bf16[4,128,256]{2,1,0:T(8,128)(2,1)S(1)}, bf16[4,128,256]{2,1,0:T(8,128)(2,1)S(1)}, u32[]{:S(2)}, u32[]{:S(2)}) %collective-permute-start.34) | collective-permute-done | bytes 262176 | tf_op jit(solution)/shard_map/ppermute | solution.py:48
  123.1 1.8 %collective-permute-done.33.refs_2_ = bf16[4,128,256]{2,1,0:T(8,128)(2,1)S(1)} collective-permute-done((bf16[4,128,256]{2,1,0:T(8,128)(2,1)S(1)}, bf16[4,128,256]{2,1,0:T(8,128)(2,1)S(1)}, u32[]{:S(2)}, u32[]{:S(2)}) %collective-permute-start.33) | collective-permute-done | bytes 262176 | tf_op jit(solution)/shard_map/ppermute | solution.py:48
  128.1 3.1 %join.1 = f32[1024,1024]{1,0:T(8,128)} custom-call(bf16[4,128,256]{2,1,0:T(8,128)(2,1)} %copy-done.1, bf16[4,128,256]{2,1,0:T(8,128)(2,1)} %copy-done.15, bf16[4,128,256]{2,1,0:T(8,128)(2,1)} %copy-done.14, bf16[4,128,256]{2,1,0:T(8,128)(2,1)} %copy-done.13, bf16[4,128,256]{2,1,0:T(8,128)(2,1)} %copy-done.19, bf16[4,128,256]{2,1,0:T(8,128)(2,1)} %copy-done.23, ...), custom_call_target="tpu_custom_call" | custom-call | tf_op jit(solution)/shard_map/join/pallas_call | solution.py:336
  (125 shorter events, 18.5 us)
Async XLA Ops:
  2.0 9.5 %collective-permute-start.2 = (bf16[128,1024]{1,0:T(8,128)(2,1)}, bf16[128,1024]{1,0:T(8,128)(2,1)S(1)}, u32[]{:S(2)}, u32[]{:S(2)}) collective-permute-start(bf16[128,1024]{1,0:T(8,128)(2,1)} %refs_4_.1), channel_id=1, source_target_pairs={{0,4},{1,5},{2,6},{3,7},{4,0},{5,1},{6,2},{7,3},{8,12},{9,13},{10,... | collective-permute-start | bytes 786440 | tf_op jit(solution)/shard_map/ppermute | solution.py:48
  5.0 6.6 %collective-permute-start = (s32[17]{0:T(128)S(1)}, s32[17]{0:T(128)S(1)}, u32[]{:S(2)}, u32[]{:S(2)}) collective-permute-start(s32[17]{0:T(128)S(1)} %pad_add_fusion.refs_0_), channel_id=1, source_target_pairs={{0,4},{1,5},{2,6},{3,7},{4,0},{5,1},{6,2},{7,3},{8,12},{9,13},{10,... | collective-permute-start | bytes 212 | tf_op jit(solution)/shard_map/ppermute | solution.py:48
  5.1 12.0 %collective-permute-start.6 = (bf16[128,1024]{1,0:T(8,128)(2,1)}, bf16[128,1024]{1,0:T(8,128)(2,1)S(1)}, u32[]{:S(2)}, u32[]{:S(2)}) collective-permute-start(bf16[128,1024]{1,0:T(8,128)(2,1)} %refs_4_.1), channel_id=1, source_target_pairs={{0,2},{1,3},{2,0},{3,1},{4,6},{5,7},{6,4},{7,5},{8,10},{9,11},{10,... | collective-permute-start | bytes 786440 | tf_op jit(solution)/shard_map/ppermute | solution.py:48
  11.6 5.8 %collective-permute-start.3 = (bf16[8,128,128]{2,1,0:T(8,128)(2,1)}, bf16[8,128,128]{2,1,0:T(8,128)(2,1)S(1)}, u32[]{:S(2)}, u32[]{:S(2)}) collective-permute-start(bf16[8,128,128]{2,1,0:T(8,128)(2,1)} %bitcast.21), channel_id=1, source_target_pairs={{0,1},{1,0},{2,3},{3,2},{4,5},{5,4},{6,7},{7,6},{8,9},{9,8},{10,11... | collective-permute-start | bytes 786440 | tf_op jit(solution)/shard_map/ppermute | solution.py:48
  11.6 8.7 %collective-permute-start.9 = (bf16[128,1024]{1,0:T(8,128)(2,1)S(1)}, bf16[128,1024]{1,0:T(8,128)(2,1)S(1)}, u32[]{:S(2)}, u32[]{:S(2)}) collective-permute-start(bf16[128,1024]{1,0:T(8,128)(2,1)S(1)} %collective-permute-done.2.refs_8_), channel_id=1, source_target_pairs={{0,2},{1,3},{2,0},{3,1},{4,6},{5,7},{6,4},{7,5},{8,10},{9,11},{10,... | collective-permute-start | bytes 786440 | tf_op jit(solution)/shard_map/ppermute | solution.py:48
  13.5 8.6 %collective-permute-start.1 = (bf16[8,128,128]{2,1,0:T(8,128)(2,1)}, bf16[8,128,128]{2,1,0:T(8,128)(2,1)S(1)}, u32[]{:S(2)}, u32[]{:S(2)}) collective-permute-start(bf16[8,128,128]{2,1,0:T(8,128)(2,1)} %bitcast.22), channel_id=1, source_target_pairs={{0,4},{1,5},{2,6},{3,7},{4,0},{5,1},{6,2},{7,3},{8,12},{9,13},{10,... | collective-permute-start | bytes 786440 | tf_op jit(solution)/shard_map/ppermute | solution.py:48
  16.8 5.2 %collective-permute-start.5 = (bf16[128,1024]{1,0:T(8,128)(2,1)}, bf16[128,1024]{1,0:T(8,128)(2,1)S(1)}, u32[]{:S(2)}, u32[]{:S(2)}) collective-permute-start(bf16[128,1024]{1,0:T(8,128)(2,1)} %refs_4_.1), channel_id=1, source_target_pairs={{0,1},{1,0},{2,3},{3,2},{4,5},{5,4},{6,7},{7,6},{8,9},{9,8},{10,11... | collective-permute-start | bytes 786440 | tf_op jit(solution)/shard_map/ppermute | solution.py:48
  17.1 5.0 %collective-permute-start.7 = (bf16[128,1024]{1,0:T(8,128)(2,1)S(1)}, bf16[128,1024]{1,0:T(8,128)(2,1)S(1)}, u32[]{:S(2)}, u32[]{:S(2)}) collective-permute-start(bf16[128,1024]{1,0:T(8,128)(2,1)S(1)} %collective-permute-done.6.refs_6_), channel_id=1, source_target_pairs={{0,1},{1,0},{2,3},{3,2},{4,5},{5,4},{6,7},{7,6},{8,9},{9,8},{10,11... | collective-permute-start | bytes 786440 | tf_op jit(solution)/shard_map/ppermute | solution.py:48
  17.4 4.7 %collective-permute-start.8 = (bf16[128,1024]{1,0:T(8,128)(2,1)S(1)}, bf16[128,1024]{1,0:T(8,128)(2,1)S(1)}, u32[]{:S(2)}, u32[]{:S(2)}) collective-permute-start(bf16[128,1024]{1,0:T(8,128)(2,1)S(1)} %collective-permute-done.2.refs_8_), channel_id=1, source_target_pairs={{0,1},{1,0},{2,3},{3,2},{4,5},{5,4},{6,7},{7,6},{8,9},{9,8},{10,11... | collective-permute-start | bytes 786440 | tf_op jit(solution)/shard_map/ppermute | solution.py:48
  27.9 14.1 %collective-permute-start.11 = (bf16[128,1024]{1,0:T(8,128)(2,1)}, bf16[128,1024]{1,0:T(8,128)(2,1)S(1)}, u32[]{:S(2)}, u32[]{:S(2)}) collective-permute-start(bf16[128,1024]{1,0:T(8,128)(2,1)} %get-tuple-element.37), channel_id=1, source_target_pairs={{0,8},{1,9},{2,10},{3,11},{4,12},{5,13},{6,14},{7,15},{8,0},{9,1},... | collective-permute-start | bytes 786440 | tf_op jit(solution)/shard_map/ppermute | solution.py:48
  29.5 21.5 %collective-permute-start.12 = (bf16[128,1024]{1,0:T(8,128)(2,1)}, bf16[128,1024]{1,0:T(8,128)(2,1)S(1)}, u32[]{:S(2)}, u32[]{:S(2)}) collective-permute-start(bf16[128,1024]{1,0:T(8,128)(2,1)} %get-tuple-element.38), channel_id=1, source_target_pairs={{0,16},{1,17},{2,18},{3,19},{4,20},{5,21},{6,22},{7,23},{8,24},{9,... | collective-permute-start | bytes 786440 | tf_op jit(solution)/shard_map/ppermute | solution.py:48
  32.1 18.9 %collective-permute-start.13 = (bf16[128,1024]{1,0:T(8,128)(2,1)}, bf16[128,1024]{1,0:T(8,128)(2,1)S(1)}, u32[]{:S(2)}, u32[]{:S(2)}) collective-permute-start(bf16[128,1024]{1,0:T(8,128)(2,1)} %get-tuple-element.39), channel_id=1, source_target_pairs={{0,24},{1,25},{2,26},{3,27},{4,28},{5,29},{6,30},{7,31},{8,16},{9,... | collective-permute-start | bytes 786440 | tf_op jit(solution)/shard_map/ppermute | solution.py:48
  56.4 6.3 %collective-permute-start.22 = (bf16[128,1536]{1,0:T(8,128)(2,1)}, bf16[128,1536]{1,0:T(8,128)(2,1)S(1)}, u32[]{:S(2)}, u32[]{:S(2)}) collective-permute-start(bf16[128,1536]{1,0:T(8,128)(2,1)} %get-tuple-element.49.share), channel_id=1, source_target_pairs={{0,1},{1,0},{2,3},{3,2},{4,5},{5,4},{6,7},{7,6},{8,9},{9,8},{10,11... | collective-permute-start | bytes 1179656 | tf_op jit(solution)/shard_map/ppermute | solution.py:48
  56.4 11.8 %collective-permute-start.17 = (bf16[128,1024]{1,0:T(8,128)(2,1)}, bf16[128,1024]{1,0:T(8,128)(2,1)S(1)}, u32[]{:S(2)}, u32[]{:S(2)}) collective-permute-start(bf16[128,1024]{1,0:T(8,128)(2,1)} %get-tuple-element.47.refs_0_), channel_id=1, source_target_pairs={{0,24},{1,25},{2,26},{3,27},{4,28},{5,29},{6,30},{7,31},{8,16},{9,... | collective-permute-start | bytes 786440 | tf_op jit(solution)/shard_map/ppermute | solution.py:48
  58.9 25.1 %collective-permute-start.16 = (bf16[128,1024]{1,0:T(8,128)(2,1)}, bf16[128,1024]{1,0:T(8,128)(2,1)S(1)}, u32[]{:S(2)}, u32[]{:S(2)}) collective-permute-start(bf16[128,1024]{1,0:T(8,128)(2,1)} %get-tuple-element.47.refs_0_), channel_id=1, source_target_pairs={{0,16},{1,17},{2,18},{3,19},{4,20},{5,21},{6,22},{7,23},{8,24},{9,... | collective-permute-start | bytes 786440 | tf_op jit(solution)/shard_map/ppermute | solution.py:48
  62.6 21.5 %collective-permute-start.15 = (bf16[128,1024]{1,0:T(8,128)(2,1)}, bf16[128,1024]{1,0:T(8,128)(2,1)S(1)}, u32[]{:S(2)}, u32[]{:S(2)}) collective-permute-start(bf16[128,1024]{1,0:T(8,128)(2,1)} %get-tuple-element.47.refs_0_), channel_id=1, source_target_pairs={{0,8},{1,9},{2,10},{3,11},{4,12},{5,13},{6,14},{7,15},{8,0},{9,1},... | collective-permute-start | bytes 786440 | tf_op jit(solution)/shard_map/ppermute | solution.py:48
  66.0 18.5 %collective-permute-start.23 = (bf16[4,128,256]{2,1,0:T(8,128)(2,1)}, bf16[4,128,256]{2,1,0:T(8,128)(2,1)S(1)}, u32[]{:S(2)}, u32[]{:S(2)}) collective-permute-start(bf16[4,128,256]{2,1,0:T(8,128)(2,1)} %get-tuple-element.51), channel_id=1, source_target_pairs={{0,2},{1,3},{2,0},{3,1},{4,6},{5,7},{6,4},{7,5},{8,10},{9,11},{10,... | collective-permute-start | bytes 786440 | tf_op jit(solution)/shard_map/ppermute | solution.py:48
  66.7 17.8 %collective-permute-start.24 = (bf16[4,128,256]{2,1,0:T(8,128)(2,1)}, bf16[4,128,256]{2,1,0:T(8,128)(2,1)S(1)}, u32[]{:S(2)}, u32[]{:S(2)}) collective-permute-start(bf16[4,128,256]{2,1,0:T(8,128)(2,1)} %get-tuple-element.52), channel_id=1, source_target_pairs={{0,4},{1,5},{2,6},{3,7},{4,0},{5,1},{6,2},{7,3},{8,12},{9,13},{10,... | collective-permute-start | bytes 786440 | tf_op jit(solution)/shard_map/ppermute | solution.py:48
  68.2 16.8 %collective-permute-start.25 = (bf16[4,128,256]{2,1,0:T(8,128)(2,1)}, bf16[4,128,256]{2,1,0:T(8,128)(2,1)S(1)}, u32[]{:S(2)}, u32[]{:S(2)}) collective-permute-start(bf16[4,128,256]{2,1,0:T(8,128)(2,1)} %get-tuple-element.53), channel_id=1, source_target_pairs={{0,6},{1,7},{2,4},{3,5},{4,2},{5,3},{6,0},{7,1},{8,14},{9,15},{10,... | collective-permute-start | bytes 786440 | tf_op jit(solution)/shard_map/ppermute | solution.py:48
  84.0 5.5 %collective-permute-start.18 = (bf16[128,1024]{1,0:T(8,128)(2,1)}, bf16[128,1024]{1,0:T(8,128)(2,1)S(1)}, u32[]{:S(2)}, u32[]{:S(2)}) collective-permute-start(bf16[128,1024]{1,0:T(8,128)(2,1)} %get-tuple-element.47.refs_0_), channel_id=1, source_target_pairs={{0,1},{1,0},{2,3},{3,2},{4,5},{5,4},{6,7},{7,6},{8,9},{9,8},{10,11... | collective-permute-start | bytes 786440 | tf_op jit(solution)/shard_map/ppermute | solution.py:48
  84.0 7.9 %collective-permute-start.21 = (bf16[128,1024]{1,0:T(8,128)(2,1)S(1)}, bf16[128,1024]{1,0:T(8,128)(2,1)S(1)}, u32[]{:S(2)}, u32[]{:S(2)}) collective-permute-start(bf16[128,1024]{1,0:T(8,128)(2,1)S(1)} %collective-permute-done.17.refs_3_), channel_id=1, source_target_pairs={{0,1},{1,0},{2,3},{3,2},{4,5},{5,4},{6,7},{7,6},{8,9},{9,8},{10,11... | collective-permute-start | bytes 786440 | tf_op jit(solution)/shard_map/ppermute | solution.py:48
  84.5 7.5 %collective-permute-start.20 = (bf16[128,1024]{1,0:T(8,128)(2,1)S(1)}, bf16[128,1024]{1,0:T(8,128)(2,1)S(1)}, u32[]{:S(2)}, u32[]{:S(2)}) collective-permute-start(bf16[128,1024]{1,0:T(8,128)(2,1)S(1)} %collective-permute-done.16.refs_2_), channel_id=1, source_target_pairs={{0,1},{1,0},{2,3},{3,2},{4,5},{5,4},{6,7},{7,6},{8,9},{9,8},{10,11... | collective-permute-start | bytes 786440 | tf_op jit(solution)/shard_map/ppermute | solution.py:48
  84.6 7.4 %collective-permute-start.19 = (bf16[128,1024]{1,0:T(8,128)(2,1)S(1)}, bf16[128,1024]{1,0:T(8,128)(2,1)S(1)}, u32[]{:S(2)}, u32[]{:S(2)}) collective-permute-start(bf16[128,1024]{1,0:T(8,128)(2,1)S(1)} %collective-permute-done.15.refs_1_), channel_id=1, source_target_pairs={{0,1},{1,0},{2,3},{3,2},{4,5},{5,4},{6,7},{7,6},{8,9},{9,8},{10,11... | collective-permute-start | bytes 786440 | tf_op jit(solution)/shard_map/ppermute | solution.py:48
  86.1 15.0 %collective-permute-start.26 = (bf16[128,256]{1,0:T(8,128)(2,1)S(1)}, bf16[128,256]{1,0:T(8,128)(2,1)S(1)}, u32[]{:S(2)}, u32[]{:S(2)}) collective-permute-start(bf16[128,256]{1,0:T(8,128)(2,1)S(1)} %get-tuple-element.57), channel_id=1, source_target_pairs={{0,8},{1,9},{2,10},{3,11},{4,12},{5,13},{6,14},{7,15},{8,0},{9,1},... | collective-permute-start | bytes 196616 | tf_op jit(solution)/shard_map/ppermute | solution.py:48
  89.5 11.6 %collective-permute-start.28 = (bf16[128,256]{1,0:T(8,128)(2,1)S(1)}, bf16[128,256]{1,0:T(8,128)(2,1)S(1)}, u32[]{:S(2)}, u32[]{:S(2)}) collective-permute-start(bf16[128,256]{1,0:T(8,128)(2,1)S(1)} %get-tuple-element.58), channel_id=1, source_target_pairs={{0,24},{1,25},{2,26},{3,27},{4,28},{5,29},{6,30},{7,31},{8,16},{9,... | collective-permute-start | bytes 196616 | tf_op jit(solution)/shard_map/ppermute | solution.py:48
  92.0 9.1 %collective-permute-start.27 = (bf16[128,256]{1,0:T(8,128)(2,1)S(1)}, bf16[128,256]{1,0:T(8,128)(2,1)S(1)}, u32[]{:S(2)}, u32[]{:S(2)}) collective-permute-start(bf16[128,256]{1,0:T(8,128)(2,1)S(1)} %get-tuple-element.59), channel_id=1, source_target_pairs={{0,16},{1,17},{2,18},{3,19},{4,20},{5,21},{6,22},{7,23},{8,24},{9,... | collective-permute-start | bytes 196616 | tf_op jit(solution)/shard_map/ppermute | solution.py:48
  97.6 28.0 %all-to-all-start = ((bf16[4,128,1024]{2,1,0:T(8,128)(2,1)}), bf16[4,128,1024]{2,1,0:T(8,128)(2,1)S(1)}, u32[]{:S(2)}, u32[]{:S(2)}) async-start(bf16[4,128,1024]{2,1,0:T(8,128)(2,1)} %bitcast.20), calls=%async_computation | async-start | bytes 2097152 | tf_op jit(solution)/shard_map/all_to_all | solution.py:56
  101.2 6.6 %collective-permute-start.31 = (bf16[128,256]{1,0:T(8,128)(2,1)S(1)}, bf16[128,256]{1,0:T(8,128)(2,1)S(1)}, u32[]{:S(2)}, u32[]{:S(2)}) collective-permute-start(bf16[128,256]{1,0:T(8,128)(2,1)S(1)} %fusion.3), channel_id=1, source_target_pairs={{0,24},{1,25},{2,26},{3,27},{4,28},{5,29},{6,30},{7,31},{8,16},{9,... | collective-permute-start | bytes 196616 | tf_op jit(solution)/shard_map/ppermute | solution.py:48
  102.7 5.8 %collective-permute-start.30 = (bf16[128,256]{1,0:T(8,128)(2,1)S(1)}, bf16[128,256]{1,0:T(8,128)(2,1)S(1)}, u32[]{:S(2)}, u32[]{:S(2)}) collective-permute-start(bf16[128,256]{1,0:T(8,128)(2,1)S(1)} %fusion.3), channel_id=1, source_target_pairs={{0,16},{1,17},{2,18},{3,19},{4,20},{5,21},{6,22},{7,23},{8,24},{9,... | collective-permute-start | bytes 196616 | tf_op jit(solution)/shard_map/ppermute | solution.py:48
  109.2 13.4 %collective-permute-start.34 = (bf16[4,128,256]{2,1,0:T(8,128)(2,1)S(1)}, bf16[4,128,256]{2,1,0:T(8,128)(2,1)S(1)}, u32[]{:S(2)}, u32[]{:S(2)}) collective-permute-start(bf16[4,128,256]{2,1,0:T(8,128)(2,1)S(1)} %pad_maximum_fusion.refs_0_), channel_id=1, source_target_pairs={{0,6},{1,7},{2,4},{3,5},{4,2},{5,3},{6,0},{7,1},{8,14},{9,15},{10,... | collective-permute-start | bytes 786440 | tf_op jit(solution)/shard_map/ppermute | solution.py:48
  111.9 13.1 %collective-permute-start.33 = (bf16[4,128,256]{2,1,0:T(8,128)(2,1)S(1)}, bf16[4,128,256]{2,1,0:T(8,128)(2,1)S(1)}, u32[]{:S(2)}, u32[]{:S(2)}) collective-permute-start(bf16[4,128,256]{2,1,0:T(8,128)(2,1)S(1)} %pad_maximum_fusion.refs_0_), channel_id=1, source_target_pairs={{0,4},{1,5},{2,6},{3,7},{4,0},{5,1},{6,2},{7,3},{8,12},{9,13},{10,... | collective-permute-start | bytes 786440 | tf_op jit(solution)/shard_map/ppermute | solution.py:48
  112.4 12.6 %collective-permute-start.32 = (bf16[4,128,256]{2,1,0:T(8,128)(2,1)S(1)}, bf16[4,128,256]{2,1,0:T(8,128)(2,1)S(1)}, u32[]{:S(2)}, u32[]{:S(2)}) collective-permute-start(bf16[4,128,256]{2,1,0:T(8,128)(2,1)S(1)} %pad_maximum_fusion.refs_0_), channel_id=1, source_target_pairs={{0,2},{1,3},{2,0},{3,1},{4,6},{5,7},{6,4},{7,5},{8,10},{9,11},{10,... | collective-permute-start | bytes 786440 | tf_op jit(solution)/shard_map/ppermute | solution.py:48
  (40 other events, 191.1 us)

commit v4 on v3

--- a/solution.py
+++ b/solution.py
@@ -9,7 +9,7 @@
 
 BF16 = jnp.bfloat16
 F32 = jnp.float32
-VMEM_LIMIT = 56 * 2**20
+VMEM_LIMIT = 64 * 2**20 - 2**18
 SMEM_SPEC = pl.BlockSpec(memory_space=pltpu.SMEM)
 VMEM_SPEC = pl.BlockSpec(memory_space=pltpu.VMEM)
 HBM_SPEC = pl.BlockSpec(memory_space=pl.ANY)

time: 132 us -> 130 us (0.985)
  local copies, waits for them, and re-layouts: 7.03 us -> 4.3 us
    unnamed x64 -> x34, local copies, waits for them, and re-layouts: 7.02 us -> 3.63 us
  transfers between devices with their start and end apart: 40 -> 40, of which waited for: 14 -> 12; matrix products, arithmetic and copies ran while one was open for 2% -> 3% of each run, Pallas kernels for 8% -> 8%
where the time goes in v4:
time: 130 us
  waiting for transfers between devices  55 us (42%)
  starting transfers between devices  43.4 us (33%)
  Pallas kernels  21.1 us (16%)
  other arithmetic  4.44 us (3%)
  local copies, waits for them, and re-layouts  4.3 us (3%)
  between operations  1.48 us (1%)
    ppermute x39, waiting for transfers between devices, move(): return lax.ppermute(value, ('row', 'col'), pairs)  55 us
    ppermute x39, starting transfers between devices, move(): return lax.ppermute(value, ('row', 'col'), pairs)  39.9 us
    pallas_call x1, Pallas kernels, forward(): pl.pallas_call(functools.partial(forward_kernel, g, slots, block, n), out...  4.18 us
    pallas_call x1, Pallas kernels, backward(): pl.pallas_call(functools.partial(backward_kernel, g, block, [len(group) f...  4.1 us
    pallas_call x1, Pallas kernels, layer(): pl.pallas_call(functools.partial(layer_kernel, g, len(parts)), out_shape=...  3.91 us
    unnamed x34, local copies, waits for them, and re-layouts  3.63 us
    all_to_all x1, starting transfers between devices, swap_xy(): lax.all_to_all(value, ('row', 'col'), 0, 0, axis_index_groups=groups, til...  3.51 us
    pallas_call x1, Pallas kernels, build(): pl.pallas_call(functools.partial(build_kernel, g, slots, block), out_shap...  3.25 us
  transfers between devices with their start and end apart: 40, of which 12 were waited for; matrix products, arithmetic and copies ran while one was open for 3% of the time, Pallas kernels for 8%

profile of v4, /device:TPU:0, one launch (start us, length us, event | category | flops | bytes accessed | tf_op | source)
XLA Modules:
  0.0 129.7 jit_solution(13589637370301467532)
XLA Ops:
  2.0 2.9 %collective-permute-start.2 = (bf16[128,1024]{1,0:T(8,128)(2,1)}, bf16[128,1024]{1,0:T(8,128)(2,1)S(1)}, u32[]{:S(2)}, u32[]{:S(2)}) collective-permute-start(bf16[128,1024]{1,0:T(8,128)(2,1)} %refs_4_.1), channel_id=1, source_target_pairs={{0,4},{1,5},{2,6},{3,7},{4,0},{5,1},{6,2},{7,3},{8,12},{9,13},{10,... | collective-permute-start | bytes 786440 | tf_op jit(solution)/shard_map/ppermute | solution.py:48
  5.1 2.0 %collective-permute-start.6 = (bf16[128,1024]{1,0:T(8,128)(2,1)}, bf16[128,1024]{1,0:T(8,128)(2,1)S(1)}, u32[]{:S(2)}, u32[]{:S(2)}) collective-permute-start(bf16[128,1024]{1,0:T(8,128)(2,1)} %refs_4_.1), channel_id=1, source_target_pairs={{0,2},{1,3},{2,0},{3,1},{4,6},{5,7},{6,4},{7,5},{8,10},{9,11},{10,... | collective-permute-start | bytes 786440 | tf_op jit(solution)/shard_map/ppermute | solution.py:48
  7.0 4.5 %collective-permute-done.refs_1_ = s32[17]{0:T(128)S(1)} collective-permute-done((s32[17]{0:T(128)S(1)}, s32[17]{0:T(128)S(1)}, u32[]{:S(2)}, u32[]{:S(2)}) %collective-permute-start) | collective-permute-done | bytes 100 | tf_op jit(solution)/shard_map/ppermute | solution.py:48
  11.6 1.8 %collective-permute-start.9 = (bf16[128,1024]{1,0:T(8,128)(2,1)S(1)}, bf16[128,1024]{1,0:T(8,128)(2,1)S(1)}, u32[]{:S(2)}, u32[]{:S(2)}) collective-permute-start(bf16[128,1024]{1,0:T(8,128)(2,1)S(1)} %collective-permute-done.2.refs_8_), channel_id=1, source_target_pairs={{0,2},{1,3},{2,0},{3,1},{4,6},{5,7},{6,4},{7,5},{8,10},{9,11},{10,... | collective-permute-start | bytes 786440 | tf_op jit(solution)/shard_map/ppermute | solution.py:48
  13.5 1.5 %collective-permute-start.1 = (bf16[8,128,128]{2,1,0:T(8,128)(2,1)}, bf16[8,128,128]{2,1,0:T(8,128)(2,1)}, u32[]{:S(2)}, u32[]{:S(2)}) collective-permute-start(bf16[8,128,128]{2,1,0:T(8,128)(2,1)} %bitcast.22), channel_id=1, source_target_pairs={{0,4},{1,5},{2,6},{3,7},{4,0},{5,1},{6,2},{7,3},{8,12},{9,13},{10,... | collective-permute-start | bytes 786440 | tf_op jit(solution)/shard_map/ppermute | solution.py:48
  15.7 1.1 collective-permute-done.4.refs_2_
  17.6 2.8 %collective-permute-done.9.refs_10_ = bf16[128,1024]{1,0:T(8,128)(2,1)S(1)} collective-permute-done((bf16[128,1024]{1,0:T(8,128)(2,1)S(1)}, bf16[128,1024]{1,0:T(8,128)(2,1)S(1)}, u32[]{:S(2)}, u32[]{:S(2)}) %collective-permute-start.9) | collective-permute-done | bytes 262176 | tf_op jit(solution)/shard_map/ppermute | solution.py:48
  20.4 1.8 %collective-permute-done.1.refs_3_.refs_4_ = bf16[8,128,128]{2,1,0:T(8,128)(2,1)} collective-permute-done((bf16[8,128,128]{2,1,0:T(8,128)(2,1)}, bf16[8,128,128]{2,1,0:T(8,128)(2,1)}, u32[]{:S(2)}, u32[]{:S(2)}) %collective-permute-start.1) | collective-permute-done | bytes 262176 | tf_op jit(solution)/shard_map/ppermute | solution.py:48
  23.7 4.2 %forward.1 = (bf16[128,1024]{1,0:T(8,128)(2,1)}, bf16[128,1024]{1,0:T(8,128)(2,1)}, bf16[128,1024]{1,0:T(8,128)(2,1)}, bf16[128,1024]{1,0:T(8,128)(2,1)}) custom-call(s32[17]{0:T(128)} %copy-done.15, s32[17]{0:T(128)} %copy-done.14, bf16[8,128,128]{2,1,0:T(8,128)(2,1)} %bitcast.23, bf16[8,128,128]{2,1,0:T(8,128)(2,1)} %collective-permute-done.1.refs_3_.refs_4_, ...), custom_call_target="tpu_custom_call" | custom-call | tf_op jit(solution)/shard_map/forward/pallas_call | solution.py:140
  27.9 1.6 %collective-permute-start.11 = (bf16[128,1024]{1,0:T(8,128)(2,1)}, bf16[128,1024]{1,0:T(8,128)(2,1)}, u32[]{:S(2)}, u32[]{:S(2)}) collective-permute-start(bf16[128,1024]{1,0:T(8,128)(2,1)} %get-tuple-element.37), channel_id=1, source_target_pairs={{0,8},{1,9},{2,10},{3,11},{4,12},{5,13},{6,14},{7,15},{8,0},{9,1},... | collective-permute-start | bytes 786440 | tf_op jit(solution)/shard_map/ppermute | solution.py:48
  29.5 2.6 %collective-permute-start.12 = (bf16[128,1024]{1,0:T(8,128)(2,1)}, bf16[128,1024]{1,0:T(8,128)(2,1)}, u32[]{:S(2)}, u32[]{:S(2)}) collective-permute-start(bf16[128,1024]{1,0:T(8,128)(2,1)} %get-tuple-element.38), channel_id=1, source_target_pairs={{0,16},{1,17},{2,18},{3,19},{4,20},{5,21},{6,22},{7,23},{8,24},{9,... | collective-permute-start | bytes 786440 | tf_op jit(solution)/shard_map/ppermute | solution.py:48
  32.3 3.2 %build.1.matrix = bf16[512,1024]{1,0:T(8,128)(2,1)} custom-call(s32[17]{0:T(128)} %copy-done.15, s32[17]{0:T(128)} %copy-done.14, s32[34]{0:T(128)} %copy-done.16, bf16[8,128,128]{2,1,0:T(8,128)(2,1)} %bitcast.24, bf16[8,128,128]{2,1,0:T(8,128)(2,1)} %collective-permute-done.1.refs_3_.refs_4_, bf16[8,128,128]{2,1,0:T(8,128)(2,1)} %collective-permute-done.3.refs_5_, ...), custom_call_target="tpu_custom_call" | custom-call | tf_op jit(solution)/shard_map/build/pallas_call | solution.py:174
  35.6 6.5 %collective-permute-done.11.refs_1_ = bf16[128,1024]{1,0:T(8,128)(2,1)} collective-permute-done((bf16[128,1024]{1,0:T(8,128)(2,1)}, bf16[128,1024]{1,0:T(8,128)(2,1)}, u32[]{:S(2)}, u32[]{:S(2)}) %collective-permute-start.11) | collective-permute-done | bytes 262176 | tf_op jit(solution)/shard_map/ppermute | solution.py:48
  42.1 9.1 %collective-permute-done.12.refs_2_ = bf16[128,1024]{1,0:T(8,128)(2,1)} collective-permute-done((bf16[128,1024]{1,0:T(8,128)(2,1)}, bf16[128,1024]{1,0:T(8,128)(2,1)}, u32[]{:S(2)}, u32[]{:S(2)}) %collective-permute-start.12) | collective-permute-done | bytes 262176 | tf_op jit(solution)/shard_map/ppermute | solution.py:48
  51.2 3.9 %layer.1 = (bf16[128,1024]{1,0:T(8,128)(2,1)}, bf16[128,1536]{1,0:T(8,128)(2,1)}, bf16[128,1024]{1,0:T(8,128)(2,1)}, bf16[128,512]{1,0:T(8,128)(2,1)}) custom-call(bf16[128,1024]{1,0:T(8,128)(2,1)} %get-tuple-element.41.refs_0_, bf16[128,1024]{1,0:T(8,128)(2,1)} %collective-permute-done.11.refs_1_, bf16[128,1024]{1,0:T(8,128)(2,1)} %collective-permute-done.12.refs_2_, ...), custom_call_target="tpu_custom_call" | custom-call | tf_op jit(solution)/shard_map/layer/pallas_call | solution.py:252
  55.1 2.5 %collective-permute-start.17 = (bf16[128,1024]{1,0:T(8,128)(2,1)}, bf16[128,1024]{1,0:T(8,128)(2,1)}, u32[]{:S(2)}, u32[]{:S(2)}) collective-permute-start(bf16[128,1024]{1,0:T(8,128)(2,1)} %get-tuple-element.47.refs_0_), channel_id=1, source_target_pairs={{0,24},{1,25},{2,26},{3,27},{4,28},{5,29},{6,30},{7,31},{8,16},{9,... | collective-permute-start | bytes 786440 | tf_op jit(solution)/shard_map/ppermute | solution.py:48
  57.6 4.4 %collective-permute-start.16 = (bf16[128,1024]{1,0:T(8,128)(2,1)}, bf16[128,1024]{1,0:T(8,128)(2,1)}, u32[]{:S(2)}, u32[]{:S(2)}) collective-permute-start(bf16[128,1024]{1,0:T(8,128)(2,1)} %get-tuple-element.47.refs_0_), channel_id=1, source_target_pairs={{0,16},{1,17},{2,18},{3,19},{4,20},{5,21},{6,22},{7,23},{8,24},{9,... | collective-permute-start | bytes 786440 | tf_op jit(solution)/shard_map/ppermute | solution.py:48
  62.1 2.5 %terms.1 = (bf16[4,128,256]{2,1,0:T(8,128)(2,1)}, bf16[4,128,256]{2,1,0:T(8,128)(2,1)}, bf16[4,128,256]{2,1,0:T(8,128)(2,1)}, bf16[4,128,256]{2,1,0:T(8,128)(2,1)}) custom-call(bf16[128,512]{1,0:T(8,128)(2,1)} %get-tuple-element.48.keep, bf16[128,1536]{1,0:T(8,128)(2,1)} %get-tuple-element.49.share, bf16[128,1536]{1,0:T(8,128)(2,1)} %collective-permute-done.22.share_got), custom_call_target="tpu_custom_call" | custom-call | tf_op jit(solution)/shard_map/terms/pallas_call | solution.py:294
  65.1 1.5 %collective-permute-start.24 = (bf16[4,128,256]{2,1,0:T(8,128)(2,1)}, bf16[4,128,256]{2,1,0:T(8,128)(2,1)S(1)}, u32[]{:S(2)}, u32[]{:S(2)}) collective-permute-start(bf16[4,128,256]{2,1,0:T(8,128)(2,1)} %get-tuple-element.52), channel_id=1, source_target_pairs={{0,4},{1,5},{2,6},{3,7},{4,0},{5,1},{6,2},{7,3},{8,12},{9,13},{10,... | collective-permute-start | bytes 786440 | tf_op jit(solution)/shard_map/ppermute | solution.py:48
  66.6 1.5 %collective-permute-start.25 = (bf16[4,128,256]{2,1,0:T(8,128)(2,1)}, bf16[4,128,256]{2,1,0:T(8,128)(2,1)S(1)}, u32[]{:S(2)}, u32[]{:S(2)}) collective-permute-start(bf16[4,128,256]{2,1,0:T(8,128)(2,1)} %get-tuple-element.53), channel_id=1, source_target_pairs={{0,6},{1,7},{2,4},{3,5},{4,2},{5,3},{6,0},{7,1},{8,14},{9,15},{10,... | collective-permute-start | bytes 786440 | tf_op jit(solution)/shard_map/ppermute | solution.py:48
  68.1 14.6 %collective-permute-done.16.refs_2_ = bf16[128,1024]{1,0:T(8,128)(2,1)} collective-permute-done((bf16[128,1024]{1,0:T(8,128)(2,1)}, bf16[128,1024]{1,0:T(8,128)(2,1)}, u32[]{:S(2)}, u32[]{:S(2)}) %collective-permute-start.16) | collective-permute-done | bytes 262176 | tf_op jit(solution)/shard_map/ppermute | solution.py:48
  86.3 3.3 %collective-permute-start.26 = (bf16[128,256]{1,0:T(8,128)(2,1)}, bf16[128,256]{1,0:T(8,128)(2,1)S(1)}, u32[]{:S(2)}, u32[]{:S(2)}) collective-permute-start(bf16[128,256]{1,0:T(8,128)(2,1)} %get-tuple-element.57), channel_id=1, source_target_pairs={{0,8},{1,9},{2,10},{3,11},{4,12},{5,13},{6,14},{7,15},{8,0},{9,1},... | collective-permute-start | bytes 196616 | tf_op jit(solution)/shard_map/ppermute | solution.py:48
  89.6 2.5 %collective-permute-start.28 = (bf16[128,256]{1,0:T(8,128)(2,1)}, bf16[128,256]{1,0:T(8,128)(2,1)S(1)}, u32[]{:S(2)}, u32[]{:S(2)}) collective-permute-start(bf16[128,256]{1,0:T(8,128)(2,1)} %get-tuple-element.58), channel_id=1, source_target_pairs={{0,24},{1,25},{2,26},{3,27},{4,28},{5,29},{6,30},{7,31},{8,16},{9,... | collective-permute-start | bytes 196616 | tf_op jit(solution)/shard_map/ppermute | solution.py:48
  92.1 4.1 %backward.1 = bf16[512,1024]{1,0:T(8,128)(2,1)} custom-call(bf16[512,1024]{1,0:T(8,128)(2,1)} %build.1.matrix, bf16[128,1024]{1,0:T(8,128)(2,1)} %get-tuple-element.47.refs_0_, bf16[128,1024]{1,0:T(8,128)(2,1)} %collective-permute-done.15.refs_1_, bf16[128,1024]{1,0:T(8,128)(2,1)} %collective-permute-done.16.refs_2_, ...), custom_call_target="tpu_custom_call" | custom-call | tf_op jit(solution)/shard_map/backward/pallas_call | solution.py:202
  96.2 3.5 %all-to-all-start = ((bf16[4,128,1024]{2,1,0:T(8,128)(2,1)}), bf16[4,128,1024]{2,1,0:T(8,128)(2,1)S(1)}, u32[]{:S(2)}, u32[]{:S(2)}) async-start(bf16[4,128,1024]{2,1,0:T(8,128)(2,1)} %bitcast.20), calls=%async_computation | async-start | bytes 2097152 | tf_op jit(solution)/shard_map/all_to_all | solution.py:56
  100.7 1.6 %collective-permute-start.31 = (bf16[128,256]{1,0:T(8,128)(2,1)S(1)}, bf16[128,256]{1,0:T(8,128)(2,1)S(1)}, u32[]{:S(2)}, u32[]{:S(2)}) collective-permute-start(bf16[128,256]{1,0:T(8,128)(2,1)S(1)} %fusion.3), channel_id=1, source_target_pairs={{0,24},{1,25},{2,26},{3,27},{4,28},{5,29},{6,30},{7,31},{8,16},{9,... | collective-permute-start | bytes 196616 | tf_op jit(solution)/shard_map/ppermute | solution.py:48
  102.2 1.8 %collective-permute-start.30 = (bf16[128,256]{1,0:T(8,128)(2,1)S(1)}, bf16[128,256]{1,0:T(8,128)(2,1)S(1)}, u32[]{:S(2)}, u32[]{:S(2)}) collective-permute-start(bf16[128,256]{1,0:T(8,128)(2,1)S(1)} %fusion.3), channel_id=1, source_target_pairs={{0,16},{1,17},{2,18},{3,19},{4,20},{5,21},{6,22},{7,23},{8,24},{9,... | collective-permute-start | bytes 196616 | tf_op jit(solution)/shard_map/ppermute | solution.py:48
  105.1 2.2 %collective-permute-done.31 = bf16[128,256]{1,0:T(8,128)(2,1)S(1)} collective-permute-done((bf16[128,256]{1,0:T(8,128)(2,1)S(1)}, bf16[128,256]{1,0:T(8,128)(2,1)S(1)}, u32[]{:S(2)}, u32[]{:S(2)}) %collective-permute-start.31) | collective-permute-done | bytes 65568 | tf_op jit(solution)/shard_map/ppermute | solution.py:48
  108.8 2.7 %collective-permute-start.34 = (bf16[4,128,256]{2,1,0:T(8,128)(2,1)S(1)}, bf16[4,128,256]{2,1,0:T(8,128)(2,1)S(1)}, u32[]{:S(2)}, u32[]{:S(2)}) collective-permute-start(bf16[4,128,256]{2,1,0:T(8,128)(2,1)S(1)} %pad_maximum_fusion.refs_0_), channel_id=1, source_target_pairs={{0,6},{1,7},{2,4},{3,5},{4,2},{5,3},{6,0},{7,1},{8,14},{9,15},{10,... | collective-permute-start | bytes 786440 | tf_op jit(solution)/shard_map/ppermute | solution.py:48
  112.3 9.0 %collective-permute-done.34.refs_3_ = bf16[4,128,256]{2,1,0:T(8,128)(2,1)S(1)} collective-permute-done((bf16[4,128,256]{2,1,0:T(8,128)(2,1)S(1)}, bf16[4,128,256]{2,1,0:T(8,128)(2,1)S(1)}, u32[]{:S(2)}, u32[]{:S(2)}) %collective-permute-start.34) | collective-permute-done | bytes 262176 | tf_op jit(solution)/shard_map/ppermute | solution.py:48
  121.8 1.8 %collective-permute-done.33.refs_2_ = bf16[4,128,256]{2,1,0:T(8,128)(2,1)S(1)} collective-permute-done((bf16[4,128,256]{2,1,0:T(8,128)(2,1)S(1)}, bf16[4,128,256]{2,1,0:T(8,128)(2,1)S(1)}, u32[]{:S(2)}, u32[]{:S(2)}) %collective-permute-start.33) | collective-permute-done | bytes 262176 | tf_op jit(solution)/shard_map/ppermute | solution.py:48
  126.6 3.1 %join.1 = f32[1024,1024]{1,0:T(8,128)} custom-call(bf16[4,128,256]{2,1,0:T(8,128)(2,1)} %copy-done.1, bf16[4,128,256]{2,1,0:T(8,128)(2,1)} %copy-done.7, bf16[4,128,256]{2,1,0:T(8,128)(2,1)} %copy-done.6, bf16[4,128,256]{2,1,0:T(8,128)(2,1)} %copy-done.5, bf16[4,128,256]{2,1,0:T(8,128)(2,1)} %copy-done.10, ...), custom_call_target="tpu_custom_call" | custom-call | tf_op jit(solution)/shard_map/join/pallas_call | solution.py:336
  (95 shorter events, 15.9 us)
Async XLA Ops:
  2.0 9.5 %collective-permute-start.2 = (bf16[128,1024]{1,0:T(8,128)(2,1)}, bf16[128,1024]{1,0:T(8,128)(2,1)S(1)}, u32[]{:S(2)}, u32[]{:S(2)}) collective-permute-start(bf16[128,1024]{1,0:T(8,128)(2,1)} %refs_4_.1), channel_id=1, source_target_pairs={{0,4},{1,5},{2,6},{3,7},{4,0},{5,1},{6,2},{7,3},{8,12},{9,13},{10,... | collective-permute-start | bytes 786440 | tf_op jit(solution)/shard_map/ppermute | solution.py:48
  5.0 6.6 %collective-permute-start = (s32[17]{0:T(128)S(1)}, s32[17]{0:T(128)S(1)}, u32[]{:S(2)}, u32[]{:S(2)}) collective-permute-start(s32[17]{0:T(128)S(1)} %pad_add_fusion.refs_0_), channel_id=1, source_target_pairs={{0,4},{1,5},{2,6},{3,7},{4,0},{5,1},{6,2},{7,3},{8,12},{9,13},{10,... | collective-permute-start | bytes 212 | tf_op jit(solution)/shard_map/ppermute | solution.py:48
  5.1 12.0 %collective-permute-start.6 = (bf16[128,1024]{1,0:T(8,128)(2,1)}, bf16[128,1024]{1,0:T(8,128)(2,1)S(1)}, u32[]{:S(2)}, u32[]{:S(2)}) collective-permute-start(bf16[128,1024]{1,0:T(8,128)(2,1)} %refs_4_.1), channel_id=1, source_target_pairs={{0,2},{1,3},{2,0},{3,1},{4,6},{5,7},{6,4},{7,5},{8,10},{9,11},{10,... | collective-permute-start | bytes 786440 | tf_op jit(solution)/shard_map/ppermute | solution.py:48
  11.6 5.8 %collective-permute-start.3 = (bf16[8,128,128]{2,1,0:T(8,128)(2,1)}, bf16[8,128,128]{2,1,0:T(8,128)(2,1)}, u32[]{:S(2)}, u32[]{:S(2)}) collective-permute-start(bf16[8,128,128]{2,1,0:T(8,128)(2,1)} %bitcast.21), channel_id=1, source_target_pairs={{0,1},{1,0},{2,3},{3,2},{4,5},{5,4},{6,7},{7,6},{8,9},{9,8},{10,11... | collective-permute-start | bytes 786440 | tf_op jit(solution)/shard_map/ppermute | solution.py:48
  11.6 8.7 %collective-permute-start.9 = (bf16[128,1024]{1,0:T(8,128)(2,1)S(1)}, bf16[128,1024]{1,0:T(8,128)(2,1)S(1)}, u32[]{:S(2)}, u32[]{:S(2)}) collective-permute-start(bf16[128,1024]{1,0:T(8,128)(2,1)S(1)} %collective-permute-done.2.refs_8_), channel_id=1, source_target_pairs={{0,2},{1,3},{2,0},{3,1},{4,6},{5,7},{6,4},{7,5},{8,10},{9,11},{10,... | collective-permute-start | bytes 786440 | tf_op jit(solution)/shard_map/ppermute | solution.py:48
  13.5 8.7 %collective-permute-start.1 = (bf16[8,128,128]{2,1,0:T(8,128)(2,1)}, bf16[8,128,128]{2,1,0:T(8,128)(2,1)}, u32[]{:S(2)}, u32[]{:S(2)}) collective-permute-start(bf16[8,128,128]{2,1,0:T(8,128)(2,1)} %bitcast.22), channel_id=1, source_target_pairs={{0,4},{1,5},{2,6},{3,7},{4,0},{5,1},{6,2},{7,3},{8,12},{9,13},{10,... | collective-permute-start | bytes 786440 | tf_op jit(solution)/shard_map/ppermute | solution.py:48
  16.8 5.3 %collective-permute-start.5 = (bf16[128,1024]{1,0:T(8,128)(2,1)}, bf16[128,1024]{1,0:T(8,128)(2,1)S(1)}, u32[]{:S(2)}, u32[]{:S(2)}) collective-permute-start(bf16[128,1024]{1,0:T(8,128)(2,1)} %refs_4_.1), channel_id=1, source_target_pairs={{0,1},{1,0},{2,3},{3,2},{4,5},{5,4},{6,7},{7,6},{8,9},{9,8},{10,11... | collective-permute-start | bytes 786440 | tf_op jit(solution)/shard_map/ppermute | solution.py:48
  17.1 5.1 %collective-permute-start.7 = (bf16[128,1024]{1,0:T(8,128)(2,1)S(1)}, bf16[128,1024]{1,0:T(8,128)(2,1)S(1)}, u32[]{:S(2)}, u32[]{:S(2)}) collective-permute-start(bf16[128,1024]{1,0:T(8,128)(2,1)S(1)} %collective-permute-done.6.refs_6_), channel_id=1, source_target_pairs={{0,1},{1,0},{2,3},{3,2},{4,5},{5,4},{6,7},{7,6},{8,9},{9,8},{10,11... | collective-permute-start | bytes 786440 | tf_op jit(solution)/shard_map/ppermute | solution.py:48
  17.4 4.8 %collective-permute-start.8 = (bf16[128,1024]{1,0:T(8,128)(2,1)S(1)}, bf16[128,1024]{1,0:T(8,128)(2,1)S(1)}, u32[]{:S(2)}, u32[]{:S(2)}) collective-permute-start(bf16[128,1024]{1,0:T(8,128)(2,1)S(1)} %collective-permute-done.2.refs_8_), channel_id=1, source_target_pairs={{0,1},{1,0},{2,3},{3,2},{4,5},{5,4},{6,7},{7,6},{8,9},{9,8},{10,11... | collective-permute-start | bytes 786440 | tf_op jit(solution)/shard_map/ppermute | solution.py:48
  27.9 14.2 %collective-permute-start.11 = (bf16[128,1024]{1,0:T(8,128)(2,1)}, bf16[128,1024]{1,0:T(8,128)(2,1)}, u32[]{:S(2)}, u32[]{:S(2)}) collective-permute-start(bf16[128,1024]{1,0:T(8,128)(2,1)} %get-tuple-element.37), channel_id=1, source_target_pairs={{0,8},{1,9},{2,10},{3,11},{4,12},{5,13},{6,14},{7,15},{8,0},{9,1},... | collective-permute-start | bytes 786440 | tf_op jit(solution)/shard_map/ppermute | solution.py:48
  29.5 21.6 %collective-permute-start.12 = (bf16[128,1024]{1,0:T(8,128)(2,1)}, bf16[128,1024]{1,0:T(8,128)(2,1)}, u32[]{:S(2)}, u32[]{:S(2)}) collective-permute-start(bf16[128,1024]{1,0:T(8,128)(2,1)} %get-tuple-element.38), channel_id=1, source_target_pairs={{0,16},{1,17},{2,18},{3,19},{4,20},{5,21},{6,22},{7,23},{8,24},{9,... | collective-permute-start | bytes 786440 | tf_op jit(solution)/shard_map/ppermute | solution.py:48
  32.1 19.0 %collective-permute-start.13 = (bf16[128,1024]{1,0:T(8,128)(2,1)}, bf16[128,1024]{1,0:T(8,128)(2,1)}, u32[]{:S(2)}, u32[]{:S(2)}) collective-permute-start(bf16[128,1024]{1,0:T(8,128)(2,1)} %get-tuple-element.39), channel_id=1, source_target_pairs={{0,24},{1,25},{2,26},{3,27},{4,28},{5,29},{6,30},{7,31},{8,16},{9,... | collective-permute-start | bytes 786440 | tf_op jit(solution)/shard_map/ppermute | solution.py:48
  55.1 7.0 %collective-permute-start.22 = (bf16[128,1536]{1,0:T(8,128)(2,1)}, bf16[128,1536]{1,0:T(8,128)(2,1)}, u32[]{:S(2)}, u32[]{:S(2)}) collective-permute-start(bf16[128,1536]{1,0:T(8,128)(2,1)} %get-tuple-element.49.share), channel_id=1, source_target_pairs={{0,1},{1,0},{2,3},{3,2},{4,5},{5,4},{6,7},{7,6},{8,9},{9,8},{10,11... | collective-permute-start | bytes 1179656 | tf_op jit(solution)/shard_map/ppermute | solution.py:48
  55.1 11.5 %collective-permute-start.17 = (bf16[128,1024]{1,0:T(8,128)(2,1)}, bf16[128,1024]{1,0:T(8,128)(2,1)}, u32[]{:S(2)}, u32[]{:S(2)}) collective-permute-start(bf16[128,1024]{1,0:T(8,128)(2,1)} %get-tuple-element.47.refs_0_), channel_id=1, source_target_pairs={{0,24},{1,25},{2,26},{3,27},{4,28},{5,29},{6,30},{7,31},{8,16},{9,... | collective-permute-start | bytes 786440 | tf_op jit(solution)/shard_map/ppermute | solution.py:48
  57.6 25.2 %collective-permute-start.16 = (bf16[128,1024]{1,0:T(8,128)(2,1)}, bf16[128,1024]{1,0:T(8,128)(2,1)}, u32[]{:S(2)}, u32[]{:S(2)}) collective-permute-start(bf16[128,1024]{1,0:T(8,128)(2,1)} %get-tuple-element.47.refs_0_), channel_id=1, source_target_pairs={{0,16},{1,17},{2,18},{3,19},{4,20},{5,21},{6,22},{7,23},{8,24},{9,... | collective-permute-start | bytes 786440 | tf_op jit(solution)/shard_map/ppermute | solution.py:48
  62.0 20.9 %collective-permute-start.15 = (bf16[128,1024]{1,0:T(8,128)(2,1)}, bf16[128,1024]{1,0:T(8,128)(2,1)}, u32[]{:S(2)}, u32[]{:S(2)}) collective-permute-start(bf16[128,1024]{1,0:T(8,128)(2,1)} %get-tuple-element.47.refs_0_), channel_id=1, source_target_pairs={{0,8},{1,9},{2,10},{3,11},{4,12},{5,13},{6,14},{7,15},{8,0},{9,1},... | collective-permute-start | bytes 786440 | tf_op jit(solution)/shard_map/ppermute | solution.py:48
  64.6 18.7 %collective-permute-start.23 = (bf16[4,128,256]{2,1,0:T(8,128)(2,1)}, bf16[4,128,256]{2,1,0:T(8,128)(2,1)S(1)}, u32[]{:S(2)}, u32[]{:S(2)}) collective-permute-start(bf16[4,128,256]{2,1,0:T(8,128)(2,1)} %get-tuple-element.51), channel_id=1, source_target_pairs={{0,2},{1,3},{2,0},{3,1},{4,6},{5,7},{6,4},{7,5},{8,10},{9,11},{10,... | collective-permute-start | bytes 786440 | tf_op jit(solution)/shard_map/ppermute | solution.py:48
  65.1 18.2 %collective-permute-start.24 = (bf16[4,128,256]{2,1,0:T(8,128)(2,1)}, bf16[4,128,256]{2,1,0:T(8,128)(2,1)S(1)}, u32[]{:S(2)}, u32[]{:S(2)}) collective-permute-start(bf16[4,128,256]{2,1,0:T(8,128)(2,1)} %get-tuple-element.52), channel_id=1, source_target_pairs={{0,4},{1,5},{2,6},{3,7},{4,0},{5,1},{6,2},{7,3},{8,12},{9,13},{10,... | collective-permute-start | bytes 786440 | tf_op jit(solution)/shard_map/ppermute | solution.py:48
  66.6 17.2 %collective-permute-start.25 = (bf16[4,128,256]{2,1,0:T(8,128)(2,1)}, bf16[4,128,256]{2,1,0:T(8,128)(2,1)S(1)}, u32[]{:S(2)}, u32[]{:S(2)}) collective-permute-start(bf16[4,128,256]{2,1,0:T(8,128)(2,1)} %get-tuple-element.53), channel_id=1, source_target_pairs={{0,6},{1,7},{2,4},{3,5},{4,2},{5,3},{6,0},{7,1},{8,14},{9,15},{10,... | collective-permute-start | bytes 786440 | tf_op jit(solution)/shard_map/ppermute | solution.py:48
  82.8 6.8 %collective-permute-start.18 = (bf16[128,1024]{1,0:T(8,128)(2,1)}, bf16[128,1024]{1,0:T(8,128)(2,1)}, u32[]{:S(2)}, u32[]{:S(2)}) collective-permute-start(bf16[128,1024]{1,0:T(8,128)(2,1)} %get-tuple-element.47.refs_0_), channel_id=1, source_target_pairs={{0,1},{1,0},{2,3},{3,2},{4,5},{5,4},{6,7},{7,6},{8,9},{9,8},{10,11... | collective-permute-start | bytes 786440 | tf_op jit(solution)/shard_map/ppermute | solution.py:48
  82.9 9.2 %collective-permute-start.21 = (bf16[128,1024]{1,0:T(8,128)(2,1)}, bf16[128,1024]{1,0:T(8,128)(2,1)}, u32[]{:S(2)}, u32[]{:S(2)}) collective-permute-start(bf16[128,1024]{1,0:T(8,128)(2,1)} %collective-permute-done.17.refs_3_), channel_id=1, source_target_pairs={{0,1},{1,0},{2,3},{3,2},{4,5},{5,4},{6,7},{7,6},{8,9},{9,8},{10,11... | collective-permute-start | bytes 786440 | tf_op jit(solution)/shard_map/ppermute | solution.py:48
  83.3 8.8 %collective-permute-start.20 = (bf16[128,1024]{1,0:T(8,128)(2,1)}, bf16[128,1024]{1,0:T(8,128)(2,1)}, u32[]{:S(2)}, u32[]{:S(2)}) collective-permute-start(bf16[128,1024]{1,0:T(8,128)(2,1)} %collective-permute-done.16.refs_2_), channel_id=1, source_target_pairs={{0,1},{1,0},{2,3},{3,2},{4,5},{5,4},{6,7},{7,6},{8,9},{9,8},{10,11... | collective-permute-start | bytes 786440 | tf_op jit(solution)/shard_map/ppermute | solution.py:48
  83.4 8.7 %collective-permute-start.19 = (bf16[128,1024]{1,0:T(8,128)(2,1)}, bf16[128,1024]{1,0:T(8,128)(2,1)}, u32[]{:S(2)}, u32[]{:S(2)}) collective-permute-start(bf16[128,1024]{1,0:T(8,128)(2,1)} %collective-permute-done.15.refs_1_), channel_id=1, source_target_pairs={{0,1},{1,0},{2,3},{3,2},{4,5},{5,4},{6,7},{7,6},{8,9},{9,8},{10,11... | collective-permute-start | bytes 786440 | tf_op jit(solution)/shard_map/ppermute | solution.py:48
  86.3 13.4 %collective-permute-start.26 = (bf16[128,256]{1,0:T(8,128)(2,1)}, bf16[128,256]{1,0:T(8,128)(2,1)S(1)}, u32[]{:S(2)}, u32[]{:S(2)}) collective-permute-start(bf16[128,256]{1,0:T(8,128)(2,1)} %get-tuple-element.57), channel_id=1, source_target_pairs={{0,8},{1,9},{2,10},{3,11},{4,12},{5,13},{6,14},{7,15},{8,0},{9,1},... | collective-permute-start | bytes 196616 | tf_op jit(solution)/shard_map/ppermute | solution.py:48
  89.6 10.2 %collective-permute-start.28 = (bf16[128,256]{1,0:T(8,128)(2,1)}, bf16[128,256]{1,0:T(8,128)(2,1)S(1)}, u32[]{:S(2)}, u32[]{:S(2)}) collective-permute-start(bf16[128,256]{1,0:T(8,128)(2,1)} %get-tuple-element.58), channel_id=1, source_target_pairs={{0,24},{1,25},{2,26},{3,27},{4,28},{5,29},{6,30},{7,31},{8,16},{9,... | collective-permute-start | bytes 196616 | tf_op jit(solution)/shard_map/ppermute | solution.py:48
  92.1 7.7 %collective-permute-start.27 = (bf16[128,256]{1,0:T(8,128)(2,1)}, bf16[128,256]{1,0:T(8,128)(2,1)S(1)}, u32[]{:S(2)}, u32[]{:S(2)}) collective-permute-start(bf16[128,256]{1,0:T(8,128)(2,1)} %get-tuple-element.59), channel_id=1, source_target_pairs={{0,16},{1,17},{2,18},{3,19},{4,20},{5,21},{6,22},{7,23},{8,24},{9,... | collective-permute-start | bytes 196616 | tf_op jit(solution)/shard_map/ppermute | solution.py:48
  96.2 28.0 %all-to-all-start = ((bf16[4,128,1024]{2,1,0:T(8,128)(2,1)}), bf16[4,128,1024]{2,1,0:T(8,128)(2,1)S(1)}, u32[]{:S(2)}, u32[]{:S(2)}) async-start(bf16[4,128,1024]{2,1,0:T(8,128)(2,1)} %bitcast.20), calls=%async_computation | async-start | bytes 2097152 | tf_op jit(solution)/shard_map/all_to_all | solution.py:56
  100.7 6.6 %collective-permute-start.31 = (bf16[128,256]{1,0:T(8,128)(2,1)S(1)}, bf16[128,256]{1,0:T(8,128)(2,1)S(1)}, u32[]{:S(2)}, u32[]{:S(2)}) collective-permute-start(bf16[128,256]{1,0:T(8,128)(2,1)S(1)} %fusion.3), channel_id=1, source_target_pairs={{0,24},{1,25},{2,26},{3,27},{4,28},{5,29},{6,30},{7,31},{8,16},{9,... | collective-permute-start | bytes 196616 | tf_op jit(solution)/shard_map/ppermute | solution.py:48
  102.2 5.8 %collective-permute-start.30 = (bf16[128,256]{1,0:T(8,128)(2,1)S(1)}, bf16[128,256]{1,0:T(8,128)(2,1)S(1)}, u32[]{:S(2)}, u32[]{:S(2)}) collective-permute-start(bf16[128,256]{1,0:T(8,128)(2,1)S(1)} %fusion.3), channel_id=1, source_target_pairs={{0,16},{1,17},{2,18},{3,19},{4,20},{5,21},{6,22},{7,23},{8,24},{9,... | collective-permute-start | bytes 196616 | tf_op jit(solution)/shard_map/ppermute | solution.py:48
  108.8 12.5 %collective-permute-start.34 = (bf16[4,128,256]{2,1,0:T(8,128)(2,1)S(1)}, bf16[4,128,256]{2,1,0:T(8,128)(2,1)S(1)}, u32[]{:S(2)}, u32[]{:S(2)}) collective-permute-start(bf16[4,128,256]{2,1,0:T(8,128)(2,1)S(1)} %pad_maximum_fusion.refs_0_), channel_id=1, source_target_pairs={{0,6},{1,7},{2,4},{3,5},{4,2},{5,3},{6,0},{7,1},{8,14},{9,15},{10,... | collective-permute-start | bytes 786440 | tf_op jit(solution)/shard_map/ppermute | solution.py:48
  111.4 12.2 %collective-permute-start.33 = (bf16[4,128,256]{2,1,0:T(8,128)(2,1)S(1)}, bf16[4,128,256]{2,1,0:T(8,128)(2,1)S(1)}, u32[]{:S(2)}, u32[]{:S(2)}) collective-permute-start(bf16[4,128,256]{2,1,0:T(8,128)(2,1)S(1)} %pad_maximum_fusion.refs_0_), channel_id=1, source_target_pairs={{0,4},{1,5},{2,6},{3,7},{4,0},{5,1},{6,2},{7,3},{8,12},{9,13},{10,... | collective-permute-start | bytes 786440 | tf_op jit(solution)/shard_map/ppermute | solution.py:48
  112.0 11.7 %collective-permute-start.32 = (bf16[4,128,256]{2,1,0:T(8,128)(2,1)S(1)}, bf16[4,128,256]{2,1,0:T(8,128)(2,1)S(1)}, u32[]{:S(2)}, u32[]{:S(2)}) collective-permute-start(bf16[4,128,256]{2,1,0:T(8,128)(2,1)S(1)} %pad_maximum_fusion.refs_0_), channel_id=1, source_target_pairs={{0,2},{1,3},{2,0},{3,1},{4,6},{5,7},{6,4},{7,5},{8,10},{9,11},{10,... | collective-permute-start | bytes 786440 | tf_op jit(solution)/shard_map/ppermute | solution.py:48
  (25 other events, 116.1 us)

commit v5 on v4

--- a/solution.py
+++ b/solution.py
@@ -390,8 +390,12 @@
     feat = g.swap_xy(deltas).astype(F32).reshape(g.X * g.Y, -1, deltas.shape[1])
     feat_grad = jnp.sum(feat, axis=0).astype(BF16)
 
-    pieces = after(fold(g, shares).astype(BF16), arrived)
-    total = pieces[0].astype(F32)
+    moved = [shares[0]]
+    moved += [g.move(v, dx=at[0], dy=at[1]) for at, v in list(zip(squares, shares))[1:]]
+    moved = after(moved, arrived)
+    pieces = [sum(v[dz].astype(F32) for v in moved) for dz in range(g.Z)]
+    total = pieces[0]
+    pieces = [v.astype(BF16) for v in pieces]
     for dz in range(1, g.Z):
         total += g.move(pieces[dz], dz=dz).astype(F32)
     factor = (features.shape[0] * g.R * g.C) ** (-0.5)

time: 130 us -> 130 us (level)
    add x0 -> x1, other arithmetic: none -> 1.67 us  [on_device(): pieces = [sum((v[dz].astype(F32) for v in moved)) for dz in range(g.Z)]]
    unnamed x34 -> x38, local copies, waits for them, and re-layouts: 3.63 us -> 3.12 us
where the time goes in v5:
time: 130 us; the launch traced here: 129 us
  waiting for transfers between devices  54.6 us (42%)
  starting transfers between devices  43.4 us (33%)
  Pallas kernels  21.4 us (16%)
  other arithmetic  5.14 us (4%)
  local copies, waits for them, and re-layouts  3.12 us (2%)
  between operations  1.48 us (1%)
    ppermute x39, waiting for transfers between devices, move(): return lax.ppermute(value, ('row', 'col'), pairs)  54.6 us
    ppermute x39, starting transfers between devices, move(): return lax.ppermute(value, ('row', 'col'), pairs)  39.9 us
    pallas_call x1, Pallas kernels, forward(): pl.pallas_call(functools.partial(forward_kernel, g, slots, block, n), out...  4.2 us
    pallas_call x1, Pallas kernels, backward(): pl.pallas_call(functools.partial(backward_kernel, g, block, [len(group) f...  4.1 us
    pallas_call x1, Pallas kernels, layer(): pl.pallas_call(functools.partial(layer_kernel, g, len(parts)), out_shape=...  3.89 us
    pallas_call x1, Pallas kernels, build(): pl.pallas_call(functools.partial(build_kernel, g, slots, block), out_shap...  3.52 us
    all_to_all x1, starting transfers between devices, swap_xy(): lax.all_to_all(value, ('row', 'col'), 0, 0, axis_index_groups=groups, til...  3.51 us
    unnamed x38, local copies, waits for them, and re-layouts  3.12 us
  transfers between devices with their start and end apart: 40, of which 12 were waited for; matrix products, arithmetic and copies ran while one was open for 3% of the time, Pallas kernels for 8%

profile of v5, /device:TPU:0, one launch (start us, length us, event | category | flops | bytes accessed | tf_op | source)
XLA Modules:
  0.0 129.1 jit_solution(8036657846500292129)
XLA Ops:
  2.0 2.9 %collective-permute-start.2 = (bf16[128,1024]{1,0:T(8,128)(2,1)}, bf16[128,1024]{1,0:T(8,128)(2,1)S(1)}, u32[]{:S(2)}, u32[]{:S(2)}) collective-permute-start(bf16[128,1024]{1,0:T(8,128)(2,1)} %refs_4_.1), channel_id=1, source_target_pairs={{0,4},{1,5},{2,6},{3,7},{4,0},{5,1},{6,2},{7,3},{8,12},{9,13},{10,... | collective-permute-start | bytes 786440 | tf_op jit(solution)/shard_map/ppermute | solution.py:48
  5.1 2.0 %collective-permute-start.6 = (bf16[128,1024]{1,0:T(8,128)(2,1)}, bf16[128,1024]{1,0:T(8,128)(2,1)S(1)}, u32[]{:S(2)}, u32[]{:S(2)}) collective-permute-start(bf16[128,1024]{1,0:T(8,128)(2,1)} %refs_4_.1), channel_id=1, source_target_pairs={{0,2},{1,3},{2,0},{3,1},{4,6},{5,7},{6,4},{7,5},{8,10},{9,11},{10,... | collective-permute-start | bytes 786440 | tf_op jit(solution)/shard_map/ppermute | solution.py:48
  7.0 4.5 %collective-permute-done.refs_1_ = s32[17]{0:T(128)S(1)} collective-permute-done((s32[17]{0:T(128)S(1)}, s32[17]{0:T(128)S(1)}, u32[]{:S(2)}, u32[]{:S(2)}) %collective-permute-start) | collective-permute-done | bytes 100 | tf_op jit(solution)/shard_map/ppermute | solution.py:48
  11.6 1.8 %collective-permute-start.9 = (bf16[128,1024]{1,0:T(8,128)(2,1)S(1)}, bf16[128,1024]{1,0:T(8,128)(2,1)S(1)}, u32[]{:S(2)}, u32[]{:S(2)}) collective-permute-start(bf16[128,1024]{1,0:T(8,128)(2,1)S(1)} %collective-permute-done.2.refs_8_), channel_id=1, source_target_pairs={{0,2},{1,3},{2,0},{3,1},{4,6},{5,7},{6,4},{7,5},{8,10},{9,11},{10,... | collective-permute-start | bytes 786440 | tf_op jit(solution)/shard_map/ppermute | solution.py:48
  13.5 1.5 %collective-permute-start.1 = (bf16[8,128,128]{2,1,0:T(8,128)(2,1)}, bf16[8,128,128]{2,1,0:T(8,128)(2,1)}, u32[]{:S(2)}, u32[]{:S(2)}) collective-permute-start(bf16[8,128,128]{2,1,0:T(8,128)(2,1)} %bitcast.29), channel_id=1, source_target_pairs={{0,4},{1,5},{2,6},{3,7},{4,0},{5,1},{6,2},{7,3},{8,12},{9,13},{10,... | collective-permute-start | bytes 786440 | tf_op jit(solution)/shard_map/ppermute | solution.py:48
  17.6 2.8 %collective-permute-done.9.refs_10_ = bf16[128,1024]{1,0:T(8,128)(2,1)S(1)} collective-permute-done((bf16[128,1024]{1,0:T(8,128)(2,1)S(1)}, bf16[128,1024]{1,0:T(8,128)(2,1)S(1)}, u32[]{:S(2)}, u32[]{:S(2)}) %collective-permute-start.9) | collective-permute-done | bytes 262176 | tf_op jit(solution)/shard_map/ppermute | solution.py:48
  20.4 1.8 %collective-permute-done.1.refs_3_.refs_4_ = bf16[8,128,128]{2,1,0:T(8,128)(2,1)} collective-permute-done((bf16[8,128,128]{2,1,0:T(8,128)(2,1)}, bf16[8,128,128]{2,1,0:T(8,128)(2,1)}, u32[]{:S(2)}, u32[]{:S(2)}) %collective-permute-start.1) | collective-permute-done | bytes 262176 | tf_op jit(solution)/shard_map/ppermute | solution.py:48
  23.7 4.2 %forward.1 = (bf16[128,1024]{1,0:T(8,128)(2,1)}, bf16[128,1024]{1,0:T(8,128)(2,1)}, bf16[128,1024]{1,0:T(8,128)(2,1)}, bf16[128,1024]{1,0:T(8,128)(2,1)}) custom-call(s32[17]{0:T(128)} %copy-done.17, s32[17]{0:T(128)} %copy-done.16, bf16[8,128,128]{2,1,0:T(8,128)(2,1)} %bitcast.30, bf16[8,128,128]{2,1,0:T(8,128)(2,1)} %collective-permute-done.1.refs_3_.refs_4_, ...), custom_call_target="tpu_custom_call" | custom-call | tf_op jit(solution)/shard_map/forward/pallas_call | solution.py:140
  27.9 1.6 %collective-permute-start.11 = (bf16[128,1024]{1,0:T(8,128)(2,1)}, bf16[128,1024]{1,0:T(8,128)(2,1)}, u32[]{:S(2)}, u32[]{:S(2)}) collective-permute-start(bf16[128,1024]{1,0:T(8,128)(2,1)} %get-tuple-element.40), channel_id=1, source_target_pairs={{0,8},{1,9},{2,10},{3,11},{4,12},{5,13},{6,14},{7,15},{8,0},{9,1},... | collective-permute-start | bytes 786440 | tf_op jit(solution)/shard_map/ppermute | solution.py:48
  29.5 2.6 %collective-permute-start.12 = (bf16[128,1024]{1,0:T(8,128)(2,1)}, bf16[128,1024]{1,0:T(8,128)(2,1)}, u32[]{:S(2)}, u32[]{:S(2)}) collective-permute-start(bf16[128,1024]{1,0:T(8,128)(2,1)} %get-tuple-element.41), channel_id=1, source_target_pairs={{0,16},{1,17},{2,18},{3,19},{4,20},{5,21},{6,22},{7,23},{8,24},{9,... | collective-permute-start | bytes 786440 | tf_op jit(solution)/shard_map/ppermute | solution.py:48
  32.3 3.5 %build.1.matrix = bf16[512,1024]{1,0:T(8,128)(2,1)} custom-call(s32[17]{0:T(128)} %copy-done.17, s32[17]{0:T(128)} %copy-done.16, s32[34]{0:T(128)} %copy-done.18, bf16[8,128,128]{2,1,0:T(8,128)(2,1)} %bitcast.31, bf16[8,128,128]{2,1,0:T(8,128)(2,1)} %collective-permute-done.1.refs_3_.refs_4_, bf16[8,128,128]{2,1,0:T(8,128)(2,1)} %collective-permute-done.3.refs_5_, ...), custom_call_target="tpu_custom_call" | custom-call | tf_op jit(solution)/shard_map/build/pallas_call | solution.py:174
  35.9 6.2 %collective-permute-done.11.refs_1_ = bf16[128,1024]{1,0:T(8,128)(2,1)} collective-permute-done((bf16[128,1024]{1,0:T(8,128)(2,1)}, bf16[128,1024]{1,0:T(8,128)(2,1)}, u32[]{:S(2)}, u32[]{:S(2)}) %collective-permute-start.11) | collective-permute-done | bytes 262176 | tf_op jit(solution)/shard_map/ppermute | solution.py:48
  42.1 9.0 %collective-permute-done.12.refs_2_ = bf16[128,1024]{1,0:T(8,128)(2,1)} collective-permute-done((bf16[128,1024]{1,0:T(8,128)(2,1)}, bf16[128,1024]{1,0:T(8,128)(2,1)}, u32[]{:S(2)}, u32[]{:S(2)}) %collective-permute-start.12) | collective-permute-done | bytes 262176 | tf_op jit(solution)/shard_map/ppermute | solution.py:48
  51.2 3.9 %layer.1 = (bf16[128,1024]{1,0:T(8,128)(2,1)}, bf16[128,1536]{1,0:T(8,128)(2,1)}, bf16[128,1024]{1,0:T(8,128)(2,1)}, bf16[128,512]{1,0:T(8,128)(2,1)}) custom-call(bf16[128,1024]{1,0:T(8,128)(2,1)} %get-tuple-element.44.refs_0_, bf16[128,1024]{1,0:T(8,128)(2,1)} %collective-permute-done.11.refs_1_, bf16[128,1024]{1,0:T(8,128)(2,1)} %collective-permute-done.12.refs_2_, ...), custom_call_target="tpu_custom_call" | custom-call | tf_op jit(solution)/shard_map/layer/pallas_call | solution.py:252
  55.1 2.5 %collective-permute-start.17 = (bf16[128,1024]{1,0:T(8,128)(2,1)}, bf16[128,1024]{1,0:T(8,128)(2,1)}, u32[]{:S(2)}, u32[]{:S(2)}) collective-permute-start(bf16[128,1024]{1,0:T(8,128)(2,1)} %get-tuple-element.50.refs_0_), channel_id=1, source_target_pairs={{0,24},{1,25},{2,26},{3,27},{4,28},{5,29},{6,30},{7,31},{8,16},{9,... | collective-permute-start | bytes 786440 | tf_op jit(solution)/shard_map/ppermute | solution.py:48
  57.6 4.4 %collective-permute-start.16 = (bf16[128,1024]{1,0:T(8,128)(2,1)}, bf16[128,1024]{1,0:T(8,128)(2,1)}, u32[]{:S(2)}, u32[]{:S(2)}) collective-permute-start(bf16[128,1024]{1,0:T(8,128)(2,1)} %get-tuple-element.50.refs_0_), channel_id=1, source_target_pairs={{0,16},{1,17},{2,18},{3,19},{4,20},{5,21},{6,22},{7,23},{8,24},{9,... | collective-permute-start | bytes 786440 | tf_op jit(solution)/shard_map/ppermute | solution.py:48
  62.1 2.5 %terms.1 = (bf16[4,128,256]{2,1,0:T(8,128)(2,1)}, bf16[4,128,256]{2,1,0:T(8,128)(2,1)}, bf16[4,128,256]{2,1,0:T(8,128)(2,1)}, bf16[4,128,256]{2,1,0:T(8,128)(2,1)}) custom-call(bf16[128,512]{1,0:T(8,128)(2,1)} %get-tuple-element.51.keep, bf16[128,1536]{1,0:T(8,128)(2,1)} %get-tuple-element.52.share, bf16[128,1536]{1,0:T(8,128)(2,1)} %collective-permute-done.22.share_got), custom_call_target="tpu_custom_call" | custom-call | tf_op jit(solution)/shard_map/terms/pallas_call | solution.py:294
  65.1 1.5 %collective-permute-start.24 = (bf16[4,128,256]{2,1,0:T(8,128)(2,1)}, bf16[4,128,256]{2,1,0:T(8,128)(2,1)S(1)}, u32[]{:S(2)}, u32[]{:S(2)}) collective-permute-start(bf16[4,128,256]{2,1,0:T(8,128)(2,1)} %get-tuple-element.55), channel_id=1, source_target_pairs={{0,4},{1,5},{2,6},{3,7},{4,0},{5,1},{6,2},{7,3},{8,12},{9,13},{10,... | collective-permute-start | bytes 786440 | tf_op jit(solution)/shard_map/ppermute | solution.py:48
  66.6 1.5 %collective-permute-start.25 = (bf16[4,128,256]{2,1,0:T(8,128)(2,1)}, bf16[4,128,256]{2,1,0:T(8,128)(2,1)S(1)}, u32[]{:S(2)}, u32[]{:S(2)}) collective-permute-start(bf16[4,128,256]{2,1,0:T(8,128)(2,1)} %get-tuple-element.56), channel_id=1, source_target_pairs={{0,6},{1,7},{2,4},{3,5},{4,2},{5,3},{6,0},{7,1},{8,14},{9,15},{10,... | collective-permute-start | bytes 786440 | tf_op jit(solution)/shard_map/ppermute | solution.py:48
  68.1 14.7 %collective-permute-done.16.refs_2_ = bf16[128,1024]{1,0:T(8,128)(2,1)} collective-permute-done((bf16[128,1024]{1,0:T(8,128)(2,1)}, bf16[128,1024]{1,0:T(8,128)(2,1)}, u32[]{:S(2)}, u32[]{:S(2)}) %collective-permute-start.16) | collective-permute-done | bytes 262176 | tf_op jit(solution)/shard_map/ppermute | solution.py:48
  84.0 1.7 %fusion.4 = (bf16[128,256]{1,0:T(8,128)(2,1)}, bf16[128,256]{1,0:T(8,128)(2,1)}, bf16[128,256]{1,0:T(8,128)(2,1)}) fusion(bf16[4,128,256]{2,1,0:T(8,128)(2,1)S(1)} %collective-permute-done.25, bf16[4,128,256]{2,1,0:T(8,128)(2,1)S(1)} %collective-permute-done.24, bf16[4,128,256]{2,1,0:T(8,128)(2,1)S(1)} %collective-permute-done.23, ...), kind=kLoop, calls=%fused_computation.9 | loop fusion | flops 786432 | bytes 983040 | tf_op jit(solution)/shard_map/add | solution.py:396
  85.6 3.2 %collective-permute-start.26 = (bf16[128,256]{1,0:T(8,128)(2,1)}, bf16[128,256]{1,0:T(8,128)(2,1)S(1)}, u32[]{:S(2)}, u32[]{:S(2)}) collective-permute-start(bf16[128,256]{1,0:T(8,128)(2,1)} %get-tuple-element.63), channel_id=1, source_target_pairs={{0,8},{1,9},{2,10},{3,11},{4,12},{5,13},{6,14},{7,15},{8,0},{9,1},... | collective-permute-start | bytes 196616 | tf_op jit(solution)/shard_map/ppermute | solution.py:48
  88.9 2.5 %collective-permute-start.28 = (bf16[128,256]{1,0:T(8,128)(2,1)}, bf16[128,256]{1,0:T(8,128)(2,1)S(1)}, u32[]{:S(2)}, u32[]{:S(2)}) collective-permute-start(bf16[128,256]{1,0:T(8,128)(2,1)} %get-tuple-element.64), channel_id=1, source_target_pairs={{0,24},{1,25},{2,26},{3,27},{4,28},{5,29},{6,30},{7,31},{8,16},{9,... | collective-permute-start | bytes 196616 | tf_op jit(solution)/shard_map/ppermute | solution.py:48
  91.4 4.1 %backward.1 = bf16[512,1024]{1,0:T(8,128)(2,1)} custom-call(bf16[512,1024]{1,0:T(8,128)(2,1)} %build.1.matrix, bf16[128,1024]{1,0:T(8,128)(2,1)} %get-tuple-element.50.refs_0_, bf16[128,1024]{1,0:T(8,128)(2,1)} %collective-permute-done.15.refs_1_, bf16[128,1024]{1,0:T(8,128)(2,1)} %collective-permute-done.16.refs_2_, ...), custom_call_target="tpu_custom_call" | custom-call | tf_op jit(solution)/shard_map/backward/pallas_call | solution.py:202
  95.5 3.5 %all-to-all-start = ((bf16[4,128,1024]{2,1,0:T(8,128)(2,1)}), bf16[4,128,1024]{2,1,0:T(8,128)(2,1)S(1)}, u32[]{:S(2)}, u32[]{:S(2)}) async-start(bf16[4,128,1024]{2,1,0:T(8,128)(2,1)} %bitcast.27), calls=%async_computation | async-start | bytes 2097152 | tf_op jit(solution)/shard_map/all_to_all | solution.py:56
  100.1 1.6 %collective-permute-start.31 = (bf16[128,256]{1,0:T(8,128)(2,1)S(1)}, bf16[128,256]{1,0:T(8,128)(2,1)S(1)}, u32[]{:S(2)}, u32[]{:S(2)}) collective-permute-start(bf16[128,256]{1,0:T(8,128)(2,1)S(1)} %fusion.3), channel_id=1, source_target_pairs={{0,24},{1,25},{2,26},{3,27},{4,28},{5,29},{6,30},{7,31},{8,16},{9,... | collective-permute-start | bytes 196616 | tf_op jit(solution)/shard_map/ppermute | solution.py:48
  101.7 1.8 %collective-permute-start.30 = (bf16[128,256]{1,0:T(8,128)(2,1)S(1)}, bf16[128,256]{1,0:T(8,128)(2,1)S(1)}, u32[]{:S(2)}, u32[]{:S(2)}) collective-permute-start(bf16[128,256]{1,0:T(8,128)(2,1)S(1)} %fusion.3), channel_id=1, source_target_pairs={{0,16},{1,17},{2,18},{3,19},{4,20},{5,21},{6,22},{7,23},{8,24},{9,... | collective-permute-start | bytes 196616 | tf_op jit(solution)/shard_map/ppermute | solution.py:48
  104.5 2.2 %collective-permute-done.31 = bf16[128,256]{1,0:T(8,128)(2,1)S(1)} collective-permute-done((bf16[128,256]{1,0:T(8,128)(2,1)S(1)}, bf16[128,256]{1,0:T(8,128)(2,1)S(1)}, u32[]{:S(2)}, u32[]{:S(2)}) %collective-permute-start.31) | collective-permute-done | bytes 65568 | tf_op jit(solution)/shard_map/ppermute | solution.py:48
  108.2 2.7 %collective-permute-start.34 = (bf16[4,128,256]{2,1,0:T(8,128)(2,1)S(1)}, bf16[4,128,256]{2,1,0:T(8,128)(2,1)S(1)}, u32[]{:S(2)}, u32[]{:S(2)}) collective-permute-start(bf16[4,128,256]{2,1,0:T(8,128)(2,1)S(1)} %pad_maximum_fusion.refs_0_), channel_id=1, source_target_pairs={{0,6},{1,7},{2,4},{3,5},{4,2},{5,3},{6,0},{7,1},{8,14},{9,15},{10,... | collective-permute-start | bytes 786440 | tf_op jit(solution)/shard_map/ppermute | solution.py:48
  111.7 8.9 %collective-permute-done.34.refs_3_ = bf16[4,128,256]{2,1,0:T(8,128)(2,1)S(1)} collective-permute-done((bf16[4,128,256]{2,1,0:T(8,128)(2,1)S(1)}, bf16[4,128,256]{2,1,0:T(8,128)(2,1)S(1)}, u32[]{:S(2)}, u32[]{:S(2)}) %collective-permute-start.34) | collective-permute-done | bytes 262176 | tf_op jit(solution)/shard_map/ppermute | solution.py:48
  121.1 1.8 %collective-permute-done.33.refs_2_ = bf16[4,128,256]{2,1,0:T(8,128)(2,1)S(1)} collective-permute-done((bf16[4,128,256]{2,1,0:T(8,128)(2,1)S(1)}, bf16[4,128,256]{2,1,0:T(8,128)(2,1)S(1)}, u32[]{:S(2)}, u32[]{:S(2)}) %collective-permute-start.33) | collective-permute-done | bytes 262176 | tf_op jit(solution)/shard_map/ppermute | solution.py:48
  125.9 3.1 %join.1 = f32[1024,1024]{1,0:T(8,128)} custom-call(bf16[4,128,256]{2,1,0:T(8,128)(2,1)} %copy-done, bf16[4,128,256]{2,1,0:T(8,128)(2,1)} %copy-done.6, bf16[4,128,256]{2,1,0:T(8,128)(2,1)} %copy-done.5, bf16[4,128,256]{2,1,0:T(8,128)(2,1)} %copy-done.4, bf16[4,128,256]{2,1,0:T(8,128)(2,1)} %copy-done.9, ...), custom_call_target="tpu_custom_call" | custom-call | tf_op jit(solution)/shard_map/join/pallas_call | solution.py:336
  (98 shorter events, 15.0 us)
Async XLA Ops:
  2.0 9.5 %collective-permute-start.2 = (bf16[128,1024]{1,0:T(8,128)(2,1)}, bf16[128,1024]{1,0:T(8,128)(2,1)S(1)}, u32[]{:S(2)}, u32[]{:S(2)}) collective-permute-start(bf16[128,1024]{1,0:T(8,128)(2,1)} %refs_4_.1), channel_id=1, source_target_pairs={{0,4},{1,5},{2,6},{3,7},{4,0},{5,1},{6,2},{7,3},{8,12},{9,13},{10,... | collective-permute-start | bytes 786440 | tf_op jit(solution)/shard_map/ppermute | solution.py:48
  5.0 6.6 %collective-permute-start = (s32[17]{0:T(128)S(1)}, s32[17]{0:T(128)S(1)}, u32[]{:S(2)}, u32[]{:S(2)}) collective-permute-start(s32[17]{0:T(128)S(1)} %pad_add_fusion.refs_0_), channel_id=1, source_target_pairs={{0,4},{1,5},{2,6},{3,7},{4,0},{5,1},{6,2},{7,3},{8,12},{9,13},{10,... | collective-permute-start | bytes 212 | tf_op jit(solution)/shard_map/ppermute | solution.py:48
  5.1 12.0 %collective-permute-start.6 = (bf16[128,1024]{1,0:T(8,128)(2,1)}, bf16[128,1024]{1,0:T(8,128)(2,1)S(1)}, u32[]{:S(2)}, u32[]{:S(2)}) collective-permute-start(bf16[128,1024]{1,0:T(8,128)(2,1)} %refs_4_.1), channel_id=1, source_target_pairs={{0,2},{1,3},{2,0},{3,1},{4,6},{5,7},{6,4},{7,5},{8,10},{9,11},{10,... | collective-permute-start | bytes 786440 | tf_op jit(solution)/shard_map/ppermute | solution.py:48
  11.6 5.8 %collective-permute-start.3 = (bf16[8,128,128]{2,1,0:T(8,128)(2,1)}, bf16[8,128,128]{2,1,0:T(8,128)(2,1)}, u32[]{:S(2)}, u32[]{:S(2)}) collective-permute-start(bf16[8,128,128]{2,1,0:T(8,128)(2,1)} %bitcast.28), channel_id=1, source_target_pairs={{0,1},{1,0},{2,3},{3,2},{4,5},{5,4},{6,7},{7,6},{8,9},{9,8},{10,11... | collective-permute-start | bytes 786440 | tf_op jit(solution)/shard_map/ppermute | solution.py:48
  11.6 8.7 %collective-permute-start.9 = (bf16[128,1024]{1,0:T(8,128)(2,1)S(1)}, bf16[128,1024]{1,0:T(8,128)(2,1)S(1)}, u32[]{:S(2)}, u32[]{:S(2)}) collective-permute-start(bf16[128,1024]{1,0:T(8,128)(2,1)S(1)} %collective-permute-done.2.refs_8_), channel_id=1, source_target_pairs={{0,2},{1,3},{2,0},{3,1},{4,6},{5,7},{6,4},{7,5},{8,10},{9,11},{10,... | collective-permute-start | bytes 786440 | tf_op jit(solution)/shard_map/ppermute | solution.py:48
  13.5 8.7 %collective-permute-start.1 = (bf16[8,128,128]{2,1,0:T(8,128)(2,1)}, bf16[8,128,128]{2,1,0:T(8,128)(2,1)}, u32[]{:S(2)}, u32[]{:S(2)}) collective-permute-start(bf16[8,128,128]{2,1,0:T(8,128)(2,1)} %bitcast.29), channel_id=1, source_target_pairs={{0,4},{1,5},{2,6},{3,7},{4,0},{5,1},{6,2},{7,3},{8,12},{9,13},{10,... | collective-permute-start | bytes 786440 | tf_op jit(solution)/shard_map/ppermute | solution.py:48
  16.8 5.3 %collective-permute-start.5 = (bf16[128,1024]{1,0:T(8,128)(2,1)}, bf16[128,1024]{1,0:T(8,128)(2,1)S(1)}, u32[]{:S(2)}, u32[]{:S(2)}) collective-permute-start(bf16[128,1024]{1,0:T(8,128)(2,1)} %refs_4_.1), channel_id=1, source_target_pairs={{0,1},{1,0},{2,3},{3,2},{4,5},{5,4},{6,7},{7,6},{8,9},{9,8},{10,11... | collective-permute-start | bytes 786440 | tf_op jit(solution)/shard_map/ppermute | solution.py:48
  17.1 5.1 %collective-permute-start.7 = (bf16[128,1024]{1,0:T(8,128)(2,1)S(1)}, bf16[128,1024]{1,0:T(8,128)(2,1)S(1)}, u32[]{:S(2)}, u32[]{:S(2)}) collective-permute-start(bf16[128,1024]{1,0:T(8,128)(2,1)S(1)} %collective-permute-done.6.refs_6_), channel_id=1, source_target_pairs={{0,1},{1,0},{2,3},{3,2},{4,5},{5,4},{6,7},{7,6},{8,9},{9,8},{10,11... | collective-permute-start | bytes 786440 | tf_op jit(solution)/shard_map/ppermute | solution.py:48
  17.4 4.8 %collective-permute-start.8 = (bf16[128,1024]{1,0:T(8,128)(2,1)S(1)}, bf16[128,1024]{1,0:T(8,128)(2,1)S(1)}, u32[]{:S(2)}, u32[]{:S(2)}) collective-permute-start(bf16[128,1024]{1,0:T(8,128)(2,1)S(1)} %collective-permute-done.2.refs_8_), channel_id=1, source_target_pairs={{0,1},{1,0},{2,3},{3,2},{4,5},{5,4},{6,7},{7,6},{8,9},{9,8},{10,11... | collective-permute-start | bytes 786440 | tf_op jit(solution)/shard_map/ppermute | solution.py:48
  27.9 14.2 %collective-permute-start.11 = (bf16[128,1024]{1,0:T(8,128)(2,1)}, bf16[128,1024]{1,0:T(8,128)(2,1)}, u32[]{:S(2)}, u32[]{:S(2)}) collective-permute-start(bf16[128,1024]{1,0:T(8,128)(2,1)} %get-tuple-element.40), channel_id=1, source_target_pairs={{0,8},{1,9},{2,10},{3,11},{4,12},{5,13},{6,14},{7,15},{8,0},{9,1},... | collective-permute-start | bytes 786440 | tf_op jit(solution)/shard_map/ppermute | solution.py:48
  29.5 21.6 %collective-permute-start.12 = (bf16[128,1024]{1,0:T(8,128)(2,1)}, bf16[128,1024]{1,0:T(8,128)(2,1)}, u32[]{:S(2)}, u32[]{:S(2)}) collective-permute-start(bf16[128,1024]{1,0:T(8,128)(2,1)} %get-tuple-element.41), channel_id=1, source_target_pairs={{0,16},{1,17},{2,18},{3,19},{4,20},{5,21},{6,22},{7,23},{8,24},{9,... | collective-permute-start | bytes 786440 | tf_op jit(solution)/shard_map/ppermute | solution.py:48
  32.1 19.0 %collective-permute-start.13 = (bf16[128,1024]{1,0:T(8,128)(2,1)}, bf16[128,1024]{1,0:T(8,128)(2,1)}, u32[]{:S(2)}, u32[]{:S(2)}) collective-permute-start(bf16[128,1024]{1,0:T(8,128)(2,1)} %get-tuple-element.42), channel_id=1, source_target_pairs={{0,24},{1,25},{2,26},{3,27},{4,28},{5,29},{6,30},{7,31},{8,16},{9,... | collective-permute-start | bytes 786440 | tf_op jit(solution)/shard_map/ppermute | solution.py:48
  55.0 7.0 %collective-permute-start.22 = (bf16[128,1536]{1,0:T(8,128)(2,1)}, bf16[128,1536]{1,0:T(8,128)(2,1)}, u32[]{:S(2)}, u32[]{:S(2)}) collective-permute-start(bf16[128,1536]{1,0:T(8,128)(2,1)} %get-tuple-element.52.share), channel_id=1, source_target_pairs={{0,1},{1,0},{2,3},{3,2},{4,5},{5,4},{6,7},{7,6},{8,9},{9,8},{10,11... | collective-permute-start | bytes 1179656 | tf_op jit(solution)/shard_map/ppermute | solution.py:48
  55.1 11.5 %collective-permute-start.17 = (bf16[128,1024]{1,0:T(8,128)(2,1)}, bf16[128,1024]{1,0:T(8,128)(2,1)}, u32[]{:S(2)}, u32[]{:S(2)}) collective-permute-start(bf16[128,1024]{1,0:T(8,128)(2,1)} %get-tuple-element.50.refs_0_), channel_id=1, source_target_pairs={{0,24},{1,25},{2,26},{3,27},{4,28},{5,29},{6,30},{7,31},{8,16},{9,... | collective-permute-start | bytes 786440 | tf_op jit(solution)/shard_map/ppermute | solution.py:48
  57.6 25.2 %collective-permute-start.16 = (bf16[128,1024]{1,0:T(8,128)(2,1)}, bf16[128,1024]{1,0:T(8,128)(2,1)}, u32[]{:S(2)}, u32[]{:S(2)}) collective-permute-start(bf16[128,1024]{1,0:T(8,128)(2,1)} %get-tuple-element.50.refs_0_), channel_id=1, source_target_pairs={{0,16},{1,17},{2,18},{3,19},{4,20},{5,21},{6,22},{7,23},{8,24},{9,... | collective-permute-start | bytes 786440 | tf_op jit(solution)/shard_map/ppermute | solution.py:48
  61.9 20.9 %collective-permute-start.15 = (bf16[128,1024]{1,0:T(8,128)(2,1)}, bf16[128,1024]{1,0:T(8,128)(2,1)}, u32[]{:S(2)}, u32[]{:S(2)}) collective-permute-start(bf16[128,1024]{1,0:T(8,128)(2,1)} %get-tuple-element.50.refs_0_), channel_id=1, source_target_pairs={{0,8},{1,9},{2,10},{3,11},{4,12},{5,13},{6,14},{7,15},{8,0},{9,1},... | collective-permute-start | bytes 786440 | tf_op jit(solution)/shard_map/ppermute | solution.py:48
  64.6 18.7 %collective-permute-start.23 = (bf16[4,128,256]{2,1,0:T(8,128)(2,1)}, bf16[4,128,256]{2,1,0:T(8,128)(2,1)S(1)}, u32[]{:S(2)}, u32[]{:S(2)}) collective-permute-start(bf16[4,128,256]{2,1,0:T(8,128)(2,1)} %get-tuple-element.54), channel_id=1, source_target_pairs={{0,2},{1,3},{2,0},{3,1},{4,6},{5,7},{6,4},{7,5},{8,10},{9,11},{10,... | collective-permute-start | bytes 786440 | tf_op jit(solution)/shard_map/ppermute | solution.py:48
  65.1 18.3 %collective-permute-start.24 = (bf16[4,128,256]{2,1,0:T(8,128)(2,1)}, bf16[4,128,256]{2,1,0:T(8,128)(2,1)S(1)}, u32[]{:S(2)}, u32[]{:S(2)}) collective-permute-start(bf16[4,128,256]{2,1,0:T(8,128)(2,1)} %get-tuple-element.55), channel_id=1, source_target_pairs={{0,4},{1,5},{2,6},{3,7},{4,0},{5,1},{6,2},{7,3},{8,12},{9,13},{10,... | collective-permute-start | bytes 786440 | tf_op jit(solution)/shard_map/ppermute | solution.py:48
  66.6 17.2 %collective-permute-start.25 = (bf16[4,128,256]{2,1,0:T(8,128)(2,1)}, bf16[4,128,256]{2,1,0:T(8,128)(2,1)S(1)}, u32[]{:S(2)}, u32[]{:S(2)}) collective-permute-start(bf16[4,128,256]{2,1,0:T(8,128)(2,1)} %get-tuple-element.56), channel_id=1, source_target_pairs={{0,6},{1,7},{2,4},{3,5},{4,2},{5,3},{6,0},{7,1},{8,14},{9,15},{10,... | collective-permute-start | bytes 786440 | tf_op jit(solution)/shard_map/ppermute | solution.py:48
  82.7 6.2 %collective-permute-start.18 = (bf16[128,1024]{1,0:T(8,128)(2,1)}, bf16[128,1024]{1,0:T(8,128)(2,1)}, u32[]{:S(2)}, u32[]{:S(2)}) collective-permute-start(bf16[128,1024]{1,0:T(8,128)(2,1)} %get-tuple-element.50.refs_0_), channel_id=1, source_target_pairs={{0,1},{1,0},{2,3},{3,2},{4,5},{5,4},{6,7},{7,6},{8,9},{9,8},{10,11... | collective-permute-start | bytes 786440 | tf_op jit(solution)/shard_map/ppermute | solution.py:48
  82.8 8.6 %collective-permute-start.21 = (bf16[128,1024]{1,0:T(8,128)(2,1)}, bf16[128,1024]{1,0:T(8,128)(2,1)}, u32[]{:S(2)}, u32[]{:S(2)}) collective-permute-start(bf16[128,1024]{1,0:T(8,128)(2,1)} %collective-permute-done.17.refs_3_), channel_id=1, source_target_pairs={{0,1},{1,0},{2,3},{3,2},{4,5},{5,4},{6,7},{7,6},{8,9},{9,8},{10,11... | collective-permute-start | bytes 786440 | tf_op jit(solution)/shard_map/ppermute | solution.py:48
  83.3 8.2 %collective-permute-start.20 = (bf16[128,1024]{1,0:T(8,128)(2,1)}, bf16[128,1024]{1,0:T(8,128)(2,1)}, u32[]{:S(2)}, u32[]{:S(2)}) collective-permute-start(bf16[128,1024]{1,0:T(8,128)(2,1)} %collective-permute-done.16.refs_2_), channel_id=1, source_target_pairs={{0,1},{1,0},{2,3},{3,2},{4,5},{5,4},{6,7},{7,6},{8,9},{9,8},{10,11... | collective-permute-start | bytes 786440 | tf_op jit(solution)/shard_map/ppermute | solution.py:48
  83.3 8.1 %collective-permute-start.19 = (bf16[128,1024]{1,0:T(8,128)(2,1)}, bf16[128,1024]{1,0:T(8,128)(2,1)}, u32[]{:S(2)}, u32[]{:S(2)}) collective-permute-start(bf16[128,1024]{1,0:T(8,128)(2,1)} %collective-permute-done.15.refs_1_), channel_id=1, source_target_pairs={{0,1},{1,0},{2,3},{3,2},{4,5},{5,4},{6,7},{7,6},{8,9},{9,8},{10,11... | collective-permute-start | bytes 786440 | tf_op jit(solution)/shard_map/ppermute | solution.py:48
  85.6 13.4 %collective-permute-start.26 = (bf16[128,256]{1,0:T(8,128)(2,1)}, bf16[128,256]{1,0:T(8,128)(2,1)S(1)}, u32[]{:S(2)}, u32[]{:S(2)}) collective-permute-start(bf16[128,256]{1,0:T(8,128)(2,1)} %get-tuple-element.63), channel_id=1, source_target_pairs={{0,8},{1,9},{2,10},{3,11},{4,12},{5,13},{6,14},{7,15},{8,0},{9,1},... | collective-permute-start | bytes 196616 | tf_op jit(solution)/shard_map/ppermute | solution.py:48
  88.9 10.2 %collective-permute-start.28 = (bf16[128,256]{1,0:T(8,128)(2,1)}, bf16[128,256]{1,0:T(8,128)(2,1)S(1)}, u32[]{:S(2)}, u32[]{:S(2)}) collective-permute-start(bf16[128,256]{1,0:T(8,128)(2,1)} %get-tuple-element.64), channel_id=1, source_target_pairs={{0,24},{1,25},{2,26},{3,27},{4,28},{5,29},{6,30},{7,31},{8,16},{9,... | collective-permute-start | bytes 196616 | tf_op jit(solution)/shard_map/ppermute | solution.py:48
  91.4 7.7 %collective-permute-start.27 = (bf16[128,256]{1,0:T(8,128)(2,1)}, bf16[128,256]{1,0:T(8,128)(2,1)S(1)}, u32[]{:S(2)}, u32[]{:S(2)}) collective-permute-start(bf16[128,256]{1,0:T(8,128)(2,1)} %get-tuple-element.65), channel_id=1, source_target_pairs={{0,16},{1,17},{2,18},{3,19},{4,20},{5,21},{6,22},{7,23},{8,24},{9,... | collective-permute-start | bytes 196616 | tf_op jit(solution)/shard_map/ppermute | solution.py:48
  95.5 28.0 %all-to-all-start = ((bf16[4,128,1024]{2,1,0:T(8,128)(2,1)}), bf16[4,128,1024]{2,1,0:T(8,128)(2,1)S(1)}, u32[]{:S(2)}, u32[]{:S(2)}) async-start(bf16[4,128,1024]{2,1,0:T(8,128)(2,1)} %bitcast.27), calls=%async_computation | async-start | bytes 2097152 | tf_op jit(solution)/shard_map/all_to_all | solution.py:56
  100.1 6.6 %collective-permute-start.31 = (bf16[128,256]{1,0:T(8,128)(2,1)S(1)}, bf16[128,256]{1,0:T(8,128)(2,1)S(1)}, u32[]{:S(2)}, u32[]{:S(2)}) collective-permute-start(bf16[128,256]{1,0:T(8,128)(2,1)S(1)} %fusion.3), channel_id=1, source_target_pairs={{0,24},{1,25},{2,26},{3,27},{4,28},{5,29},{6,30},{7,31},{8,16},{9,... | collective-permute-start | bytes 196616 | tf_op jit(solution)/shard_map/ppermute | solution.py:48
  101.7 5.8 %collective-permute-start.30 = (bf16[128,256]{1,0:T(8,128)(2,1)S(1)}, bf16[128,256]{1,0:T(8,128)(2,1)S(1)}, u32[]{:S(2)}, u32[]{:S(2)}) collective-permute-start(bf16[128,256]{1,0:T(8,128)(2,1)S(1)} %fusion.3), channel_id=1, source_target_pairs={{0,16},{1,17},{2,18},{3,19},{4,20},{5,21},{6,22},{7,23},{8,24},{9,... | collective-permute-start | bytes 196616 | tf_op jit(solution)/shard_map/ppermute | solution.py:48
  108.2 12.4 %collective-permute-start.34 = (bf16[4,128,256]{2,1,0:T(8,128)(2,1)S(1)}, bf16[4,128,256]{2,1,0:T(8,128)(2,1)S(1)}, u32[]{:S(2)}, u32[]{:S(2)}) collective-permute-start(bf16[4,128,256]{2,1,0:T(8,128)(2,1)S(1)} %pad_maximum_fusion.refs_0_), channel_id=1, source_target_pairs={{0,6},{1,7},{2,4},{3,5},{4,2},{5,3},{6,0},{7,1},{8,14},{9,15},{10,... | collective-permute-start | bytes 786440 | tf_op jit(solution)/shard_map/ppermute | solution.py:48
  110.8 12.1 %collective-permute-start.33 = (bf16[4,128,256]{2,1,0:T(8,128)(2,1)S(1)}, bf16[4,128,256]{2,1,0:T(8,128)(2,1)S(1)}, u32[]{:S(2)}, u32[]{:S(2)}) collective-permute-start(bf16[4,128,256]{2,1,0:T(8,128)(2,1)S(1)} %pad_maximum_fusion.refs_0_), channel_id=1, source_target_pairs={{0,4},{1,5},{2,6},{3,7},{4,0},{5,1},{6,2},{7,3},{8,12},{9,13},{10,... | collective-permute-start | bytes 786440 | tf_op jit(solution)/shard_map/ppermute | solution.py:48
  111.4 11.6 %collective-permute-start.32 = (bf16[4,128,256]{2,1,0:T(8,128)(2,1)S(1)}, bf16[4,128,256]{2,1,0:T(8,128)(2,1)S(1)}, u32[]{:S(2)}, u32[]{:S(2)}) collective-permute-start(bf16[4,128,256]{2,1,0:T(8,128)(2,1)S(1)} %pad_maximum_fusion.refs_0_), channel_id=1, source_target_pairs={{0,2},{1,3},{2,0},{3,1},{4,6},{5,7},{6,4},{7,5},{8,10},{9,11},{10,... | collective-permute-start | bytes 786440 | tf_op jit(solution)/shard_map/ppermute | solution.py:48
  (27 other events, 120.1 us)

commit v6 on v5

--- a/solution.py
+++ b/solution.py
@@ -269,8 +269,8 @@
 def terms_kernel(g, keep, share, share_got, *refs):
     outs, turned, grads = refs[:-2], refs[-2], refs[-1]
     nodes, half = keep.shape
-    both = jnp.concatenate([keep[...].astype(F32), share_got[:, :half].astype(F32)], axis=0)
-    turned[...] = both.T.astype(BF16)
+    turned[:, :nodes] = keep[...].T
+    turned[:, nodes:] = share_got[:, :half].T
     z, x, y, _ = g.here()
     rows, width = outs[0].shape[1:]
     for dz in range(g.Z):

time: 130 us -> 130 us (level)
  transfers between devices with their start and end apart: 40 -> 40, of which waited for: 12 -> 12; matrix products, arithmetic and copies ran while one was open for 3% -> 3% of each run, Pallas kernels for 8% -> 7%
where the time goes in v6:
time: 130 us; the launch traced here: 129 us
  waiting for transfers between devices  55.2 us (42%)
  starting transfers between devices  43.3 us (33%)
  Pallas kernels  20.8 us (16%)
  other arithmetic  5.14 us (4%)
  local copies, waits for them, and re-layouts  3.12 us (2%)
  between operations  1.48 us (1%)
    ppermute x39, waiting for transfers between devices, move(): return lax.ppermute(value, ('row', 'col'), pairs)  55.2 us
    ppermute x39, starting transfers between devices, move(): return lax.ppermute(value, ('row', 'col'), pairs)  39.8 us
    pallas_call x1, Pallas kernels, forward(): pl.pallas_call(functools.partial(forward_kernel, g, slots, block, n), out...  4.19 us
    pallas_call x1, Pallas kernels, backward(): pl.pallas_call(functools.partial(backward_kernel, g, block, [len(group) f...  4.1 us
    pallas_call x1, Pallas kernels, layer(): pl.pallas_call(functools.partial(layer_kernel, g, len(parts)), out_shape=...  3.9 us
    all_to_all x1, starting transfers between devices, swap_xy(): lax.all_to_all(value, ('row', 'col'), 0, 0, axis_index_groups=groups, til...  3.51 us
    unnamed x38, local copies, waits for them, and re-layouts  3.12 us
    pallas_call x1, Pallas kernels, join(): pl.pallas_call(functools.partial(join_kernel, g, places), out_shape=jax.S...  3.12 us
  transfers between devices with their start and end apart: 40, of which 12 were waited for; matrix products, arithmetic and copies ran while one was open for 3% of the time, Pallas kernels for 7%

profile of v6, /device:TPU:0, one launch (start us, length us, event | category | flops | bytes accessed | tf_op | source)
XLA Modules:
  0.0 129.0 jit_solution(9006373669553143019)
XLA Ops:
  2.0 2.9 %collective-permute-start.2 = (bf16[128,1024]{1,0:T(8,128)(2,1)}, bf16[128,1024]{1,0:T(8,128)(2,1)S(1)}, u32[]{:S(2)}, u32[]{:S(2)}) collective-permute-start(bf16[128,1024]{1,0:T(8,128)(2,1)} %refs_4_.1), channel_id=1, source_target_pairs={{0,4},{1,5},{2,6},{3,7},{4,0},{5,1},{6,2},{7,3},{8,12},{9,13},{10,... | collective-permute-start | bytes 786440 | tf_op jit(solution)/shard_map/ppermute | solution.py:48
  5.1 2.0 %collective-permute-start.6 = (bf16[128,1024]{1,0:T(8,128)(2,1)}, bf16[128,1024]{1,0:T(8,128)(2,1)S(1)}, u32[]{:S(2)}, u32[]{:S(2)}) collective-permute-start(bf16[128,1024]{1,0:T(8,128)(2,1)} %refs_4_.1), channel_id=1, source_target_pairs={{0,2},{1,3},{2,0},{3,1},{4,6},{5,7},{6,4},{7,5},{8,10},{9,11},{10,... | collective-permute-start | bytes 786440 | tf_op jit(solution)/shard_map/ppermute | solution.py:48
  7.0 4.5 %collective-permute-done.refs_1_ = s32[17]{0:T(128)S(1)} collective-permute-done((s32[17]{0:T(128)S(1)}, s32[17]{0:T(128)S(1)}, u32[]{:S(2)}, u32[]{:S(2)}) %collective-permute-start) | collective-permute-done | bytes 100 | tf_op jit(solution)/shard_map/ppermute | solution.py:48
  11.6 1.8 %collective-permute-start.9 = (bf16[128,1024]{1,0:T(8,128)(2,1)S(1)}, bf16[128,1024]{1,0:T(8,128)(2,1)S(1)}, u32[]{:S(2)}, u32[]{:S(2)}) collective-permute-start(bf16[128,1024]{1,0:T(8,128)(2,1)S(1)} %collective-permute-done.2.refs_8_), channel_id=1, source_target_pairs={{0,2},{1,3},{2,0},{3,1},{4,6},{5,7},{6,4},{7,5},{8,10},{9,11},{10,... | collective-permute-start | bytes 786440 | tf_op jit(solution)/shard_map/ppermute | solution.py:48
  13.5 1.5 %collective-permute-start.1 = (bf16[8,128,128]{2,1,0:T(8,128)(2,1)}, bf16[8,128,128]{2,1,0:T(8,128)(2,1)}, u32[]{:S(2)}, u32[]{:S(2)}) collective-permute-start(bf16[8,128,128]{2,1,0:T(8,128)(2,1)} %bitcast.29), channel_id=1, source_target_pairs={{0,4},{1,5},{2,6},{3,7},{4,0},{5,1},{6,2},{7,3},{8,12},{9,13},{10,... | collective-permute-start | bytes 786440 | tf_op jit(solution)/shard_map/ppermute | solution.py:48
  17.6 2.8 %collective-permute-done.9.refs_10_ = bf16[128,1024]{1,0:T(8,128)(2,1)S(1)} collective-permute-done((bf16[128,1024]{1,0:T(8,128)(2,1)S(1)}, bf16[128,1024]{1,0:T(8,128)(2,1)S(1)}, u32[]{:S(2)}, u32[]{:S(2)}) %collective-permute-start.9) | collective-permute-done | bytes 262176 | tf_op jit(solution)/shard_map/ppermute | solution.py:48
  20.4 1.8 %collective-permute-done.1.refs_3_.refs_4_ = bf16[8,128,128]{2,1,0:T(8,128)(2,1)} collective-permute-done((bf16[8,128,128]{2,1,0:T(8,128)(2,1)}, bf16[8,128,128]{2,1,0:T(8,128)(2,1)}, u32[]{:S(2)}, u32[]{:S(2)}) %collective-permute-start.1) | collective-permute-done | bytes 262176 | tf_op jit(solution)/shard_map/ppermute | solution.py:48
  23.7 4.2 %forward.1 = (bf16[128,1024]{1,0:T(8,128)(2,1)}, bf16[128,1024]{1,0:T(8,128)(2,1)}, bf16[128,1024]{1,0:T(8,128)(2,1)}, bf16[128,1024]{1,0:T(8,128)(2,1)}) custom-call(s32[17]{0:T(128)} %copy-done.17, s32[17]{0:T(128)} %copy-done.16, bf16[8,128,128]{2,1,0:T(8,128)(2,1)} %bitcast.30, bf16[8,128,128]{2,1,0:T(8,128)(2,1)} %collective-permute-done.1.refs_3_.refs_4_, ...), custom_call_target="tpu_custom_call" | custom-call | tf_op jit(solution)/shard_map/forward/pallas_call | solution.py:140
  27.9 1.6 %collective-permute-start.11 = (bf16[128,1024]{1,0:T(8,128)(2,1)}, bf16[128,1024]{1,0:T(8,128)(2,1)}, u32[]{:S(2)}, u32[]{:S(2)}) collective-permute-start(bf16[128,1024]{1,0:T(8,128)(2,1)} %get-tuple-element.40), channel_id=1, source_target_pairs={{0,8},{1,9},{2,10},{3,11},{4,12},{5,13},{6,14},{7,15},{8,0},{9,1},... | collective-permute-start | bytes 786440 | tf_op jit(solution)/shard_map/ppermute | solution.py:48
  29.5 2.6 %collective-permute-start.12 = (bf16[128,1024]{1,0:T(8,128)(2,1)}, bf16[128,1024]{1,0:T(8,128)(2,1)}, u32[]{:S(2)}, u32[]{:S(2)}) collective-permute-start(bf16[128,1024]{1,0:T(8,128)(2,1)} %get-tuple-element.41), channel_id=1, source_target_pairs={{0,16},{1,17},{2,18},{3,19},{4,20},{5,21},{6,22},{7,23},{8,24},{9,... | collective-permute-start | bytes 786440 | tf_op jit(solution)/shard_map/ppermute | solution.py:48
  32.3 3.0 %build.1.matrix = bf16[512,1024]{1,0:T(8,128)(2,1)} custom-call(s32[17]{0:T(128)} %copy-done.17, s32[17]{0:T(128)} %copy-done.16, s32[34]{0:T(128)} %copy-done.18, bf16[8,128,128]{2,1,0:T(8,128)(2,1)} %bitcast.31, bf16[8,128,128]{2,1,0:T(8,128)(2,1)} %collective-permute-done.1.refs_3_.refs_4_, bf16[8,128,128]{2,1,0:T(8,128)(2,1)} %collective-permute-done.3.refs_5_, ...), custom_call_target="tpu_custom_call" | custom-call | tf_op jit(solution)/shard_map/build/pallas_call | solution.py:174
  35.3 6.8 %collective-permute-done.11.refs_1_ = bf16[128,1024]{1,0:T(8,128)(2,1)} collective-permute-done((bf16[128,1024]{1,0:T(8,128)(2,1)}, bf16[128,1024]{1,0:T(8,128)(2,1)}, u32[]{:S(2)}, u32[]{:S(2)}) %collective-permute-start.11) | collective-permute-done | bytes 262176 | tf_op jit(solution)/shard_map/ppermute | solution.py:48
  42.1 9.1 %collective-permute-done.12.refs_2_ = bf16[128,1024]{1,0:T(8,128)(2,1)} collective-permute-done((bf16[128,1024]{1,0:T(8,128)(2,1)}, bf16[128,1024]{1,0:T(8,128)(2,1)}, u32[]{:S(2)}, u32[]{:S(2)}) %collective-permute-start.12) | collective-permute-done | bytes 262176 | tf_op jit(solution)/shard_map/ppermute | solution.py:48
  51.2 3.9 %layer.1 = (bf16[128,1024]{1,0:T(8,128)(2,1)}, bf16[128,1536]{1,0:T(8,128)(2,1)}, bf16[128,1024]{1,0:T(8,128)(2,1)}, bf16[128,512]{1,0:T(8,128)(2,1)}) custom-call(bf16[128,1024]{1,0:T(8,128)(2,1)} %get-tuple-element.44.refs_0_, bf16[128,1024]{1,0:T(8,128)(2,1)} %collective-permute-done.11.refs_1_, bf16[128,1024]{1,0:T(8,128)(2,1)} %collective-permute-done.12.refs_2_, ...), custom_call_target="tpu_custom_call" | custom-call | tf_op jit(solution)/shard_map/layer/pallas_call | solution.py:252
  55.1 2.5 %collective-permute-start.17 = (bf16[128,1024]{1,0:T(8,128)(2,1)}, bf16[128,1024]{1,0:T(8,128)(2,1)}, u32[]{:S(2)}, u32[]{:S(2)}) collective-permute-start(bf16[128,1024]{1,0:T(8,128)(2,1)} %get-tuple-element.50.refs_0_), channel_id=1, source_target_pairs={{0,24},{1,25},{2,26},{3,27},{4,28},{5,29},{6,30},{7,31},{8,16},{9,... | collective-permute-start | bytes 786440 | tf_op jit(solution)/shard_map/ppermute | solution.py:48
  57.5 4.4 %collective-permute-start.16 = (bf16[128,1024]{1,0:T(8,128)(2,1)}, bf16[128,1024]{1,0:T(8,128)(2,1)}, u32[]{:S(2)}, u32[]{:S(2)}) collective-permute-start(bf16[128,1024]{1,0:T(8,128)(2,1)} %get-tuple-element.50.refs_0_), channel_id=1, source_target_pairs={{0,16},{1,17},{2,18},{3,19},{4,20},{5,21},{6,22},{7,23},{8,24},{9,... | collective-permute-start | bytes 786440 | tf_op jit(solution)/shard_map/ppermute | solution.py:48
  62.1 2.5 %terms.1 = (bf16[4,128,256]{2,1,0:T(8,128)(2,1)}, bf16[4,128,256]{2,1,0:T(8,128)(2,1)}, bf16[4,128,256]{2,1,0:T(8,128)(2,1)}, bf16[4,128,256]{2,1,0:T(8,128)(2,1)}) custom-call(bf16[128,512]{1,0:T(8,128)(2,1)} %get-tuple-element.51.keep, bf16[128,1536]{1,0:T(8,128)(2,1)} %get-tuple-element.52.share, bf16[128,1536]{1,0:T(8,128)(2,1)} %collective-permute-done.22.share_got), custom_call_target="tpu_custom_call" | custom-call | tf_op jit(solution)/shard_map/terms/pallas_call | solution.py:294
  65.1 1.5 %collective-permute-start.24 = (bf16[4,128,256]{2,1,0:T(8,128)(2,1)}, bf16[4,128,256]{2,1,0:T(8,128)(2,1)S(1)}, u32[]{:S(2)}, u32[]{:S(2)}) collective-permute-start(bf16[4,128,256]{2,1,0:T(8,128)(2,1)} %get-tuple-element.55), channel_id=1, source_target_pairs={{0,4},{1,5},{2,6},{3,7},{4,0},{5,1},{6,2},{7,3},{8,12},{9,13},{10,... | collective-permute-start | bytes 786440 | tf_op jit(solution)/shard_map/ppermute | solution.py:48
  66.5 1.5 %collective-permute-start.25 = (bf16[4,128,256]{2,1,0:T(8,128)(2,1)}, bf16[4,128,256]{2,1,0:T(8,128)(2,1)S(1)}, u32[]{:S(2)}, u32[]{:S(2)}) collective-permute-start(bf16[4,128,256]{2,1,0:T(8,128)(2,1)} %get-tuple-element.56), channel_id=1, source_target_pairs={{0,6},{1,7},{2,4},{3,5},{4,2},{5,3},{6,0},{7,1},{8,14},{9,15},{10,... | collective-permute-start | bytes 786440 | tf_op jit(solution)/shard_map/ppermute | solution.py:48
  68.0 14.7 %collective-permute-done.16.refs_2_ = bf16[128,1024]{1,0:T(8,128)(2,1)} collective-permute-done((bf16[128,1024]{1,0:T(8,128)(2,1)}, bf16[128,1024]{1,0:T(8,128)(2,1)}, u32[]{:S(2)}, u32[]{:S(2)}) %collective-permute-start.16) | collective-permute-done | bytes 262176 | tf_op jit(solution)/shard_map/ppermute | solution.py:48
  84.0 1.7 %fusion.4 = (bf16[128,256]{1,0:T(8,128)(2,1)}, bf16[128,256]{1,0:T(8,128)(2,1)}, bf16[128,256]{1,0:T(8,128)(2,1)}) fusion(bf16[4,128,256]{2,1,0:T(8,128)(2,1)S(1)} %collective-permute-done.25, bf16[4,128,256]{2,1,0:T(8,128)(2,1)S(1)} %collective-permute-done.24, bf16[4,128,256]{2,1,0:T(8,128)(2,1)S(1)} %collective-permute-done.23, ...), kind=kLoop, calls=%fused_computation.9 | loop fusion | flops 786432 | bytes 983040 | tf_op jit(solution)/shard_map/add | solution.py:396
  85.7 3.2 %collective-permute-start.26 = (bf16[128,256]{1,0:T(8,128)(2,1)}, bf16[128,256]{1,0:T(8,128)(2,1)S(1)}, u32[]{:S(2)}, u32[]{:S(2)}) collective-permute-start(bf16[128,256]{1,0:T(8,128)(2,1)} %get-tuple-element.63), channel_id=1, source_target_pairs={{0,8},{1,9},{2,10},{3,11},{4,12},{5,13},{6,14},{7,15},{8,0},{9,1},... | collective-permute-start | bytes 196616 | tf_op jit(solution)/shard_map/ppermute | solution.py:48
  88.9 2.5 %collective-permute-start.28 = (bf16[128,256]{1,0:T(8,128)(2,1)}, bf16[128,256]{1,0:T(8,128)(2,1)S(1)}, u32[]{:S(2)}, u32[]{:S(2)}) collective-permute-start(bf16[128,256]{1,0:T(8,128)(2,1)} %get-tuple-element.64), channel_id=1, source_target_pairs={{0,24},{1,25},{2,26},{3,27},{4,28},{5,29},{6,30},{7,31},{8,16},{9,... | collective-permute-start | bytes 196616 | tf_op jit(solution)/shard_map/ppermute | solution.py:48
  91.4 4.1 %backward.1 = bf16[512,1024]{1,0:T(8,128)(2,1)} custom-call(bf16[512,1024]{1,0:T(8,128)(2,1)} %build.1.matrix, bf16[128,1024]{1,0:T(8,128)(2,1)} %get-tuple-element.50.refs_0_, bf16[128,1024]{1,0:T(8,128)(2,1)} %collective-permute-done.15.refs_1_, bf16[128,1024]{1,0:T(8,128)(2,1)} %collective-permute-done.16.refs_2_, ...), custom_call_target="tpu_custom_call" | custom-call | tf_op jit(solution)/shard_map/backward/pallas_call | solution.py:202
  95.5 3.5 %all-to-all-start = ((bf16[4,128,1024]{2,1,0:T(8,128)(2,1)}), bf16[4,128,1024]{2,1,0:T(8,128)(2,1)S(1)}, u32[]{:S(2)}, u32[]{:S(2)}) async-start(bf16[4,128,1024]{2,1,0:T(8,128)(2,1)} %bitcast.27), calls=%async_computation | async-start | bytes 2097152 | tf_op jit(solution)/shard_map/all_to_all | solution.py:56
  100.1 1.6 %collective-permute-start.31 = (bf16[128,256]{1,0:T(8,128)(2,1)S(1)}, bf16[128,256]{1,0:T(8,128)(2,1)S(1)}, u32[]{:S(2)}, u32[]{:S(2)}) collective-permute-start(bf16[128,256]{1,0:T(8,128)(2,1)S(1)} %fusion.3), channel_id=1, source_target_pairs={{0,24},{1,25},{2,26},{3,27},{4,28},{5,29},{6,30},{7,31},{8,16},{9,... | collective-permute-start | bytes 196616 | tf_op jit(solution)/shard_map/ppermute | solution.py:48
  101.7 1.8 %collective-permute-start.30 = (bf16[128,256]{1,0:T(8,128)(2,1)S(1)}, bf16[128,256]{1,0:T(8,128)(2,1)S(1)}, u32[]{:S(2)}, u32[]{:S(2)}) collective-permute-start(bf16[128,256]{1,0:T(8,128)(2,1)S(1)} %fusion.3), channel_id=1, source_target_pairs={{0,16},{1,17},{2,18},{3,19},{4,20},{5,21},{6,22},{7,23},{8,24},{9,... | collective-permute-start | bytes 196616 | tf_op jit(solution)/shard_map/ppermute | solution.py:48
  104.5 2.2 %collective-permute-done.31 = bf16[128,256]{1,0:T(8,128)(2,1)S(1)} collective-permute-done((bf16[128,256]{1,0:T(8,128)(2,1)S(1)}, bf16[128,256]{1,0:T(8,128)(2,1)S(1)}, u32[]{:S(2)}, u32[]{:S(2)}) %collective-permute-start.31) | collective-permute-done | bytes 65568 | tf_op jit(solution)/shard_map/ppermute | solution.py:48
  108.2 2.7 %collective-permute-start.34 = (bf16[4,128,256]{2,1,0:T(8,128)(2,1)S(1)}, bf16[4,128,256]{2,1,0:T(8,128)(2,1)S(1)}, u32[]{:S(2)}, u32[]{:S(2)}) collective-permute-start(bf16[4,128,256]{2,1,0:T(8,128)(2,1)S(1)} %pad_maximum_fusion.refs_0_), channel_id=1, source_target_pairs={{0,6},{1,7},{2,4},{3,5},{4,2},{5,3},{6,0},{7,1},{8,14},{9,15},{10,... | collective-permute-start | bytes 786440 | tf_op jit(solution)/shard_map/ppermute | solution.py:48
  111.7 8.9 %collective-permute-done.34.refs_3_ = bf16[4,128,256]{2,1,0:T(8,128)(2,1)S(1)} collective-permute-done((bf16[4,128,256]{2,1,0:T(8,128)(2,1)S(1)}, bf16[4,128,256]{2,1,0:T(8,128)(2,1)S(1)}, u32[]{:S(2)}, u32[]{:S(2)}) %collective-permute-start.34) | collective-permute-done | bytes 262176 | tf_op jit(solution)/shard_map/ppermute | solution.py:48
  121.1 1.8 %collective-permute-done.33.refs_2_ = bf16[4,128,256]{2,1,0:T(8,128)(2,1)S(1)} collective-permute-done((bf16[4,128,256]{2,1,0:T(8,128)(2,1)S(1)}, bf16[4,128,256]{2,1,0:T(8,128)(2,1)S(1)}, u32[]{:S(2)}, u32[]{:S(2)}) %collective-permute-start.33) | collective-permute-done | bytes 262176 | tf_op jit(solution)/shard_map/ppermute | solution.py:48
  125.9 3.1 %join.1 = f32[1024,1024]{1,0:T(8,128)} custom-call(bf16[4,128,256]{2,1,0:T(8,128)(2,1)} %copy-done, bf16[4,128,256]{2,1,0:T(8,128)(2,1)} %copy-done.6, bf16[4,128,256]{2,1,0:T(8,128)(2,1)} %copy-done.5, bf16[4,128,256]{2,1,0:T(8,128)(2,1)} %copy-done.4, bf16[4,128,256]{2,1,0:T(8,128)(2,1)} %copy-done.9, ...), custom_call_target="tpu_custom_call" | custom-call | tf_op jit(solution)/shard_map/join/pallas_call | solution.py:336
  (98 shorter events, 14.9 us)
Async XLA Ops:
  2.0 9.5 %collective-permute-start.2 = (bf16[128,1024]{1,0:T(8,128)(2,1)}, bf16[128,1024]{1,0:T(8,128)(2,1)S(1)}, u32[]{:S(2)}, u32[]{:S(2)}) collective-permute-start(bf16[128,1024]{1,0:T(8,128)(2,1)} %refs_4_.1), channel_id=1, source_target_pairs={{0,4},{1,5},{2,6},{3,7},{4,0},{5,1},{6,2},{7,3},{8,12},{9,13},{10,... | collective-permute-start | bytes 786440 | tf_op jit(solution)/shard_map/ppermute | solution.py:48
  5.0 6.6 %collective-permute-start = (s32[17]{0:T(128)S(1)}, s32[17]{0:T(128)S(1)}, u32[]{:S(2)}, u32[]{:S(2)}) collective-permute-start(s32[17]{0:T(128)S(1)} %pad_add_fusion.refs_0_), channel_id=1, source_target_pairs={{0,4},{1,5},{2,6},{3,7},{4,0},{5,1},{6,2},{7,3},{8,12},{9,13},{10,... | collective-permute-start | bytes 212 | tf_op jit(solution)/shard_map/ppermute | solution.py:48
  5.1 12.0 %collective-permute-start.6 = (bf16[128,1024]{1,0:T(8,128)(2,1)}, bf16[128,1024]{1,0:T(8,128)(2,1)S(1)}, u32[]{:S(2)}, u32[]{:S(2)}) collective-permute-start(bf16[128,1024]{1,0:T(8,128)(2,1)} %refs_4_.1), channel_id=1, source_target_pairs={{0,2},{1,3},{2,0},{3,1},{4,6},{5,7},{6,4},{7,5},{8,10},{9,11},{10,... | collective-permute-start | bytes 786440 | tf_op jit(solution)/shard_map/ppermute | solution.py:48
  11.6 5.8 %collective-permute-start.3 = (bf16[8,128,128]{2,1,0:T(8,128)(2,1)}, bf16[8,128,128]{2,1,0:T(8,128)(2,1)}, u32[]{:S(2)}, u32[]{:S(2)}) collective-permute-start(bf16[8,128,128]{2,1,0:T(8,128)(2,1)} %bitcast.28), channel_id=1, source_target_pairs={{0,1},{1,0},{2,3},{3,2},{4,5},{5,4},{6,7},{7,6},{8,9},{9,8},{10,11... | collective-permute-start | bytes 786440 | tf_op jit(solution)/shard_map/ppermute | solution.py:48
  11.6 8.7 %collective-permute-start.9 = (bf16[128,1024]{1,0:T(8,128)(2,1)S(1)}, bf16[128,1024]{1,0:T(8,128)(2,1)S(1)}, u32[]{:S(2)}, u32[]{:S(2)}) collective-permute-start(bf16[128,1024]{1,0:T(8,128)(2,1)S(1)} %collective-permute-done.2.refs_8_), channel_id=1, source_target_pairs={{0,2},{1,3},{2,0},{3,1},{4,6},{5,7},{6,4},{7,5},{8,10},{9,11},{10,... | collective-permute-start | bytes 786440 | tf_op jit(solution)/shard_map/ppermute | solution.py:48
  13.5 8.7 %collective-permute-start.1 = (bf16[8,128,128]{2,1,0:T(8,128)(2,1)}, bf16[8,128,128]{2,1,0:T(8,128)(2,1)}, u32[]{:S(2)}, u32[]{:S(2)}) collective-permute-start(bf16[8,128,128]{2,1,0:T(8,128)(2,1)} %bitcast.29), channel_id=1, source_target_pairs={{0,4},{1,5},{2,6},{3,7},{4,0},{5,1},{6,2},{7,3},{8,12},{9,13},{10,... | collective-permute-start | bytes 786440 | tf_op jit(solution)/shard_map/ppermute | solution.py:48
  16.8 5.3 %collective-permute-start.5 = (bf16[128,1024]{1,0:T(8,128)(2,1)}, bf16[128,1024]{1,0:T(8,128)(2,1)S(1)}, u32[]{:S(2)}, u32[]{:S(2)}) collective-permute-start(bf16[128,1024]{1,0:T(8,128)(2,1)} %refs_4_.1), channel_id=1, source_target_pairs={{0,1},{1,0},{2,3},{3,2},{4,5},{5,4},{6,7},{7,6},{8,9},{9,8},{10,11... | collective-permute-start | bytes 786440 | tf_op jit(solution)/shard_map/ppermute | solution.py:48
  17.1 5.1 %collective-permute-start.7 = (bf16[128,1024]{1,0:T(8,128)(2,1)S(1)}, bf16[128,1024]{1,0:T(8,128)(2,1)S(1)}, u32[]{:S(2)}, u32[]{:S(2)}) collective-permute-start(bf16[128,1024]{1,0:T(8,128)(2,1)S(1)} %collective-permute-done.6.refs_6_), channel_id=1, source_target_pairs={{0,1},{1,0},{2,3},{3,2},{4,5},{5,4},{6,7},{7,6},{8,9},{9,8},{10,11... | collective-permute-start | bytes 786440 | tf_op jit(solution)/shard_map/ppermute | solution.py:48
  17.4 4.8 %collective-permute-start.8 = (bf16[128,1024]{1,0:T(8,128)(2,1)S(1)}, bf16[128,1024]{1,0:T(8,128)(2,1)S(1)}, u32[]{:S(2)}, u32[]{:S(2)}) collective-permute-start(bf16[128,1024]{1,0:T(8,128)(2,1)S(1)} %collective-permute-done.2.refs_8_), channel_id=1, source_target_pairs={{0,1},{1,0},{2,3},{3,2},{4,5},{5,4},{6,7},{7,6},{8,9},{9,8},{10,11... | collective-permute-start | bytes 786440 | tf_op jit(solution)/shard_map/ppermute | solution.py:48
  27.9 14.2 %collective-permute-start.11 = (bf16[128,1024]{1,0:T(8,128)(2,1)}, bf16[128,1024]{1,0:T(8,128)(2,1)}, u32[]{:S(2)}, u32[]{:S(2)}) collective-permute-start(bf16[128,1024]{1,0:T(8,128)(2,1)} %get-tuple-element.40), channel_id=1, source_target_pairs={{0,8},{1,9},{2,10},{3,11},{4,12},{5,13},{6,14},{7,15},{8,0},{9,1},... | collective-permute-start | bytes 786440 | tf_op jit(solution)/shard_map/ppermute | solution.py:48
  29.5 21.6 %collective-permute-start.12 = (bf16[128,1024]{1,0:T(8,128)(2,1)}, bf16[128,1024]{1,0:T(8,128)(2,1)}, u32[]{:S(2)}, u32[]{:S(2)}) collective-permute-start(bf16[128,1024]{1,0:T(8,128)(2,1)} %get-tuple-element.41), channel_id=1, source_target_pairs={{0,16},{1,17},{2,18},{3,19},{4,20},{5,21},{6,22},{7,23},{8,24},{9,... | collective-permute-start | bytes 786440 | tf_op jit(solution)/shard_map/ppermute | solution.py:48
  32.1 19.0 %collective-permute-start.13 = (bf16[128,1024]{1,0:T(8,128)(2,1)}, bf16[128,1024]{1,0:T(8,128)(2,1)}, u32[]{:S(2)}, u32[]{:S(2)}) collective-permute-start(bf16[128,1024]{1,0:T(8,128)(2,1)} %get-tuple-element.42), channel_id=1, source_target_pairs={{0,24},{1,25},{2,26},{3,27},{4,28},{5,29},{6,30},{7,31},{8,16},{9,... | collective-permute-start | bytes 786440 | tf_op jit(solution)/shard_map/ppermute | solution.py:48
  55.1 7.0 %collective-permute-start.22 = (bf16[128,1536]{1,0:T(8,128)(2,1)}, bf16[128,1536]{1,0:T(8,128)(2,1)}, u32[]{:S(2)}, u32[]{:S(2)}) collective-permute-start(bf16[128,1536]{1,0:T(8,128)(2,1)} %get-tuple-element.52.share), channel_id=1, source_target_pairs={{0,1},{1,0},{2,3},{3,2},{4,5},{5,4},{6,7},{7,6},{8,9},{9,8},{10,11... | collective-permute-start | bytes 1179656 | tf_op jit(solution)/shard_map/ppermute | solution.py:48
  55.1 11.5 %collective-permute-start.17 = (bf16[128,1024]{1,0:T(8,128)(2,1)}, bf16[128,1024]{1,0:T(8,128)(2,1)}, u32[]{:S(2)}, u32[]{:S(2)}) collective-permute-start(bf16[128,1024]{1,0:T(8,128)(2,1)} %get-tuple-element.50.refs_0_), channel_id=1, source_target_pairs={{0,24},{1,25},{2,26},{3,27},{4,28},{5,29},{6,30},{7,31},{8,16},{9,... | collective-permute-start | bytes 786440 | tf_op jit(solution)/shard_map/ppermute | solution.py:48
  57.5 25.2 %collective-permute-start.16 = (bf16[128,1024]{1,0:T(8,128)(2,1)}, bf16[128,1024]{1,0:T(8,128)(2,1)}, u32[]{:S(2)}, u32[]{:S(2)}) collective-permute-start(bf16[128,1024]{1,0:T(8,128)(2,1)} %get-tuple-element.50.refs_0_), channel_id=1, source_target_pairs={{0,16},{1,17},{2,18},{3,19},{4,20},{5,21},{6,22},{7,23},{8,24},{9,... | collective-permute-start | bytes 786440 | tf_op jit(solution)/shard_map/ppermute | solution.py:48
  61.9 20.9 %collective-permute-start.15 = (bf16[128,1024]{1,0:T(8,128)(2,1)}, bf16[128,1024]{1,0:T(8,128)(2,1)}, u32[]{:S(2)}, u32[]{:S(2)}) collective-permute-start(bf16[128,1024]{1,0:T(8,128)(2,1)} %get-tuple-element.50.refs_0_), channel_id=1, source_target_pairs={{0,8},{1,9},{2,10},{3,11},{4,12},{5,13},{6,14},{7,15},{8,0},{9,1},... | collective-permute-start | bytes 786440 | tf_op jit(solution)/shard_map/ppermute | solution.py:48
  64.5 18.7 %collective-permute-start.23 = (bf16[4,128,256]{2,1,0:T(8,128)(2,1)}, bf16[4,128,256]{2,1,0:T(8,128)(2,1)S(1)}, u32[]{:S(2)}, u32[]{:S(2)}) collective-permute-start(bf16[4,128,256]{2,1,0:T(8,128)(2,1)} %get-tuple-element.54), channel_id=1, source_target_pairs={{0,2},{1,3},{2,0},{3,1},{4,6},{5,7},{6,4},{7,5},{8,10},{9,11},{10,... | collective-permute-start | bytes 786440 | tf_op jit(solution)/shard_map/ppermute | solution.py:48
  65.1 18.3 %collective-permute-start.24 = (bf16[4,128,256]{2,1,0:T(8,128)(2,1)}, bf16[4,128,256]{2,1,0:T(8,128)(2,1)S(1)}, u32[]{:S(2)}, u32[]{:S(2)}) collective-permute-start(bf16[4,128,256]{2,1,0:T(8,128)(2,1)} %get-tuple-element.55), channel_id=1, source_target_pairs={{0,4},{1,5},{2,6},{3,7},{4,0},{5,1},{6,2},{7,3},{8,12},{9,13},{10,... | collective-permute-start | bytes 786440 | tf_op jit(solution)/shard_map/ppermute | solution.py:48
  66.5 17.3 %collective-permute-start.25 = (bf16[4,128,256]{2,1,0:T(8,128)(2,1)}, bf16[4,128,256]{2,1,0:T(8,128)(2,1)S(1)}, u32[]{:S(2)}, u32[]{:S(2)}) collective-permute-start(bf16[4,128,256]{2,1,0:T(8,128)(2,1)} %get-tuple-element.56), channel_id=1, source_target_pairs={{0,6},{1,7},{2,4},{3,5},{4,2},{5,3},{6,0},{7,1},{8,14},{9,15},{10,... | collective-permute-start | bytes 786440 | tf_op jit(solution)/shard_map/ppermute | solution.py:48
  82.8 6.2 %collective-permute-start.18 = (bf16[128,1024]{1,0:T(8,128)(2,1)}, bf16[128,1024]{1,0:T(8,128)(2,1)}, u32[]{:S(2)}, u32[]{:S(2)}) collective-permute-start(bf16[128,1024]{1,0:T(8,128)(2,1)} %get-tuple-element.50.refs_0_), channel_id=1, source_target_pairs={{0,1},{1,0},{2,3},{3,2},{4,5},{5,4},{6,7},{7,6},{8,9},{9,8},{10,11... | collective-permute-start | bytes 786440 | tf_op jit(solution)/shard_map/ppermute | solution.py:48
  82.8 8.6 %collective-permute-start.21 = (bf16[128,1024]{1,0:T(8,128)(2,1)}, bf16[128,1024]{1,0:T(8,128)(2,1)}, u32[]{:S(2)}, u32[]{:S(2)}) collective-permute-start(bf16[128,1024]{1,0:T(8,128)(2,1)} %collective-permute-done.17.refs_3_), channel_id=1, source_target_pairs={{0,1},{1,0},{2,3},{3,2},{4,5},{5,4},{6,7},{7,6},{8,9},{9,8},{10,11... | collective-permute-start | bytes 786440 | tf_op jit(solution)/shard_map/ppermute | solution.py:48
  83.3 8.1 %collective-permute-start.20 = (bf16[128,1024]{1,0:T(8,128)(2,1)}, bf16[128,1024]{1,0:T(8,128)(2,1)}, u32[]{:S(2)}, u32[]{:S(2)}) collective-permute-start(bf16[128,1024]{1,0:T(8,128)(2,1)} %collective-permute-done.16.refs_2_), channel_id=1, source_target_pairs={{0,1},{1,0},{2,3},{3,2},{4,5},{5,4},{6,7},{7,6},{8,9},{9,8},{10,11... | collective-permute-start | bytes 786440 | tf_op jit(solution)/shard_map/ppermute | solution.py:48
  83.4 8.0 %collective-permute-start.19 = (bf16[128,1024]{1,0:T(8,128)(2,1)}, bf16[128,1024]{1,0:T(8,128)(2,1)}, u32[]{:S(2)}, u32[]{:S(2)}) collective-permute-start(bf16[128,1024]{1,0:T(8,128)(2,1)} %collective-permute-done.15.refs_1_), channel_id=1, source_target_pairs={{0,1},{1,0},{2,3},{3,2},{4,5},{5,4},{6,7},{7,6},{8,9},{9,8},{10,11... | collective-permute-start | bytes 786440 | tf_op jit(solution)/shard_map/ppermute | solution.py:48
  85.7 13.4 %collective-permute-start.26 = (bf16[128,256]{1,0:T(8,128)(2,1)}, bf16[128,256]{1,0:T(8,128)(2,1)S(1)}, u32[]{:S(2)}, u32[]{:S(2)}) collective-permute-start(bf16[128,256]{1,0:T(8,128)(2,1)} %get-tuple-element.63), channel_id=1, source_target_pairs={{0,8},{1,9},{2,10},{3,11},{4,12},{5,13},{6,14},{7,15},{8,0},{9,1},... | collective-permute-start | bytes 196616 | tf_op jit(solution)/shard_map/ppermute | solution.py:48
  88.9 10.1 %collective-permute-start.28 = (bf16[128,256]{1,0:T(8,128)(2,1)}, bf16[128,256]{1,0:T(8,128)(2,1)S(1)}, u32[]{:S(2)}, u32[]{:S(2)}) collective-permute-start(bf16[128,256]{1,0:T(8,128)(2,1)} %get-tuple-element.64), channel_id=1, source_target_pairs={{0,24},{1,25},{2,26},{3,27},{4,28},{5,29},{6,30},{7,31},{8,16},{9,... | collective-permute-start | bytes 196616 | tf_op jit(solution)/shard_map/ppermute | solution.py:48
  91.4 7.7 %collective-permute-start.27 = (bf16[128,256]{1,0:T(8,128)(2,1)}, bf16[128,256]{1,0:T(8,128)(2,1)S(1)}, u32[]{:S(2)}, u32[]{:S(2)}) collective-permute-start(bf16[128,256]{1,0:T(8,128)(2,1)} %get-tuple-element.65), channel_id=1, source_target_pairs={{0,16},{1,17},{2,18},{3,19},{4,20},{5,21},{6,22},{7,23},{8,24},{9,... | collective-permute-start | bytes 196616 | tf_op jit(solution)/shard_map/ppermute | solution.py:48
  95.5 28.0 %all-to-all-start = ((bf16[4,128,1024]{2,1,0:T(8,128)(2,1)}), bf16[4,128,1024]{2,1,0:T(8,128)(2,1)S(1)}, u32[]{:S(2)}, u32[]{:S(2)}) async-start(bf16[4,128,1024]{2,1,0:T(8,128)(2,1)} %bitcast.27), calls=%async_computation | async-start | bytes 2097152 | tf_op jit(solution)/shard_map/all_to_all | solution.py:56
  100.1 6.6 %collective-permute-start.31 = (bf16[128,256]{1,0:T(8,128)(2,1)S(1)}, bf16[128,256]{1,0:T(8,128)(2,1)S(1)}, u32[]{:S(2)}, u32[]{:S(2)}) collective-permute-start(bf16[128,256]{1,0:T(8,128)(2,1)S(1)} %fusion.3), channel_id=1, source_target_pairs={{0,24},{1,25},{2,26},{3,27},{4,28},{5,29},{6,30},{7,31},{8,16},{9,... | collective-permute-start | bytes 196616 | tf_op jit(solution)/shard_map/ppermute | solution.py:48
  101.7 5.8 %collective-permute-start.30 = (bf16[128,256]{1,0:T(8,128)(2,1)S(1)}, bf16[128,256]{1,0:T(8,128)(2,1)S(1)}, u32[]{:S(2)}, u32[]{:S(2)}) collective-permute-start(bf16[128,256]{1,0:T(8,128)(2,1)S(1)} %fusion.3), channel_id=1, source_target_pairs={{0,16},{1,17},{2,18},{3,19},{4,20},{5,21},{6,22},{7,23},{8,24},{9,... | collective-permute-start | bytes 196616 | tf_op jit(solution)/shard_map/ppermute | solution.py:48
  108.2 12.4 %collective-permute-start.34 = (bf16[4,128,256]{2,1,0:T(8,128)(2,1)S(1)}, bf16[4,128,256]{2,1,0:T(8,128)(2,1)S(1)}, u32[]{:S(2)}, u32[]{:S(2)}) collective-permute-start(bf16[4,128,256]{2,1,0:T(8,128)(2,1)S(1)} %pad_maximum_fusion.refs_0_), channel_id=1, source_target_pairs={{0,6},{1,7},{2,4},{3,5},{4,2},{5,3},{6,0},{7,1},{8,14},{9,15},{10,... | collective-permute-start | bytes 786440 | tf_op jit(solution)/shard_map/ppermute | solution.py:48
  110.8 12.1 %collective-permute-start.33 = (bf16[4,128,256]{2,1,0:T(8,128)(2,1)S(1)}, bf16[4,128,256]{2,1,0:T(8,128)(2,1)S(1)}, u32[]{:S(2)}, u32[]{:S(2)}) collective-permute-start(bf16[4,128,256]{2,1,0:T(8,128)(2,1)S(1)} %pad_maximum_fusion.refs_0_), channel_id=1, source_target_pairs={{0,4},{1,5},{2,6},{3,7},{4,0},{5,1},{6,2},{7,3},{8,12},{9,13},{10,... | collective-permute-start | bytes 786440 | tf_op jit(solution)/shard_map/ppermute | solution.py:48
  111.4 11.6 %collective-permute-start.32 = (bf16[4,128,256]{2,1,0:T(8,128)(2,1)S(1)}, bf16[4,128,256]{2,1,0:T(8,128)(2,1)S(1)}, u32[]{:S(2)}, u32[]{:S(2)}) collective-permute-start(bf16[4,128,256]{2,1,0:T(8,128)(2,1)S(1)} %pad_maximum_fusion.refs_0_), channel_id=1, source_target_pairs={{0,2},{1,3},{2,0},{3,1},{4,6},{5,7},{6,4},{7,5},{8,10},{9,11},{10,... | collective-permute-start | bytes 786440 | tf_op jit(solution)/shard_map/ppermute | solution.py:48
  (27 other events, 120.1 us)
